TPU v7x, 32 devices: a whole 2x2x4 slice. The times are simulated.
32 devices in a mesh: visit: 4 (over x, core), patch: 8 (over z, y).
Axes of the slice: x: 2, y: 2, z: 4, core: 2. Of those that a mesh axis runs over, the one named last changes fastest.
Arguments:
- images: bfloat16 [256, 512, 512], P(('visit', 'patch')), may hold values from -10 to 10
- warp_rows: bfloat16 [256, 512, 512], P(('visit', 'patch')), may hold values from -2 to 2
- warp_cols: bfloat16 [256, 512, 512], P(('visit', 'patch')), may hold values from -2 to 2
- tile_weight: bfloat16 [256], P(('visit', 'patch')), may hold values from 0.5 to 4
- tile_patch: int32 [256], P(('visit', 'patch')), may hold values from 0 to 7, as said below
- match_rows: float32 [8, 512, 512], P('patch'), may hold values from -2 to 2
- match_cols: float32 [8, 512, 512], P('patch'), may hold values from -2 to 2
- src_row: int32 [8, 512], P('patch'), may hold values from 0 to 511
- src_col: int32 [8, 512], P('patch'), may hold values from 0 to 511
Outputs:
- coadd: float32 [8, 512, 512], P('patch', 'visit')
- zero_point: float32 [16], P('visit')
- flux_resid: float32 [256, 512], P(('visit', 'patch'))
Inputs may be any that keep to these rules, and one draw needn't show every extreme that they name: `tile_patch`: among the 8 tiles of one device no patch is named more than 2 times; in each visit row one patch is named exactly 2 times by every device of the row; every patch is named by some tile of every visit row.
All inputs are finite; a program needn't handle non-finite values.
Results may differ from a plain program's by a relative error of at most 0.0065.
Values may be sent and summed in bfloat16 or wider, within the bound.
No kernel may reach another device: no remote copies, remote signals or barrier semaphores. Data moves between devices by JAX's collectives and lax.ppermute only.
A program may use at most 128 MiB of HBM per device.

v0:
```python
import jax
import jax.numpy as jnp
from jax import lax
from jax.sharding import PartitionSpec as P

VIS_ROW = 4
CAP = 2


HIGHEST = lax.Precision.HIGHEST
APERTURE = 2.5


def profiles(centers, length):
    pixel_grid = jnp.arange(length).astype(jnp.float32)
    distance = pixel_grid[None, :] - centers.astype(jnp.float32)[:, None]
    return jnp.exp(-distance * distance / (2.0 * APERTURE * APERTURE)).astype(jnp.bfloat16)


def measure(received, row_block, col_prof):
    by_column = jnp.einsum("nyx,qx->nyq", received, col_prof, preferred_element_type=jnp.float32)
    return jnp.einsum("nyq,qy->nq", by_column, row_block.astype(jnp.float32), precision=HIGHEST)


def coadd_flux(matched, row_block, col_prof):
    by_column = jnp.dot(matched, col_prof.astype(jnp.float32).T, precision=HIGHEST)
    return jnp.einsum("yq,qy->q", by_column, row_block.astype(jnp.float32), precision=HIGHEST)


def match_after(stacked_share, kernel_rows, kernel_cols, row_offset, row_share):
    partial_value = jnp.dot(stacked_share, kernel_cols.T, precision=HIGHEST)
    own_rows = lax.dynamic_slice_in_dim(kernel_rows, row_offset, row_share, 0)
    return jnp.dot(
        own_rows, lax.all_gather(partial_value, "visit", axis=0, tiled=True), precision=HIGHEST
    )


def shards(
    images, warp_rows, warp_cols, tile_weight, tile_patch, match_rows, match_cols, src_row, src_col
):
    tile_count, tile_side, _ = images.shape
    visit_count = lax.axis_size("visit")
    patch_count = lax.axis_size("patch")
    row_share = tile_side // visit_count
    row_offset = lax.axis_index("visit") * row_share
    half_warp = jnp.einsum(
        "tij,tkj->tik", images, warp_cols, preferred_element_type=jnp.float32
    ).astype(jnp.bfloat16)
    warped = jnp.einsum(
        "tij,tjk->tik", warp_rows, half_warp, preferred_element_type=jnp.float32
    ).astype(jnp.bfloat16)
    tile_order = jnp.arange(tile_count)
    same_patch = (tile_patch[:, None] == tile_patch[None, :]) & (
        tile_order[None, :] < tile_order[:, None]
    )
    slot_index = jnp.sum(same_patch.astype(jnp.int32), axis=1)
    target = tile_patch * CAP + slot_index
    row_prof = profiles(src_row[0], tile_side)
    col_prof = profiles(src_col[0], tile_side)
    source_count = row_prof.shape[0]
    kernel_rows = match_rows[0]
    kernel_cols = match_cols[0]
    outgoing_weight = jnp.zeros((patch_count * CAP,), jnp.bfloat16).at[target].set(tile_weight)
    row_block = lax.dynamic_slice_in_dim(row_prof, row_offset, row_share, 1)
    row_pieces = warped.reshape(tile_count, visit_count, row_share, tile_side).transpose(1, 0, 2, 3)
    outgoing = (
        jnp.zeros((visit_count, patch_count * CAP, row_share, tile_side), jnp.bfloat16)
        .at[:, target]
        .set(row_pieces)
    )
    spread_weight = jnp.broadcast_to(outgoing_weight[None, :], (visit_count, patch_count * CAP))
    received, received_weight = (
        lax.all_to_all(
            outgoing.reshape(visit_count * patch_count, CAP, row_share, tile_side),
            ("visit", "patch"),
            split_axis=0,
            concat_axis=0,
            tiled=True,
        ),
        lax.all_to_all(
            spread_weight.reshape(visit_count * patch_count, CAP),
            ("visit", "patch"),
            split_axis=0,
            concat_axis=0,
            tiled=True,
        ),
    )
    slot_total = visit_count * patch_count * CAP
    received = received.reshape(slot_total, row_share, tile_side)
    received_weight = received_weight.reshape(-1).astype(jnp.float32)
    stacked = jnp.sum(received_weight[:, None, None] * received.astype(jnp.float32), axis=0)
    weight_all = jnp.sum(received_weight)
    fluxes = measure(received, row_block, col_prof)
    matched = match_after(stacked, kernel_rows, kernel_cols, row_offset, row_share)
    coadd = matched / weight_all
    flux_part = coadd_flux(matched, row_block, col_prof) / weight_all
    returned, returned_template = (
        lax.all_to_all(
            fluxes.reshape(visit_count * patch_count, CAP, source_count),
            ("visit", "patch"),
            split_axis=0,
            concat_axis=0,
            tiled=True,
        ),
        lax.all_to_all(
            jnp.broadcast_to(
                flux_part[None, None, :], (visit_count * patch_count, 1, source_count)
            ),
            ("visit", "patch"),
            split_axis=0,
            concat_axis=0,
            tiled=True,
        ),
    )
    returned = jnp.sum(returned.reshape(visit_count, patch_count * CAP, source_count), axis=0)
    returned_template = jnp.sum(
        returned_template.reshape(visit_count, patch_count, source_count), axis=0
    )
    tile_flux = returned[target]
    tile_ref = returned_template[tile_patch]
    visit_local = tile_order % VIS_ROW
    visit_pick = (visit_local[:, None] == jnp.arange(VIS_ROW)[None, :]).astype(jnp.float32)
    numerator = jnp.dot(visit_pick.T, jnp.sum(tile_flux * tile_ref, axis=1), precision=HIGHEST)
    denominator = jnp.dot(visit_pick.T, jnp.sum(tile_ref * tile_ref, axis=1), precision=HIGHEST)
    numerator_all, denominator_all = lax.psum((numerator, denominator), "patch")
    zero_point = numerator_all / denominator_all
    flux_resid = tile_flux - zero_point[visit_local][:, None] * tile_ref
    return (coadd[None], zero_point, flux_resid)


def solution(mesh):
    in_specs = (
        P(("visit", "patch"), None, None),
        P(("visit", "patch"), None, None),
        P(("visit", "patch"), None, None),
        P(("visit", "patch")),
        P(("visit", "patch")),
        P("patch", None, None),
        P("patch", None, None),
        P("patch", None),
        P("patch", None),
    )
    out_specs = (P("patch", "visit", None), P("visit"), P(("visit", "patch"), None))
    return jax.shard_map(shards, mesh=mesh, in_specs=in_specs, out_specs=out_specs, check_vma=False)
```

profile of v0, /device:TPU:0, one launch (start us, length us, event | category | flops | bytes accessed | tf_op | source)
XLA Modules:
  0.0 322.4 jit_solution(7391711750597145678)
XLA Ops:
  7.2 0.9 convert_reduce_fusion
  8.1 0.7 compare_select_fusion.1
  8.8 0.7 scatter_custom_fusion
  9.8 0.7 copy.25
  10.5 7.3 %all-to-all-start = ((bf16[32,1,2]{2,1,0:T(2,128)(2,1)}), bf16[32,1,2]{2,1,0:T(2,128)(2,1)S(1)}, u32[]{:S(2)}, u32[]{:S(2)}) async-start(bf16[32,1,2]{2,1,0:T(2,128)(2,1)} %copy.25), calls=%async_computation | async-start | bytes 32768 | tf_op jit(solution)/shard_map/all_to_all | solution.py:80
  17.8 11.1 %fusion.2 = bf16[8,512,512]{1,2,0:T(8,128)(2,1)} fusion(bf16[8,512,512]{2,1,0:T(8,128)(2,1)} %param.10, bf16[8,512,512]{2,1,0:T(8,128)(2,1)} %param.9, bf16[8,512,512]{2,1,0:T(8,128)(2,1)} %param.11), kind=kOutput, calls=%fused_computation.9 | convolution fusion | flops 4299161600 | bytes 16777216 | tf_op jit(solution)/shard_map/tij,tjk->tik/dot_general | solution.py:49
  29.0 4.2 %broadcast_in_dim.17 = bf16[4,16,128,512]{3,2,1,0:T(8,128)(2,1)} broadcast(bf16[]{:T(256)} %constant.36.clone.1), dimensions={} | broadcast | bytes 8388610 | tf_op jit(solution)/shard_map/broadcast_in_dim | solution.py:67
  33.2 10.8 %scatter_fusion = bf16[4,16,128,512]{3,2,1,0:T(8,128)(2,1)} fusion(bf16[4,16,128,512]{3,2,1,0:T(8,128)(2,1)} %broadcast_in_dim.17, s32[8]{0:T(128)S(1)} %get-tuple-element.10, bf16[8,4,128,512]{3,2,1,0:T(8,128)(2,1)} %bitcast.48), kind=kCustom, calls=%fused_computation.4 | custom fusion | bytes 12582944 | tf_op jit(solution)/shard_map/scatter | solution.py:69
  44.0 6.0 %all-to-all-start.1 = ((bf16[32,2,128,512]{3,2,1,0:T(8,128)(2,1)}), bf16[32,2,128,512]{3,2,1,0:T(8,128)(2,1)}, u32[]{:S(2)}, u32[]{:S(2)}) async-start(bf16[32,2,128,512]{3,2,1,0:T(8,128)(2,1)} %bitcast.47), calls=%async_computation.1 | async-start | bytes 16777216 | tf_op jit(solution)/shard_map/all_to_all | solution.py:73
  50.1 189.5 %all-to-all-done.1 = bf16[32,2,128,512]{3,2,1,0:T(8,128)(2,1)} async-done(((bf16[32,2,128,512]{3,2,1,0:T(8,128)(2,1)}), bf16[32,2,128,512]{3,2,1,0:T(8,128)(2,1)}, u32[]{:S(2)}, u32[]{:S(2)}) %all-to-all-start.1) | async-done | bytes 8388640 | tf_op jit(solution)/shard_map/all_to_all | solution.py:73
  239.5 5.4 %multiply_reduce_fusion.1 = f32[128,512]{1,0:T(8,128)S(1)} fusion(bf16[32,2,128,512]{3,2,1,0:T(8,128)(2,1)} %all-to-all-done.1, f32[32,2]{1,0:T(8,128)S(1)} %bitcast.50), kind=kLoop, calls=%fused_computation.6 | loop fusion | flops 12517376 | bytes 8651008 | tf_op jit(solution)/shard_map/reduce_sum | solution.py:91
  245.0 1.9 fusion.10
  247.0 0.6 convert_reduce_fusion.1
  247.7 12.6 %all-gather.2.cloned.1.call-done = f32[512,512]{1,0:T(8,128)} async-done(((f32[128,512]{1,0:T(8,128)}), f32[512,512]{1,0:T(8,128)}) %all-gather.2.cloned.1.call-update) | async-done | bytes 1048592 | tf_op jit(solution)/shard_map/all_gather | solution.py:34
  260.3 2.0 fusion.18
  262.3 0.8 convolution_bitcast_fusion
  263.3 0.2 fusion.21
  263.5 0.1 copy.41
  263.7 0.7 broadcast_divide_fusion
  264.3 0.7 broadcast_in_dim.19
  265.0 4.8 %all-to-all-start.3 = ((f32[32,1,512]{2,1,0:T(1,128)}), f32[32,1,512]{2,1,0:T(1,128)S(1)}, u32[]{:S(2)}, u32[]{:S(2)}) async-start(f32[32,1,512]{2,1,0:T(1,128)} %broadcast_in_dim.19), calls=%async_computation.3 | async-start | bytes 131072 | tf_op jit(solution)/shard_map/all_to_all | solution.py:105
  269.8 8.6 %multiply_reduce_fusion = f32[512,64]{0,1:T(8,128)S(1)} fusion(bf16[64,128,512]{2,1,0:T(8,128)(2,1)} %bitcast.10, f32[512,128]{0,1:T(8,128)S(1)} %copy.41, f32[512]{0:T(512)S(1)} %bitcast.53, f32[512]{0:T(512)S(1)} %iota_convert_fusion), kind=kOutput, calls=%fused_computation.5 | convolution fusion | flops 4304633856 | bytes 8785920 | tf_op jit(solution)/shard_map/nyx,qx->nyq/dot_general | solution.py:21
  278.4 0.7 reshape.101
  279.1 5.7 %all-to-all-start.2 = ((f32[32,2,512]{2,1,0:T(2,128)}), f32[32,2,512]{2,1,0:T(2,128)S(1)}, u32[]{:S(2)}, u32[]{:S(2)}) async-start(f32[32,2,512]{2,1,0:T(2,128)} %reshape.101), calls=%async_computation.2 | async-start | bytes 262144 | tf_op jit(solution)/shard_map/all_to_all | solution.py:98
  284.9 0.6 gather_fusion.1
  285.4 7.1 %all-to-all-done.2 = f32[32,2,512]{2,1,0:T(2,128)S(1)} async-done(((f32[32,2,512]{2,1,0:T(2,128)}), f32[32,2,512]{2,1,0:T(2,128)S(1)}, u32[]{:S(2)}, u32[]{:S(2)}) %all-to-all-start.2) | async-done | bytes 131104 | tf_op jit(solution)/shard_map/all_to_all | solution.py:98
  292.7 0.6 gather_fusion
  293.2 0.1 multiply_reduce_fusion.3
  293.6 1.4 divide_bitcast_fusion
  295.0 19.2 %all-reduce = (f32[4]{0:T(128)S(1)}, f32[4]{0:T(128)S(1)}) all-reduce(f32[4]{0:T(128)S(1)} %convolution_bitcast_fusion.2, f32[4]{0:T(128)S(1)} %convolution_bitcast_fusion.1), channel_id=1, replica_groups=mesh['visit'=4,'patch'=8] {'patch'}, use_global_device_ids=true, to_apply=%region_8.9 | all-reduce | flops 8 | bytes 64 | tf_op jit(solution)/shard_map/psum | solution.py:125
  314.2 0.6 gather_fusion.2
  314.9 0.7 multiply_subtract_fusion
  (32 shorter events, 1.0 us)
Async XLA Ops:
  7.2 237.8 %copy-start = (f32[1,512,512]{2,1,0:T(8,128)S(1)}, f32[1,512,512]{2,1,0:T(8,128)}, u32[]{:S(2)}) copy-start(f32[1,512,512]{2,1,0:T(8,128)} %param.15) | copy-start | bytes 3145732
  10.5 33.4 %all-to-all-start = ((bf16[32,1,2]{2,1,0:T(2,128)(2,1)}), bf16[32,1,2]{2,1,0:T(2,128)(2,1)S(1)}, u32[]{:S(2)}, u32[]{:S(2)}) async-start(bf16[32,1,2]{2,1,0:T(2,128)(2,1)} %copy.25), calls=%async_computation | async-start | bytes 32768 | tf_op jit(solution)/shard_map/all_to_all | solution.py:80
  44.0 195.5 %all-to-all-start.1 = ((bf16[32,2,128,512]{3,2,1,0:T(8,128)(2,1)}), bf16[32,2,128,512]{3,2,1,0:T(8,128)(2,1)}, u32[]{:S(2)}, u32[]{:S(2)}) async-start(bf16[32,2,128,512]{3,2,1,0:T(8,128)(2,1)} %bitcast.47), calls=%async_computation.1 | async-start | bytes 16777216 | tf_op jit(solution)/shard_map/all_to_all | solution.py:73
  50.0 210.3 %all-gather.2.cloned.1.call-start = ((), (), s32[]{:S(2)}) async-start(), calls=%async_computation.4 | async-start | bytes 1310720 | tf_op jit(solution)/shard_map/all_gather | solution.py:34
  239.5 7.4 %copy-start.2 = (s32[1,512]{1,0:T(1,128)S(1)}, s32[1,512]{1,0:T(1,128)}, u32[]{:S(2)}) copy-start(s32[1,512]{1,0:T(1,128)} %param.17) | copy-start | bytes 6148
  239.5 7.4 %copy-start.3 = (s32[1,512]{1,0:T(1,128)S(1)}, s32[1,512]{1,0:T(1,128)}, u32[]{:S(2)}) copy-start(s32[1,512]{1,0:T(1,128)} %param.16) | copy-start | bytes 6148
  265.0 14.1 %all-to-all-start.3 = ((f32[32,1,512]{2,1,0:T(1,128)}), f32[32,1,512]{2,1,0:T(1,128)S(1)}, u32[]{:S(2)}, u32[]{:S(2)}) async-start(f32[32,1,512]{2,1,0:T(1,128)} %broadcast_in_dim.19), calls=%async_computation.3 | async-start | bytes 131072 | tf_op jit(solution)/shard_map/all_to_all | solution.py:105
  279.1 13.4 %all-to-all-start.2 = ((f32[32,2,512]{2,1,0:T(2,128)}), f32[32,2,512]{2,1,0:T(2,128)S(1)}, u32[]{:S(2)}, u32[]{:S(2)}) async-start(f32[32,2,512]{2,1,0:T(2,128)} %reshape.101), calls=%async_computation.2 | async-start | bytes 262144 | tf_op jit(solution)/shard_map/all_to_all | solution.py:98
  314.2 1.3 copy-start.1
Sparse Core Ops, SparseCore 0:
  247.0 13.2 all-gather.1
where the time goes:
time: 323 us; the launch traced here: 322 us
  waiting for transfers between devices  209 us (65%)
  matrix products  24.7 us (8%)
  starting transfers between devices  23.8 us (7%)
  local copies, waits for them, and re-layouts  20.3 us (6%)
  blocking collectives  19.2 us (6%)
  between operations  14.2 us (4%)
  other arithmetic  10.9 us (3%)
    all_to_all x1, waiting for transfers between devices, shards(): lax.all_to_all(outgoing.reshape(visit_count * patch_count, CAP, row_share...  189 us
    psum x1, blocking collectives, shards(): numerator_all, denominator_all = lax.psum((numerator, denominator), 'patch')  19.2 us
    all_gather x1, waiting for transfers between devices, match_after(): lax.all_gather(partial_value, 'visit', axis=0, tiled=True)  12.6 us
    dot_general x1, matrix products, shards(): jnp.einsum('tij,tjk->tik', warp_rows, half_warp, preferred_element_type=j...  11.1 us
    scatter x1, local copies, waits for them, and re-layouts, shards(): outgoing = jnp.zeros((visit_count, patch_count * CAP, row_share, tile_sid...  10.8 us
    dot_general x1, matrix products, measure(): jnp.einsum('nyx,qx->nyq', received, col_prof, preferred_element_type=jnp....  8.6 us
    all_to_all x1, starting transfers between devices, shards(): lax.all_to_all(spread_weight.reshape(visit_count * patch_count, CAP), ('v...  7.3 us
    all_to_all x1, waiting for transfers between devices, shards(): lax.all_to_all(fluxes.reshape(visit_count * patch_count, CAP, source_coun...  7.13 us
  transfers between devices with their start and end apart: 5, of which 3 were waited for; matrix products, arithmetic and copies ran while one was open for 11% of the time, Pallas kernels for 0%

commit v1 on v0

v1 whole, which is shorter than its diff:
```python
import functools

import jax
import jax.numpy as jnp
from jax import lax
from jax.experimental import pallas as pl
from jax.experimental.pallas import tpu as pltpu
from jax.sharding import PartitionSpec as P

VIS_ROW = 4
APERTURE = 2.5
HIGHEST = lax.Precision.HIGHEST
F32 = jnp.float32
BF16 = jnp.bfloat16
AXES = ("visit", "patch")
EXPONENT = -1.4426950408889634 / (2.0 * APERTURE * APERTURE)
VMEM_LIMIT = 56 * 1024 * 1024
NT = (((1,), (1,)), ((), ()))
TN = (((0,), (0,)), ((), ()))


class Layout:
    def __init__(self, tiles, side):
        self.tiles, self.side = tiles, side
        self.visits, self.patches = lax.axis_size("visit"), lax.axis_size("patch")
        self.group = self.visits // 2
        self.highs = self.patches // self.group
        self.width = side // self.visits
        self.part = self.width // 2
        self.rows = self.part * self.visits

    def place(self):
        visit, patch = lax.axis_index("visit"), lax.axis_index("patch")
        return visit % 2, visit // 2, patch // self.group, patch % self.group

    def permute(self, array, partner):
        pairs = []
        for visit in range(self.visits):
            for patch in range(self.patches):
                x, core, high, low = partner(visit // 2, visit % 2, patch // self.group, patch % self.group)
                target = (2 * x + core) * self.patches + self.group * high + low
                pairs.append((visit * self.patches + patch, target))
        return lax.ppermute(array, AXES, pairs)

    def swap_core(self, array):
        return self.permute(array, lambda x, core, high, low: (x, 1 - core, high, low))

    def swap_first(self, array, step):
        def partner(x, core, high, low):
            return (x ^ step, core, high, low) if core == 0 else (x, core, high, low ^ step)

        return self.permute(array, partner)

    def swap_second(self, array, step):
        def partner(x, core, high, low):
            return (x, core, high, low ^ step) if core == 0 else (x ^ step, core, high, low)

        return self.permute(array, partner)

    def swap_low(self, array, step):
        return self.permute(array, lambda x, core, high, low: (x, core, high, low ^ step))

    def swap_high(self, array, step):
        return self.permute(array, lambda x, core, high, low: (x, core, high ^ step, low))

    def swap_visit(self, array, step):
        def partner(x, core, high, low):
            visit = (2 * x + core) ^ step
            return visit // 2, visit % 2, high, low

        return self.permute(array, partner)


def warp_kernel(lay, patch_ref, weight_ref, image, rows, cols, warped, send, keep, total):
    tile = pl.program_id(0)

    @pl.when(tile == 0)
    def _():
        total[...] = jnp.zeros_like(total)

    cols_part = cols[0].reshape(lay.rows, lay.side)
    half = lax.dot_general(cols_part, image[0], NT, preferred_element_type=F32).astype(BF16)
    result = lax.dot_general(half, rows[0], NT, preferred_element_type=F32).astype(BF16)
    warped[0] = result
    total[patch_ref[tile]] += weight_ref[tile] * result.astype(F32)

    @pl.when(tile == lay.tiles - 1)
    def _():
        core = lax.axis_index("visit") % 2
        for out, own in ((send, 1 - core), (keep, core)):
            for first in range(lay.group):
                for second in range(lay.group):
                    x = jnp.where(own == 0, first, second)
                    low = jnp.where(own == 0, second, first)
                    start = pl.multiple_of((2 * x + own) * lay.part, lay.part)
                    for high in range(lay.highs):
                        block = total[high * lay.group + low, pl.ds(start, lay.part), :]
                        out[first, second, high] = block.astype(BF16)


def warp(lay, part, tile_patch, weight, images, warp_rows, cols):
    tiles, side = lay.tiles, lay.side
    pieces = (lay.group, lay.group, lay.highs, lay.part, side)
    whole = lambda tile, *_: (0, 0, 0, 0, 0)
    return pl.pallas_call(
        functools.partial(warp_kernel, lay),
        grid_spec=pltpu.PrefetchScalarGridSpec(
            num_scalar_prefetch=2,
            grid=(tiles,),
            in_specs=[
                pl.BlockSpec((1, side, side), lambda tile, *_: (tile, 0, 0)),
                pl.BlockSpec((1, side, side), lambda tile, *_: (tile, 0, 0)),
                pl.BlockSpec((1, lay.visits, None, lay.part, side), lambda tile, *_: (tile, 0, part, 0, 0)),
            ],
            out_specs=[
                pl.BlockSpec((1, lay.rows, side), lambda tile, *_: (tile, 0, 0)),
                pl.BlockSpec(pieces, whole),
                pl.BlockSpec(pieces, whole),
            ],
            scratch_shapes=[pltpu.VMEM((lay.patches, lay.rows, side), F32)],
        ),
        out_shape=[
            jax.ShapeDtypeStruct((tiles, lay.rows, side), BF16),
            jax.ShapeDtypeStruct(pieces, BF16),
            jax.ShapeDtypeStruct(pieces, BF16),
        ],
        compiler_params=pltpu.CompilerParams(vmem_limit_bytes=VMEM_LIMIT),
        cost_estimate=pl.CostEstimate(
            flops=4 * tiles * lay.rows * side * side, bytes_accessed=6 * tiles * side * side, transcendentals=0
        ),
        name="warp",
    )(tile_patch, weight, images, warp_rows, cols)


def profile(position, centers):
    distance = position - centers
    return jnp.exp2(distance * distance * EXPONENT).astype(BF16)


def flux_kernel(lay, patch_ref, place_ref, warped_a, warped_b, src_row, src_col, flux, sums):
    tile = pl.program_id(0)
    side = lay.side

    @pl.when(tile == 0)
    def _():
        sums[...] = jnp.zeros_like(sums)

    row_prof = profile(lax.broadcasted_iota(jnp.int32, (side, side), 0).astype(F32), src_row[0])
    local = lax.broadcasted_iota(jnp.int32, (lay.rows, side), 0)
    value = jnp.zeros((1, side), F32)
    for part, warped in enumerate((warped_a, warped_b)):
        by_row = jnp.dot(warped[0], row_prof, preferred_element_type=F32)
        column = (local // lay.part) * lay.width + part * lay.part + local % lay.part
        col_prof = profile(column.astype(F32), src_col[0])
        value += jnp.sum(by_row * col_prof.astype(F32), axis=0, keepdims=True)
    flux[0] = value
    spot = (tile % VIS_ROW) * lay.patches + patch_ref[tile]
    sums[pl.ds(spot, 1), :] += value


def forced_flux(lay, tile_patch, tile_place, warped_a, warped_b, src_row, src_col):
    tiles, side = lay.tiles, lay.side
    return pl.pallas_call(
        functools.partial(flux_kernel, lay),
        grid_spec=pltpu.PrefetchScalarGridSpec(
            num_scalar_prefetch=2,
            grid=(tiles,),
            in_specs=[
                pl.BlockSpec((1, lay.rows, side), lambda tile, *_: (tile, 0, 0)),
                pl.BlockSpec((1, lay.rows, side), lambda tile, *_: (tile, 0, 0)),
                pl.BlockSpec((1, 1, side), lambda tile, patch, place: (place[tile], 0, 0)),
                pl.BlockSpec((1, 1, side), lambda tile, patch, place: (place[tile], 0, 0)),
            ],
            out_specs=[
                pl.BlockSpec((1, 1, side), lambda tile, *_: (tile, 0, 0)),
                pl.BlockSpec((VIS_ROW * lay.patches, side), lambda tile, *_: (0, 0)),
            ],
        ),
        out_shape=[
            jax.ShapeDtypeStruct((tiles, 1, side), F32),
            jax.ShapeDtypeStruct((VIS_ROW * lay.patches, side), F32),
        ],
        compiler_params=pltpu.CompilerParams(vmem_limit_bytes=VMEM_LIMIT),
        cost_estimate=pl.CostEstimate(
            flops=2 * tiles * side**3, bytes_accessed=2 * tiles * side * side, transcendentals=2 * tiles * side * side
        ),
        name="forced_flux",
    )(tile_patch, tile_place, warped_a, warped_b, src_row, src_col)


def prepare_kernel(lay, src_row, src_col, match_cols, row_prof, col_match):
    position = lax.broadcasted_iota(jnp.int32, (lay.side, lay.side), 0).astype(F32)
    row_prof[...] = profile(position, src_row[...])
    col_prof = profile(position, src_col[...]).astype(F32)
    product = lax.dot_general(match_cols[...], col_prof, TN, precision=HIGHEST, preferred_element_type=F32)
    col_match[...] = product.reshape(lay.visits, lay.width, lay.side)


def prepare(lay, src_row, src_col, match_cols):
    side = lay.side
    return pl.pallas_call(
        functools.partial(prepare_kernel, lay),
        out_shape=[
            jax.ShapeDtypeStruct((side, side), BF16),
            jax.ShapeDtypeStruct((lay.visits, lay.width, side), F32),
        ],
        compiler_params=pltpu.CompilerParams(vmem_limit_bytes=VMEM_LIMIT),
        cost_estimate=pl.CostEstimate(
            flops=12 * side**3, bytes_accessed=10 * side * side, transcendentals=2 * side * side
        ),
        name="prepare",
    )(src_row, src_col, match_cols)


def match_kernel(lay, extra, stacked_a, stacked_b, match_rows, row_prof, col_match, weight, message):
    side, width = lay.side, lay.width
    visit = lax.axis_index("visit")
    stacked = jnp.concatenate([stacked_a[...], stacked_b[...]], axis=0)
    matched = lax.dot_general(match_rows[...], stacked, NT, precision=HIGHEST, preferred_element_type=F32)
    by_row = lax.dot_general(
        matched.T, row_prof[...].astype(F32), (((1,), (0,)), ((), ())), precision=HIGHEST, preferred_element_type=F32
    )
    flux = jnp.sum(by_row * col_match[visit], axis=0, keepdims=True)
    tail = jnp.concatenate(
        [flux[:, block * width : (block + 1) * width] for block in range(lay.visits)]
        + [jnp.broadcast_to(weight[...], (extra - lay.visits, width))],
        axis=0,
    )
    for block in range(lay.visits):
        message[block, :width] = matched[block * width : (block + 1) * width]
        message[block, width:] = tail


def match(lay, extra, stacked_a, stacked_b, match_rows, row_prof, col_match, weight):
    side, width = lay.side, lay.width
    return pl.pallas_call(
        functools.partial(match_kernel, lay, extra),
        out_shape=jax.ShapeDtypeStruct((lay.visits, width + extra, width), F32),
        compiler_params=pltpu.CompilerParams(vmem_limit_bytes=VMEM_LIMIT),
        cost_estimate=pl.CostEstimate(
            flops=24 * width * side * side, bytes_accessed=8 * side * side, transcendentals=0
        ),
        name="match",
    )(stacked_a, stacked_b, match_rows, row_prof, col_match, weight)


def finish_kernel(lay, patch_ref, counts, flux, sums, *refs):
    messages, zero, resid, table = refs[: lay.highs], refs[-3], refs[-2], refs[-1]
    patch = lax.axis_index("patch")
    high, low = patch // lay.group, patch % lay.group
    for step_high in range(lay.highs):
        for step_low in range(lay.group):
            data = messages[step_high][step_low]
            rows = data[: lay.visits] / data[lay.visits : lay.visits + 1]
            spot = (high ^ step_high) * lay.group + (low ^ step_low)
            line = jnp.concatenate([rows[block : block + 1] for block in range(lay.visits)], axis=1)
            table[pl.ds(spot, 1), :] = line
    reference = table[...]
    squares = jnp.sum(reference * reference, axis=1, keepdims=True)
    scales = []
    for visit in range(VIS_ROW):
        numerator = jnp.sum(sums[visit * lay.patches : (visit + 1) * lay.patches] * reference, keepdims=True)
        denominator = jnp.sum(counts[visit * lay.patches : (visit + 1) * lay.patches] * squares, keepdims=True)
        scales.append(numerator / denominator)
        zero[visit : visit + 1, :] = jnp.broadcast_to(scales[-1], (1, zero.shape[1]))
    for tile in range(lay.tiles):
        own = table[pl.ds(patch_ref[tile], 1), :]
        resid[tile : tile + 1, :] = flux[tile] - scales[tile % VIS_ROW] * own


def finish(lay, tile_patch, counts, flux, sums, messages):
    vmem = pl.BlockSpec(memory_space=pltpu.VMEM)
    return pl.pallas_call(
        functools.partial(finish_kernel, lay),
        in_specs=[pl.BlockSpec(memory_space=pltpu.SMEM)] + [vmem] * (3 + len(messages)),
        out_specs=[vmem, vmem],
        out_shape=[
            jax.ShapeDtypeStruct((VIS_ROW, 128), F32),
            jax.ShapeDtypeStruct((lay.tiles, lay.side), F32),
        ],
        scratch_shapes=[pltpu.VMEM((lay.patches, lay.side), F32)],
        name="finish",
    )(tile_patch, counts, flux, sums, *messages)


def pick(array, index):
    return lax.dynamic_index_in_dim(array, index, 0, keepdims=False).astype(F32)


def scatter_sum(lay, send, keep):
    core, x, high, low = lay.place()
    first = jnp.where(core == 0, x, low)
    second = jnp.where(core == 0, low, x)
    terms = [keep, lay.swap_core(send)]
    for index, size, swap in (
        (first, lay.group, lay.swap_first),
        (second, lay.group, lay.swap_second),
        (high, lay.highs, lay.swap_high),
    ):
        received = []
        for step in range(1, size):
            outgoing = sum(pick(term, index ^ step) for term in terms).astype(BF16)
            received.append(swap(outgoing, step))
        terms = [sum(pick(term, index) for term in terms)] + received
    return sum(term.astype(F32) for term in terms)


def gather_patch(lay, array):
    near = jnp.stack([array] + [lay.swap_low(array, step) for step in range(1, lay.group)])
    return [near] + [lay.swap_high(near, step) for step in range(1, lay.highs)]


def sum_patch(lay, array):
    array = sum([lay.swap_low(array, step) for step in range(1, lay.group)], array)
    return sum([lay.swap_high(array, step) for step in range(1, lay.highs)], array)


def shards(
    images, warp_rows, warp_cols, tile_weight, tile_patch, match_rows, match_cols, src_row, src_col
):
    lay = Layout(images.shape[0], images.shape[1])
    tiles, side = lay.tiles, lay.side
    core, x, high, low = lay.place()
    visit, patch = lax.axis_index("visit"), lax.axis_index("patch")
    weight = tile_weight.astype(F32)
    cols = warp_cols.reshape(tiles, lay.visits, 2, lay.part, side)

    warped_a, send_a, keep_a = warp(lay, 0, tile_patch, weight, images, warp_rows, cols)
    warped_b, send_b, keep_b = warp(lay, 1, tile_patch, weight, images, warp_rows, cols)

    named = (tile_patch[:, None] == jnp.arange(lay.patches)[None, :]).astype(F32)
    local_counts = jnp.sum(named.reshape(tiles // VIS_ROW, VIS_ROW, lay.patches), axis=0).reshape(-1)
    local_weight = jnp.sum(named * weight[:, None], axis=0)
    extras = jnp.concatenate([local_counts, local_weight])
    extras = jnp.pad(extras, (0, side - extras.shape[0]))
    sources = jnp.stack([src_row[0].astype(F32), src_col[0].astype(F32), extras])
    gathered = jnp.stack(gather_patch(lay, sources)).reshape(lay.patches, 3, side)
    all_rows, all_cols = gathered[:, 0:1, :], gathered[:, 1:2, :]
    extras = jnp.sum(gathered[:, 2, :], axis=0)
    counts = extras[: VIS_ROW * lay.patches].reshape(VIS_ROW * lay.patches, 1)
    weight_part = lax.dynamic_slice_in_dim(extras, VIS_ROW * lay.patches + patch, 1, 0).reshape(1, 1)
    tile_place = ((tile_patch // lay.group) ^ high) * lay.group + ((tile_patch % lay.group) ^ low)

    stacked_a = scatter_sum(lay, send_a, keep_a)
    stacked_b = scatter_sum(lay, send_b, keep_b)

    flux, sums = forced_flux(lay, tile_patch, tile_place, warped_a, warped_b, all_rows, all_cols)
    sums = sum_patch(lay, sums)
    row_prof, col_match = prepare(lay, src_row.astype(F32), src_col.astype(F32), match_cols[0])

    extra = -(-(lay.visits + 1) // 8) * 8
    width = lay.width
    message = match(lay, extra, stacked_a, stacked_b, match_rows[0], row_prof, col_match, weight_part)
    parts = [pick(message, visit)]
    parts += [lay.swap_visit(pick(message, visit ^ step), step) for step in range(1, lay.visits)]
    reference = sum(part[width:] for part in parts)
    messages = gather_patch(lay, reference)

    by_visit = match_cols[0].reshape(side, lay.visits, width).transpose(1, 0, 2)
    coadd = sum(
        lax.dot_general(
            part[:width],
            lax.dynamic_index_in_dim(by_visit, visit ^ step, 0, keepdims=False),
            NT,
            precision=HIGHEST,
            preferred_element_type=F32,
        )
        for step, part in enumerate(parts)
    )
    coadd = coadd / reference[lay.visits, 0]

    zero, resid = finish(lay, tile_patch, counts, flux, sums, messages)
    return (coadd[None], zero[:, 0], resid)


def solution(mesh):
    in_specs = (
        P(AXES, None, None),
        P(AXES, None, None),
        P(AXES, None, None),
        P(AXES),
        P(AXES),
        P("patch", None, None),
        P("patch", None, None),
        P("patch", None),
        P("patch", None),
    )
    out_specs = (P("patch", "visit", None), P("visit"), P(AXES, None))
    return jax.shard_map(shards, mesh=mesh, in_specs=in_specs, out_specs=out_specs, check_vma=False)
```

time: 323 us -> 121 us (0.37)
  waiting for transfers between devices: 209 us -> 20.9 us
  Pallas kernels: 0 us -> 42.3 us
  matrix products: 24.7 us -> 3.7 us
  blocking collectives: 19.2 us -> 0 us
  between operations: 14.2 us -> 0.95 us
  local copies, waits for them, and re-layouts: 20.3 us -> 7.08 us
  starting transfers between devices: 23.8 us -> 30.6 us
    all_to_all x4 -> x0, waiting for transfers between devices: 197 us -> none  [the longest x1 189 us: shards(): lax.all_to_all(outgoing.reshape(visit_count * patch_count, CAP, row_share...]
    pallas_call x0 -> x6, Pallas kernels: none -> 42.3 us  [the longest x2 22.2 us: warp(): pl.pallas_call(functools.partial(warp_kernel, lay), grid_spec=pltpu.Prefe...]
    ppermute x0 -> x27, starting transfers between devices: none -> 30.6 us  [permute(): return lax.ppermute(array, AXES, pairs)]
    all_to_all x4 -> x0, starting transfers between devices: 23.7 us -> none  [the longest x1 7.3 us: shards(): lax.all_to_all(spread_weight.reshape(visit_count * patch_count, CAP), ('v...]
    dot_general x7 -> x4, matrix products: 24.7 us -> 3.7 us  [shards(): lax.dot_general(part[:width], lax.dynamic_index_in_dim(by_visit, visit ^...]
    ppermute x0 -> x27, waiting for transfers between devices: none -> 20.9 us  [permute(): return lax.ppermute(array, AXES, pairs)]
    psum x1 -> x0, blocking collectives: 19.2 us -> none  [shards(): numerator_all, denominator_all = lax.psum((numerator, denominator), 'patch')]
    all_gather x1 -> x0, waiting for transfers between devices: 12.6 us -> none  [match_after(): lax.all_gather(partial_value, 'visit', axis=0, tiled=True)]
  transfers between devices with their start and end apart: 5 -> 27, of which waited for: 3 -> 10; matrix products, arithmetic and copies ran while one was open for 11% -> 15% of each run, Pallas kernels for 0% -> 20%
where the time goes in v1:
time: 121 us; the launch traced here: 119 us
  Pallas kernels  42.3 us (35%)
  starting transfers between devices  30.6 us (25%)
  waiting for transfers between devices  20.9 us (17%)
  other arithmetic  13.9 us (11%)
  local copies, waits for them, and re-layouts  7.08 us (6%)
  matrix products  3.7 us (3%)
    ppermute x27, starting transfers between devices, permute(): return lax.ppermute(array, AXES, pairs)  30.6 us
    pallas_call x2, Pallas kernels, warp(): pl.pallas_call(functools.partial(warp_kernel, lay), grid_spec=pltpu.Prefe...  22.2 us
    ppermute x27, waiting for transfers between devices, permute(): return lax.ppermute(array, AXES, pairs)  20.9 us
    pallas_call x1, Pallas kernels, forced_flux(): pl.pallas_call(functools.partial(flux_kernel, lay), grid_spec=pltpu.Prefe...  8.63 us
    convert_element_type x6, other arithmetic, scatter_sum(): outgoing = sum((pick(term, index ^ step) for term in terms)).astype(BF16)  7.72 us
    pallas_call x1, Pallas kernels, match(): pl.pallas_call(functools.partial(match_kernel, lay, extra), out_shape=jax...  5.44 us
    pallas_call x1, Pallas kernels, prepare(): pl.pallas_call(functools.partial(prepare_kernel, lay), out_shape=[jax.Sha...  4.23 us
    dot_general x4, matrix products, shards(): lax.dot_general(part[:width], lax.dynamic_index_in_dim(by_visit, visit ^...  3.7 us
  transfers between devices with their start and end apart: 27, of which 10 were waited for; matrix products, arithmetic and copies ran while one was open for 15% of the time, Pallas kernels for 20%

profile of v1, /device:TPU:0, one launch (start us, length us, event | category | flops | bytes accessed | tf_op | source)
XLA Modules:
  0.0 119.4 jit_solution(18251716092184926315)
XLA Ops:
  1.8 11.1 %warp.3 = (bf16[8,256,512]{2,1,0:T(8,128)(2,1)}, bf16[2,2,4,64,512]{4,3,2,1,0:T(8,128)(2,1)}, bf16[2,2,4,64,512]{4,3,2,1,0:T(8,128)(2,1)}) custom-call(s32[8]{0:T(128)} %patch_ref.7, f32[8]{0:T(128)} %convert_element_type.177.weight_ref, bf16[8,512,512]{2,1,0:T(8,128)(2,1)} %image.3, bf16[8,512,512]{2,1,0:T(8,128)(2,1)} %rows.3, ...), custom_call_target="tpu_custom_call" | custom-call | flops 2147483648 | bytes 12582912 | tf_op jit(solution)/shard_map/warp/pallas_call | solution.py:105
  13.5 11.1 %warp.2 = (bf16[8,256,512]{2,1,0:T(8,128)(2,1)}, bf16[2,2,4,64,512]{4,3,2,1,0:T(8,128)(2,1)}, bf16[2,2,4,64,512]{4,3,2,1,0:T(8,128)(2,1)}) custom-call(s32[8]{0:T(128)} %patch_ref.7, f32[8]{0:T(128)} %convert_element_type.177.weight_ref, bf16[8,512,512]{2,1,0:T(8,128)(2,1)} %image.3, bf16[8,512,512]{2,1,0:T(8,128)(2,1)} %rows.3, ...), custom_call_target="tpu_custom_call" | custom-call | flops 2147483648 | bytes 12582912 | tf_op jit(solution)/shard_map/warp/pallas_call | solution.py:105
  25.2 3.0 %collective-permute-start.12 = (f32[3,512]{1,0:T(4,128)S(1)}, f32[3,512]{1,0:T(4,128)S(1)}, u32[]{:S(2)}, u32[]{:S(2)}) collective-permute-start(f32[3,512]{1,0:T(4,128)S(1)} %get-tuple-element.54), channel_id=1, source_target_pairs={{0,1},{1,0},{2,3},{3,2},{4,5},{5,4},{6,7},{7,6},{8,9},{9,8},{10,11... | collective-permute-start | bytes 18440 | tf_op jit(solution)/shard_map/ppermute | solution.py:43
  28.7 4.2 %prepare.1 = (bf16[512,512]{1,0:T(8,128)(2,1)}, f32[4,128,512]{2,1,0:T(8,128)}) custom-call(f32[1,512]{1,0:T(1,128)} %copy-done.7, f32[1,512]{1,0:T(1,128)} %copy-done.8, f32[512,512]{1,0:T(8,128)} %bitcast.143), custom_call_target="tpu_custom_call" | custom-call | flops 1610612736 | bytes 2621440 | tf_op jit(solution)/shard_map/prepare/pallas_call | solution.py:201
  33.4 1.6 %collective-permute-start.13 = (f32[2,3,512]{2,1,0:T(4,128)S(1)}, f32[2,3,512]{2,1,0:T(4,128)S(1)}, u32[]{:S(2)}, u32[]{:S(2)}) collective-permute-start(f32[2,3,512]{2,1,0:T(4,128)S(1)} %get-tuple-element.52), channel_id=1, source_target_pairs={{0,2},{1,3},{2,0},{3,1},{4,6},{5,7},{6,4},{7,5},{8,10},{9,11},{10,... | collective-permute-start | bytes 36872 | tf_op jit(solution)/shard_map/ppermute | solution.py:43
  35.0 2.6 %collective-permute-start.14 = (f32[2,3,512]{2,1,0:T(4,128)S(1)}, f32[2,3,512]{2,1,0:T(4,128)S(1)}, u32[]{:S(2)}, u32[]{:S(2)}) collective-permute-start(f32[2,3,512]{2,1,0:T(4,128)S(1)} %get-tuple-element.52), channel_id=1, source_target_pairs={{0,4},{1,5},{2,6},{3,7},{4,0},{5,1},{6,2},{7,3},{8,12},{9,13},{10,... | collective-permute-start | bytes 36872 | tf_op jit(solution)/shard_map/ppermute | solution.py:43
  39.8 3.3 %collective-permute-done.15 = f32[2,3,512]{2,1,0:T(4,128)S(1)} collective-permute-done((f32[2,3,512]{2,1,0:T(4,128)S(1)}, f32[2,3,512]{2,1,0:T(4,128)S(1)}, u32[]{:S(2)}, u32[]{:S(2)}) %collective-permute-start.15) | collective-permute-done | bytes 12320 | tf_op jit(solution)/shard_map/ppermute | solution.py:43
  44.8 2.6 %fusion.4 = (bf16[2,4,64,512]{3,2,1,0:T(8,128)(2,1)}, f32[1,2,4,64,512]{4,3,2,1,0:T(8,128)S(1)}) fusion(bf16[2,2,4,64,512]{4,3,2,1,0:T(8,128)(2,1)} %copy-done.1, s32[]{:T(128)S(6)} %select_n.127, bf16[2,2,4,64,512]{4,3,2,1,0:T(8,128)(2,1)} %get-tuple-element.17, s32[]{:T(128)S(6)} %select_n.124), kind=kLoop, calls=%fused_computation.10 | loop fusion | flops 1835008 | bytes 3670024 | tf_op jit(solution)/shard_map/convert_element_type | solution.py:302
  47.4 1.5 %collective-permute-start.7 = (bf16[2,4,64,512]{3,2,1,0:T(8,128)(2,1)}, bf16[2,4,64,512]{3,2,1,0:T(8,128)(2,1)}, u32[]{:S(2)}, u32[]{:S(2)}) collective-permute-start(bf16[2,4,64,512]{3,2,1,0:T(8,128)(2,1)} %get-tuple-element.27), channel_id=1, source_target_pairs={{0,16},{1,17},{2,18},{3,19},{4,20},{5,21},{6,22},{7,23},{8,9},{9,8... | collective-permute-start | bytes 1572872 | tf_op jit(solution)/shard_map/ppermute | solution.py:43
  48.9 2.6 %fusion.3 = (bf16[2,4,64,512]{3,2,1,0:T(8,128)(2,1)}, f32[1,2,4,64,512]{4,3,2,1,0:T(8,128)S(1)}) fusion(bf16[2,2,4,64,512]{4,3,2,1,0:T(8,128)(2,1)} %collective-permute-done, s32[]{:T(128)S(6)} %select_n.127, bf16[2,2,4,64,512]{4,3,2,1,0:T(8,128)(2,1)} %get-tuple-element.15, s32[]{:T(128)S(6)} %select_n.124), kind=kLoop, calls=%fused_computation.9 | loop fusion | flops 1835008 | bytes 3670024 | tf_op jit(solution)/shard_map/convert_element_type | solution.py:302
  52.1 8.6 %forced_flux.1 = (f32[8,1,512]{2,1,0:T(1,128)}, f32[32,512]{1,0:T(8,128)}) custom-call(s32[8]{0:T(128)} %patch_ref.7, s32[8]{0:T(128)} %fusion.36.place_ref, bf16[8,256,512]{2,1,0:T(8,128)(2,1)} %get-tuple-element.21.warped_a, bf16[8,256,512]{2,1,0:T(8,128)(2,1)} %get-tuple-element.22.warped_b, f32[8,1,512]{2,1,0:T(1,128)} %get-tuple-element.49.src_row, ...), custom_call_target="tpu_custom_call" | custom-call | flops 2147483648 | bytes 4194304 | tf_op jit(solution)/shard_map/forced_flux/pallas_call | solution.py:163
  62.5 2.7 %collective-permute-done.19 = f32[32,512]{1,0:T(8,128)S(1)} collective-permute-done((f32[32,512]{1,0:T(8,128)}, f32[32,512]{1,0:T(8,128)S(1)}, u32[]{:S(2)}, u32[]{:S(2)}) %collective-permute-start.19) | collective-permute-done | bytes 65568 | tf_op jit(solution)/shard_map/ppermute | solution.py:43
  66.9 3.6 %collective-permute-start.22 = (f32[32,512]{1,0:T(8,128)S(1)}, f32[32,512]{1,0:T(8,128)S(1)}, u32[]{:S(2)}, u32[]{:S(2)}) collective-permute-start(f32[32,512]{1,0:T(8,128)S(1)} %add.263), channel_id=1, source_target_pairs={{0,6},{1,7},{2,4},{3,5},{4,2},{5,3},{6,0},{7,1},{8,14},{9,15},{10,... | collective-permute-start | bytes 196616 | tf_op jit(solution)/shard_map/ppermute | solution.py:43
  73.4 1.6 %collective-permute-start.2 = (bf16[4,64,512]{2,1,0:T(8,128)(2,1)S(1)}, bf16[4,64,512]{2,1,0:T(8,128)(2,1)S(1)}, u32[]{:S(2)}, u32[]{:S(2)}) collective-permute-start(bf16[4,64,512]{2,1,0:T(8,128)(2,1)S(1)} %get-tuple-element.33), channel_id=1, source_target_pairs={{0,1},{1,0},{2,3},{3,2},{4,5},{5,4},{6,7},{7,6},{8,24},{9,25},{10,... | collective-permute-start | bytes 786440 | tf_op jit(solution)/shard_map/ppermute | solution.py:43
  75.7 2.4 %collective-permute-done.8 = bf16[4,64,512]{2,1,0:T(8,128)(2,1)S(1)} collective-permute-done((bf16[4,64,512]{2,1,0:T(8,128)(2,1)S(1)}, bf16[4,64,512]{2,1,0:T(8,128)(2,1)S(1)}, u32[]{:S(2)}, u32[]{:S(2)}) %collective-permute-start.8) | collective-permute-done | bytes 262176 | tf_op jit(solution)/shard_map/ppermute | solution.py:43
  78.2 1.5 %collective-permute-start.11 = (bf16[64,512]{1,0:T(8,128)(2,1)S(1)}, bf16[64,512]{1,0:T(8,128)(2,1)S(1)}, u32[]{:S(2)}, u32[]{:S(2)}) collective-permute-start(bf16[64,512]{1,0:T(8,128)(2,1)S(1)} %get-tuple-element.40), channel_id=1, source_target_pairs={{0,6},{1,7},{2,4},{3,5},{4,2},{5,3},{6,0},{7,1},{8,14},{9,15},{10,... | collective-permute-start | bytes 196616 | tf_op jit(solution)/shard_map/ppermute | solution.py:43
  79.8 1.9 %collective-permute-start.9 = (bf16[64,512]{1,0:T(8,128)(2,1)S(1)}, bf16[64,512]{1,0:T(8,128)(2,1)S(1)}, u32[]{:S(2)}, u32[]{:S(2)}) collective-permute-start(bf16[64,512]{1,0:T(8,128)(2,1)S(1)} %get-tuple-element.39), channel_id=1, source_target_pairs={{0,2},{1,3},{2,0},{3,1},{4,6},{5,7},{6,4},{7,5},{8,10},{9,11},{10,... | collective-permute-start | bytes 196616 | tf_op jit(solution)/shard_map/ppermute | solution.py:43
  81.9 1.4 %collective-permute-start.4 = (bf16[64,512]{1,0:T(8,128)(2,1)S(1)}, bf16[64,512]{1,0:T(8,128)(2,1)S(1)}, u32[]{:S(2)}, u32[]{:S(2)}) collective-permute-start(bf16[64,512]{1,0:T(8,128)(2,1)S(1)} %get-tuple-element.44), channel_id=1, source_target_pairs={{0,4},{1,5},{2,6},{3,7},{4,0},{5,1},{6,2},{7,3},{8,12},{9,13},{10,... | collective-permute-start | bytes 196616 | tf_op jit(solution)/shard_map/ppermute | solution.py:43
  83.3 1.7 %collective-permute-done.10 = bf16[64,512]{1,0:T(8,128)(2,1)S(1)} collective-permute-done((bf16[64,512]{1,0:T(8,128)(2,1)S(1)}, bf16[64,512]{1,0:T(8,128)(2,1)S(1)}, u32[]{:S(2)}, u32[]{:S(2)}) %collective-permute-start.10) | collective-permute-done | bytes 65568 | tf_op jit(solution)/shard_map/ppermute | solution.py:43
  85.0 1.4 %collective-permute-start.5 = (bf16[64,512]{1,0:T(8,128)(2,1)S(1)}, bf16[64,512]{1,0:T(8,128)(2,1)S(1)}, u32[]{:S(2)}, u32[]{:S(2)}) collective-permute-start(bf16[64,512]{1,0:T(8,128)(2,1)S(1)} %get-tuple-element.43), channel_id=1, source_target_pairs={{0,6},{1,7},{2,4},{3,5},{4,2},{5,3},{6,0},{7,1},{8,14},{9,15},{10,... | collective-permute-start | bytes 196616 | tf_op jit(solution)/shard_map/ppermute | solution.py:43
  87.1 4.0 %collective-permute-done.5 = bf16[64,512]{1,0:T(8,128)(2,1)S(1)} collective-permute-done((bf16[64,512]{1,0:T(8,128)(2,1)S(1)}, bf16[64,512]{1,0:T(8,128)(2,1)S(1)}, u32[]{:S(2)}, u32[]{:S(2)}) %collective-permute-start.5) | collective-permute-done | bytes 65568 | tf_op jit(solution)/shard_map/ppermute | solution.py:43
  91.8 5.4 %match.1 = f32[4,136,128]{2,1,0:T(8,128)} custom-call(f32[64,512]{1,0:T(8,128)} %fusion.18.stacked_a, f32[64,512]{1,0:T(8,128)} %fusion.13.stacked_b, f32[512,512]{1,0:T(8,128)} %bitcast.144, bf16[512,512]{1,0:T(8,128)(2,1)} %get-tuple-element.19.row_prof, f32[4,128,512]{2,1,0:T(8,128)} %get-tuple-element.20.col_match, f32[1,1]{1,0:T(1,128)} %bitcast.35.weight), custom_call_target="tpu_custom_call" | custom-call | flops 805306368 | bytes 2097152 | tf_op jit(solution)/shard_map/match/pallas_call | solution.py:236
  98.3 1.6 %collective-permute-start.17 = (f32[136,128]{1,0:T(8,128)S(1)}, f32[136,128]{1,0:T(8,128)S(1)}, u32[]{:S(2)}, u32[]{:S(2)}) collective-permute-start(f32[136,128]{1,0:T(8,128)S(1)} %get-tuple-element.45), channel_id=1, source_target_pairs={{0,16},{1,17},{2,18},{3,19},{4,20},{5,21},{6,22},{7,23},{8,24},{9,... | collective-permute-start | bytes 208904 | tf_op jit(solution)/shard_map/ppermute | solution.py:43
  100.1 1.2 %fusion.29 = f32[128,512]{1,0:T(8,128)S(1)} fusion(f32[512,128]{1,0:T(8,128)S(1)} %bitcast.142, f32[4,136,128]{2,1,0:T(8,128)} %match.1, s32[]{:T(128)S(6)} %select_n.135), kind=kOutput, calls=%fused_computation.53 | convolution fusion | flops 100663296 | bytes 589828 | tf_op jit(solution)/shard_map/dot_general | solution.py:361
  101.4 1.6 %collective-permute-done.17 = f32[136,128]{1,0:T(8,128)S(1)} collective-permute-done((f32[136,128]{1,0:T(8,128)S(1)}, f32[136,128]{1,0:T(8,128)S(1)}, u32[]{:S(2)}, u32[]{:S(2)}) %collective-permute-start.17) | collective-permute-done | bytes 69664 | tf_op jit(solution)/shard_map/ppermute | solution.py:43
  106.5 1.8 %collective-permute-done.23 = f32[8,128]{1,0:T(8,128)S(1)} collective-permute-done((f32[8,128]{1,0:T(8,128)S(1)}, f32[8,128]{1,0:T(8,128)S(1)}, u32[]{:S(2)}, u32[]{:S(2)}) %collective-permute-start.23) | collective-permute-done | bytes 4128 | tf_op jit(solution)/shard_map/ppermute | solution.py:43
  108.4 1.9 %collective-permute-start.25 = (f32[2,8,128]{2,1,0:T(8,128)S(1)}, f32[2,8,128]{2,1,0:T(8,128)S(1)}, u32[]{:S(2)}, u32[]{:S(2)}) collective-permute-start(f32[2,8,128]{2,1,0:T(8,128)S(1)} %pad_maximum_fusion.3.refs_0_), channel_id=1, source_target_pairs={{0,4},{1,5},{2,6},{3,7},{4,0},{5,1},{6,2},{7,3},{8,12},{9,13},{10,... | collective-permute-start | bytes 24584 | tf_op jit(solution)/shard_map/ppermute | solution.py:43
  110.3 2.4 %collective-permute-start.26 = (f32[2,8,128]{2,1,0:T(8,128)S(1)}, f32[2,8,128]{2,1,0:T(8,128)S(1)}, u32[]{:S(2)}, u32[]{:S(2)}) collective-permute-start(f32[2,8,128]{2,1,0:T(8,128)S(1)} %pad_maximum_fusion.3.refs_0_), channel_id=1, source_target_pairs={{0,6},{1,7},{2,4},{3,5},{4,2},{5,3},{6,0},{7,1},{8,14},{9,15},{10,... | collective-permute-start | bytes 24584 | tf_op jit(solution)/shard_map/ppermute | solution.py:43
  112.7 1.7 %fusion.2 = f32[1,128,512]{2,1,0:T(8,128)} fusion(f32[128,512]{1,0:T(8,128)S(1)} %fusion.25, f32[128,512]{1,0:T(8,128)S(1)} %convolution_add_fusion.1, f32[512,128]{1,0:T(8,128)S(1)} %bitcast.145, f32[]{:T(128)} %bitcast.45, f32[136,128]{1,0:T(8,128)S(1)} %collective-permute-done.17), kind=kOutput, calls=%fused_computation.3 | convolution fusion | flops 100859904 | bytes 1114116 | tf_op jit(solution)/shard_map/dot_general | solution.py:361
  114.5 1.3 %collective-permute-done.26.refs_3_ = f32[2,8,128]{2,1,0:T(8,128)S(1)} collective-permute-done((f32[2,8,128]{2,1,0:T(8,128)S(1)}, f32[2,8,128]{2,1,0:T(8,128)S(1)}, u32[]{:S(2)}, u32[]{:S(2)}) %collective-permute-start.26) | collective-permute-done | bytes 8224 | tf_op jit(solution)/shard_map/ppermute | solution.py:43
  116.4 1.8 %finish.1 = (f32[4,128]{1,0:T(4,128)}, f32[8,512]{1,0:T(8,128)}) custom-call(s32[8]{0:T(128)} %patch_ref.7, f32[32,1]{1,0:T(8,128)} %copy.14.counts, f32[8,1,512]{2,1,0:T(1,128)} %get-tuple-element.23.flux, f32[32,512]{1,0:T(8,128)} %add_add_fusion.sums, f32[2,8,128]{2,1,0:T(8,128)} %copy-done.2, f32[2,8,128]{2,1,0:T(8,128)} %copy-done.4, ...), custom_call_target="tpu_custom_call" | custom-call | tf_op jit(solution)/shard_map/finish/pallas_call | solution.py:273
  118.1 1.3 %slice_reduce_fusion.1 = f32[4]{0:T(128)} fusion(f32[4,128]{1,0:T(4,128)} %get-tuple-element.25), kind=kLoop, calls=%fused_computation.76 | loop fusion | bytes 32 | tf_op jit(solution)/shard_map/slice | solution.py:373
  (89 shorter events, 21.8 us)
Async XLA Ops:
  12.9 11.8 %copy-start.3 = (s32[8]{0:T(128)S(1)}, s32[8]{0:T(128)}, u32[]{:S(2)}) copy-start(s32[8]{0:T(128)} %patch_ref.7) | copy-start | bytes 100
  12.9 11.8 %copy-start.9 = (f32[8]{0:T(128)S(1)}, f32[8]{0:T(128)}, u32[]{:S(2)}) copy-start(f32[8]{0:T(128)} %convert_element_type.177.weight_ref) | copy-start | bytes 100
  12.9 12.1 %copy-start.10 = (s32[1,512]{1,0:T(1,128)S(1)}, s32[1,512]{1,0:T(1,128)}, u32[]{:S(2)}) copy-start(s32[1,512]{1,0:T(1,128)} %param.16) | copy-start | bytes 6148
  12.9 12.1 %copy-start.11 = (s32[1,512]{1,0:T(1,128)S(1)}, s32[1,512]{1,0:T(1,128)}, u32[]{:S(2)}) copy-start(s32[1,512]{1,0:T(1,128)} %param.17) | copy-start | bytes 6148
  13.0 30.9 %collective-permute-start.6 = (bf16[2,2,4,64,512]{4,3,2,1,0:T(8,128)(2,1)}, bf16[2,2,4,64,512]{4,3,2,1,0:T(8,128)(2,1)S(1)}, u32[]{:S(2)}, u32[]{:S(2)}) collective-permute-start(bf16[2,2,4,64,512]{4,3,2,1,0:T(8,128)(2,1)} %get-tuple-element.18), channel_id=1, source_target_pairs={{0,8},{1,9},{2,10},{3,11},{4,12},{5,13},{6,14},{7,15},{8,0},{9,1},... | collective-permute-start | bytes 3145736 | tf_op jit(solution)/shard_map/ppermute | solution.py:43
  24.6 8.4 %copy-start = (f32[1,512,512]{2,1,0:T(8,128)S(1)}, f32[1,512,512]{2,1,0:T(8,128)}, u32[]{:S(2)}) copy-start(f32[1,512,512]{2,1,0:T(8,128)} %param.15) | copy-start | bytes 3145732
  24.6 24.3 %collective-permute-start = (bf16[2,2,4,64,512]{4,3,2,1,0:T(8,128)(2,1)}, bf16[2,2,4,64,512]{4,3,2,1,0:T(8,128)(2,1)}, u32[]{:S(2)}, u32[]{:S(2)}) collective-permute-start(bf16[2,2,4,64,512]{4,3,2,1,0:T(8,128)(2,1)} %get-tuple-element.16), channel_id=1, source_target_pairs={{0,8},{1,9},{2,10},{3,11},{4,12},{5,13},{6,14},{7,15},{8,0},{9,1},... | collective-permute-start | bytes 3145736 | tf_op jit(solution)/shard_map/ppermute | solution.py:43
  25.2 8.2 %collective-permute-start.12 = (f32[3,512]{1,0:T(4,128)S(1)}, f32[3,512]{1,0:T(4,128)S(1)}, u32[]{:S(2)}, u32[]{:S(2)}) collective-permute-start(f32[3,512]{1,0:T(4,128)S(1)} %get-tuple-element.54), channel_id=1, source_target_pairs={{0,1},{1,0},{2,3},{3,2},{4,5},{5,4},{6,7},{7,6},{8,9},{9,8},{10,11... | collective-permute-start | bytes 18440 | tf_op jit(solution)/shard_map/ppermute | solution.py:43
  33.4 5.4 %collective-permute-start.13 = (f32[2,3,512]{2,1,0:T(4,128)S(1)}, f32[2,3,512]{2,1,0:T(4,128)S(1)}, u32[]{:S(2)}, u32[]{:S(2)}) collective-permute-start(f32[2,3,512]{2,1,0:T(4,128)S(1)} %get-tuple-element.52), channel_id=1, source_target_pairs={{0,2},{1,3},{2,0},{3,1},{4,6},{5,7},{6,4},{7,5},{8,10},{9,11},{10,... | collective-permute-start | bytes 36872 | tf_op jit(solution)/shard_map/ppermute | solution.py:43
  35.0 4.8 %collective-permute-start.14 = (f32[2,3,512]{2,1,0:T(4,128)S(1)}, f32[2,3,512]{2,1,0:T(4,128)S(1)}, u32[]{:S(2)}, u32[]{:S(2)}) collective-permute-start(f32[2,3,512]{2,1,0:T(4,128)S(1)} %get-tuple-element.52), channel_id=1, source_target_pairs={{0,4},{1,5},{2,6},{3,7},{4,0},{5,1},{6,2},{7,3},{8,12},{9,13},{10,... | collective-permute-start | bytes 36872 | tf_op jit(solution)/shard_map/ppermute | solution.py:43
  37.6 5.5 %collective-permute-start.15 = (f32[2,3,512]{2,1,0:T(4,128)S(1)}, f32[2,3,512]{2,1,0:T(4,128)S(1)}, u32[]{:S(2)}, u32[]{:S(2)}) collective-permute-start(f32[2,3,512]{2,1,0:T(4,128)S(1)} %get-tuple-element.52), channel_id=1, source_target_pairs={{0,6},{1,7},{2,4},{3,5},{4,2},{5,3},{6,0},{7,1},{8,14},{9,15},{10,... | collective-permute-start | bytes 36872 | tf_op jit(solution)/shard_map/ppermute | solution.py:43
  47.4 23.1 %collective-permute-start.7 = (bf16[2,4,64,512]{3,2,1,0:T(8,128)(2,1)}, bf16[2,4,64,512]{3,2,1,0:T(8,128)(2,1)}, u32[]{:S(2)}, u32[]{:S(2)}) collective-permute-start(bf16[2,4,64,512]{3,2,1,0:T(8,128)(2,1)} %get-tuple-element.27), channel_id=1, source_target_pairs={{0,16},{1,17},{2,18},{3,19},{4,20},{5,21},{6,22},{7,23},{8,9},{9,8... | collective-permute-start | bytes 1572872 | tf_op jit(solution)/shard_map/ppermute | solution.py:43
  51.5 20.7 %collective-permute-start.1 = (bf16[2,4,64,512]{3,2,1,0:T(8,128)(2,1)}, bf16[2,4,64,512]{3,2,1,0:T(8,128)(2,1)}, u32[]{:S(2)}, u32[]{:S(2)}) collective-permute-start(bf16[2,4,64,512]{3,2,1,0:T(8,128)(2,1)} %get-tuple-element.29), channel_id=1, source_target_pairs={{0,16},{1,17},{2,18},{3,19},{4,20},{5,21},{6,22},{7,23},{8,9},{9,8... | collective-permute-start | bytes 1572872 | tf_op jit(solution)/shard_map/ppermute | solution.py:43
  60.7 4.5 %collective-permute-start.19 = (f32[32,512]{1,0:T(8,128)}, f32[32,512]{1,0:T(8,128)S(1)}, u32[]{:S(2)}, u32[]{:S(2)}) collective-permute-start(f32[32,512]{1,0:T(8,128)} %get-tuple-element.24), channel_id=1, source_target_pairs={{0,1},{1,0},{2,3},{3,2},{4,5},{5,4},{6,7},{7,6},{8,9},{9,8},{10,11... | collective-permute-start | bytes 196616 | tf_op jit(solution)/shard_map/ppermute | solution.py:43
  66.0 9.0 %collective-permute-start.20 = (f32[32,512]{1,0:T(8,128)S(1)}, f32[32,512]{1,0:T(8,128)S(1)}, u32[]{:S(2)}, u32[]{:S(2)}) collective-permute-start(f32[32,512]{1,0:T(8,128)S(1)} %add.263), channel_id=1, source_target_pairs={{0,2},{1,3},{2,0},{3,1},{4,6},{5,7},{6,4},{7,5},{8,10},{9,11},{10,... | collective-permute-start | bytes 196616 | tf_op jit(solution)/shard_map/ppermute | solution.py:43
  66.1 8.9 %collective-permute-start.21 = (f32[32,512]{1,0:T(8,128)S(1)}, f32[32,512]{1,0:T(8,128)S(1)}, u32[]{:S(2)}, u32[]{:S(2)}) collective-permute-start(f32[32,512]{1,0:T(8,128)S(1)} %add.263), channel_id=1, source_target_pairs={{0,4},{1,5},{2,6},{3,7},{4,0},{5,1},{6,2},{7,3},{8,12},{9,13},{10,... | collective-permute-start | bytes 196616 | tf_op jit(solution)/shard_map/ppermute | solution.py:43
  66.9 8.2 %collective-permute-start.22 = (f32[32,512]{1,0:T(8,128)S(1)}, f32[32,512]{1,0:T(8,128)S(1)}, u32[]{:S(2)}, u32[]{:S(2)}) collective-permute-start(f32[32,512]{1,0:T(8,128)S(1)} %add.263), channel_id=1, source_target_pairs={{0,6},{1,7},{2,4},{3,5},{4,2},{5,3},{6,0},{7,1},{8,14},{9,15},{10,... | collective-permute-start | bytes 196616 | tf_op jit(solution)/shard_map/ppermute | solution.py:43
  71.7 6.4 %collective-permute-start.8 = (bf16[4,64,512]{2,1,0:T(8,128)(2,1)S(1)}, bf16[4,64,512]{2,1,0:T(8,128)(2,1)S(1)}, u32[]{:S(2)}, u32[]{:S(2)}) collective-permute-start(bf16[4,64,512]{2,1,0:T(8,128)(2,1)S(1)} %get-tuple-element.31), channel_id=1, source_target_pairs={{0,1},{1,0},{2,3},{3,2},{4,5},{5,4},{6,7},{7,6},{8,24},{9,25},{10,... | collective-permute-start | bytes 786440 | tf_op jit(solution)/shard_map/ppermute | solution.py:43
  73.4 8.3 %collective-permute-start.2 = (bf16[4,64,512]{2,1,0:T(8,128)(2,1)S(1)}, bf16[4,64,512]{2,1,0:T(8,128)(2,1)S(1)}, u32[]{:S(2)}, u32[]{:S(2)}) collective-permute-start(bf16[4,64,512]{2,1,0:T(8,128)(2,1)S(1)} %get-tuple-element.33), channel_id=1, source_target_pairs={{0,1},{1,0},{2,3},{3,2},{4,5},{5,4},{6,7},{7,6},{8,24},{9,25},{10,... | collective-permute-start | bytes 786440 | tf_op jit(solution)/shard_map/ppermute | solution.py:43
  78.2 6.9 %collective-permute-start.10 = (bf16[64,512]{1,0:T(8,128)(2,1)S(1)}, bf16[64,512]{1,0:T(8,128)(2,1)S(1)}, u32[]{:S(2)}, u32[]{:S(2)}) collective-permute-start(bf16[64,512]{1,0:T(8,128)(2,1)S(1)} %get-tuple-element.41), channel_id=1, source_target_pairs={{0,4},{1,5},{2,6},{3,7},{4,0},{5,1},{6,2},{7,3},{8,12},{9,13},{10,... | collective-permute-start | bytes 196616 | tf_op jit(solution)/shard_map/ppermute | solution.py:43
  78.2 8.2 %collective-permute-start.11 = (bf16[64,512]{1,0:T(8,128)(2,1)S(1)}, bf16[64,512]{1,0:T(8,128)(2,1)S(1)}, u32[]{:S(2)}, u32[]{:S(2)}) collective-permute-start(bf16[64,512]{1,0:T(8,128)(2,1)S(1)} %get-tuple-element.40), channel_id=1, source_target_pairs={{0,6},{1,7},{2,4},{3,5},{4,2},{5,3},{6,0},{7,1},{8,14},{9,15},{10,... | collective-permute-start | bytes 196616 | tf_op jit(solution)/shard_map/ppermute | solution.py:43
  79.8 6.6 %collective-permute-start.9 = (bf16[64,512]{1,0:T(8,128)(2,1)S(1)}, bf16[64,512]{1,0:T(8,128)(2,1)S(1)}, u32[]{:S(2)}, u32[]{:S(2)}) collective-permute-start(bf16[64,512]{1,0:T(8,128)(2,1)S(1)} %get-tuple-element.39), channel_id=1, source_target_pairs={{0,2},{1,3},{2,0},{3,1},{4,6},{5,7},{6,4},{7,5},{8,10},{9,11},{10,... | collective-permute-start | bytes 196616 | tf_op jit(solution)/shard_map/ppermute | solution.py:43
  81.8 5.3 %collective-permute-start.3 = (bf16[64,512]{1,0:T(8,128)(2,1)S(1)}, bf16[64,512]{1,0:T(8,128)(2,1)S(1)}, u32[]{:S(2)}, u32[]{:S(2)}) collective-permute-start(bf16[64,512]{1,0:T(8,128)(2,1)S(1)} %get-tuple-element.42), channel_id=1, source_target_pairs={{0,2},{1,3},{2,0},{3,1},{4,6},{5,7},{6,4},{7,5},{8,10},{9,11},{10,... | collective-permute-start | bytes 196616 | tf_op jit(solution)/shard_map/ppermute | solution.py:43
  81.9 5.2 %collective-permute-start.4 = (bf16[64,512]{1,0:T(8,128)(2,1)S(1)}, bf16[64,512]{1,0:T(8,128)(2,1)S(1)}, u32[]{:S(2)}, u32[]{:S(2)}) collective-permute-start(bf16[64,512]{1,0:T(8,128)(2,1)S(1)} %get-tuple-element.44), channel_id=1, source_target_pairs={{0,4},{1,5},{2,6},{3,7},{4,0},{5,1},{6,2},{7,3},{8,12},{9,13},{10,... | collective-permute-start | bytes 196616 | tf_op jit(solution)/shard_map/ppermute | solution.py:43
  85.0 6.1 %collective-permute-start.5 = (bf16[64,512]{1,0:T(8,128)(2,1)S(1)}, bf16[64,512]{1,0:T(8,128)(2,1)S(1)}, u32[]{:S(2)}, u32[]{:S(2)}) collective-permute-start(bf16[64,512]{1,0:T(8,128)(2,1)S(1)} %get-tuple-element.43), channel_id=1, source_target_pairs={{0,6},{1,7},{2,4},{3,5},{4,2},{5,3},{6,0},{7,1},{8,14},{9,15},{10,... | collective-permute-start | bytes 196616 | tf_op jit(solution)/shard_map/ppermute | solution.py:43
  98.2 3.2 %collective-permute-start.16 = (f32[136,128]{1,0:T(8,128)S(1)}, f32[136,128]{1,0:T(8,128)S(1)}, u32[]{:S(2)}, u32[]{:S(2)}) collective-permute-start(f32[136,128]{1,0:T(8,128)S(1)} %get-tuple-element.47), channel_id=1, source_target_pairs={{0,8},{1,9},{2,10},{3,11},{4,12},{5,13},{6,14},{7,15},{8,0},{9,1},... | collective-permute-start | bytes 208904 | tf_op jit(solution)/shard_map/ppermute | solution.py:43
  98.3 4.7 %collective-permute-start.17 = (f32[136,128]{1,0:T(8,128)S(1)}, f32[136,128]{1,0:T(8,128)S(1)}, u32[]{:S(2)}, u32[]{:S(2)}) collective-permute-start(f32[136,128]{1,0:T(8,128)S(1)} %get-tuple-element.45), channel_id=1, source_target_pairs={{0,16},{1,17},{2,18},{3,19},{4,20},{5,21},{6,22},{7,23},{8,24},{9,... | collective-permute-start | bytes 208904 | tf_op jit(solution)/shard_map/ppermute | solution.py:43
  99.8 4.2 %collective-permute-start.18 = (f32[136,128]{1,0:T(8,128)S(1)}, f32[136,128]{1,0:T(8,128)S(1)}, u32[]{:S(2)}, u32[]{:S(2)}) collective-permute-start(f32[136,128]{1,0:T(8,128)S(1)} %get-tuple-element.46), channel_id=1, source_target_pairs={{0,24},{1,25},{2,26},{3,27},{4,28},{5,29},{6,30},{7,31},{8,16},{9,... | collective-permute-start | bytes 208904 | tf_op jit(solution)/shard_map/ppermute | solution.py:43
  104.7 3.6 %collective-permute-start.23 = (f32[8,128]{1,0:T(8,128)S(1)}, f32[8,128]{1,0:T(8,128)S(1)}, u32[]{:S(2)}, u32[]{:S(2)}) collective-permute-start(f32[8,128]{1,0:T(8,128)S(1)} %fusion.34), channel_id=1, source_target_pairs={{0,1},{1,0},{2,3},{3,2},{4,5},{5,4},{6,7},{7,6},{8,9},{9,8},{10,11... | collective-permute-start | bytes 12296 | tf_op jit(solution)/shard_map/ppermute | solution.py:43
  108.4 6.1 %collective-permute-start.24 = (f32[2,8,128]{2,1,0:T(8,128)S(1)}, f32[2,8,128]{2,1,0:T(8,128)S(1)}, u32[]{:S(2)}, u32[]{:S(2)}) collective-permute-start(f32[2,8,128]{2,1,0:T(8,128)S(1)} %pad_maximum_fusion.3.refs_0_), channel_id=1, source_target_pairs={{0,2},{1,3},{2,0},{3,1},{4,6},{5,7},{6,4},{7,5},{8,10},{9,11},{10,... | collective-permute-start | bytes 24584 | tf_op jit(solution)/shard_map/ppermute | solution.py:43
  108.4 6.1 %collective-permute-start.25 = (f32[2,8,128]{2,1,0:T(8,128)S(1)}, f32[2,8,128]{2,1,0:T(8,128)S(1)}, u32[]{:S(2)}, u32[]{:S(2)}) collective-permute-start(f32[2,8,128]{2,1,0:T(8,128)S(1)} %pad_maximum_fusion.3.refs_0_), channel_id=1, source_target_pairs={{0,4},{1,5},{2,6},{3,7},{4,0},{5,1},{6,2},{7,3},{8,12},{9,13},{10,... | collective-permute-start | bytes 24584 | tf_op jit(solution)/shard_map/ppermute | solution.py:43
  110.3 5.4 %collective-permute-start.26 = (f32[2,8,128]{2,1,0:T(8,128)S(1)}, f32[2,8,128]{2,1,0:T(8,128)S(1)}, u32[]{:S(2)}, u32[]{:S(2)}) collective-permute-start(f32[2,8,128]{2,1,0:T(8,128)S(1)} %pad_maximum_fusion.3.refs_0_), channel_id=1, source_target_pairs={{0,6},{1,7},{2,4},{3,5},{4,2},{5,3},{6,0},{7,1},{8,14},{9,15},{10,... | collective-permute-start | bytes 24584 | tf_op jit(solution)/shard_map/ppermute | solution.py:43
  (7 other events, 18.9 us)

commit v2 on v1

v2 whole, which is shorter than its diff:
```python
import functools

import jax
import jax.numpy as jnp
from jax import lax
from jax.experimental import pallas as pl
from jax.experimental.pallas import tpu as pltpu
from jax.sharding import PartitionSpec as P

VIS_ROW = 4
APERTURE = 2.5
HIGHEST = lax.Precision.HIGHEST
F32 = jnp.float32
BF16 = jnp.bfloat16
AXES = ("visit", "patch")
EXPONENT = -1.4426950408889634 / (2.0 * APERTURE * APERTURE)
VMEM_LIMIT = 20 * 1024 * 1024
WARP_LIMIT = 38 * 1024 * 1024
PARTS = 1
PAIR = 2
IN_VMEM = pl.BlockSpec(memory_space=pltpu.VMEM)
NT = (((1,), (1,)), ((), ()))
TN = (((0,), (0,)), ((), ()))


class Layout:
    def __init__(self, tiles, side):
        self.tiles, self.side = tiles, side
        self.visits, self.patches = lax.axis_size("visit"), lax.axis_size("patch")
        self.group = self.visits // 2
        self.highs = self.patches // self.group
        self.width = side // self.visits
        self.part = side // PARTS

    def place(self):
        visit, patch = lax.axis_index("visit"), lax.axis_index("patch")
        return visit % 2, visit // 2, patch // self.group, patch % self.group

    def permute(self, array, partner):
        pairs = []
        for visit in range(self.visits):
            for patch in range(self.patches):
                x, core, high, low = partner(visit // 2, visit % 2, patch // self.group, patch % self.group)
                target = (2 * x + core) * self.patches + self.group * high + low
                pairs.append((visit * self.patches + patch, target))
        return lax.ppermute(array, AXES, pairs)

    def swap_core(self, array):
        return self.permute(array, lambda x, core, high, low: (x, 1 - core, high, low))

    def swap_first(self, array, step):
        def partner(x, core, high, low):
            return (x ^ step, core, high, low) if core == 0 else (x, core, high, low ^ step)

        return self.permute(array, partner)

    def swap_second(self, array, step):
        def partner(x, core, high, low):
            return (x, core, high, low ^ step) if core == 0 else (x ^ step, core, high, low)

        return self.permute(array, partner)

    def swap_low(self, array, step):
        return self.permute(array, lambda x, core, high, low: (x, core, high, low ^ step))

    def swap_high(self, array, step):
        return self.permute(array, lambda x, core, high, low: (x, core, high ^ step, low))

    def swap_visit(self, array, step):
        def partner(x, core, high, low):
            visit = (2 * x + core) ^ step
            return visit // 2, visit % 2, high, low

        return self.permute(array, partner)


def warp_kernel(lay, patch_ref, weight_ref, images, rows, cols, warped, *refs):
    outs, (image, row, col, half, result, weights, total, arrive, leave, small) = refs[: 2 * PARTS], refs[2 * PARTS :]
    sends, keeps = outs[:PARTS], outs[PARTS:]
    fetch = pltpu.make_async_copy(weight_ref, weights, small)
    fetch.start()
    loads = []
    for tile in range(lay.tiles):
        loads.append(
            [
                pltpu.make_async_copy(source.at[tile], target.at[tile], arrive.at[kind, tile])
                for kind, (source, target) in enumerate(((images, image), (cols, col), (rows, row)))
            ]
        )
        for load in loads[-1]:
            load.start()
    total[...] = jnp.zeros_like(total)
    fetch.wait()
    lane = lax.broadcasted_iota(jnp.int32, (1, lay.tiles), 1)
    stores = []
    for tile in range(lay.tiles + 1):
        if tile < lay.tiles:
            loads[tile][0].wait()
            loads[tile][1].wait()
            half[tile % 2] = lax.dot_general(image[tile], col[tile], NT, preferred_element_type=F32).astype(BF16)
        if tile:
            last = tile - 1
            loads[last][2].wait()
            value = jnp.dot(row[last], half[last % 2], preferred_element_type=F32).astype(BF16)
            result[last] = value
            stores.append(pltpu.make_async_copy(result.at[last], warped.at[last], leave.at[last]))
            stores[-1].start()
            spread = weights[...].astype(F32).reshape(1, lay.tiles)
            weight = jnp.sum(jnp.where(lane == last, spread, 0.0), keepdims=True)
            total[patch_ref[last]] += weight * value.astype(F32)

    def write(outs, core):
        for first in range(lay.group):
            for second in range(lay.group):
                x, low = (first, second) if core == 0 else (second, first)
                start = (2 * x + core) * lay.width
                for high in range(lay.highs):
                    for part, out in enumerate(outs):
                        block = total[
                            high * lay.group + low,
                            part * lay.part : (part + 1) * lay.part,
                            start : start + lay.width,
                        ]
                        out[first, second, high] = block.astype(BF16)

    core = lax.axis_index("visit") % 2
    for own in range(2):

        @pl.when(core == own)
        def _():
            write(sends, 1 - own)
            write(keeps, own)

    for store in stores:
        store.wait()


def in_hbm(array):
    return pltpu.with_memory_space_constraint(array, pltpu.HBM)


def warp(lay, tile_patch, weight, images, warp_rows, warp_cols):
    tiles, side = lay.tiles, lay.side
    pieces = (lay.group, lay.group, lay.highs, lay.part, lay.width)
    in_any = pl.BlockSpec(memory_space=pltpu.HBM)
    stack = pltpu.VMEM((tiles, side, side), BF16)
    out = pl.pallas_call(
        functools.partial(warp_kernel, lay),
        in_specs=[pl.BlockSpec(memory_space=pltpu.SMEM)] + [in_any] * 4,
        out_specs=[in_any] + [IN_VMEM] * (2 * PARTS),
        out_shape=[pltpu.HBM((tiles, side, side), BF16)] + [pltpu.VMEM(pieces, BF16)] * (2 * PARTS),
        scratch_shapes=[
            stack,
            stack,
            stack,
            pltpu.VMEM((2, side, side), BF16),
            stack,
            pltpu.VMEM((tiles,), BF16),
            pltpu.VMEM((lay.patches, side, side), F32),
            pltpu.SemaphoreType.DMA((3, tiles)),
            pltpu.SemaphoreType.DMA((tiles,)),
            pltpu.SemaphoreType.DMA,
        ],
        compiler_params=pltpu.CompilerParams(vmem_limit_bytes=WARP_LIMIT),
        cost_estimate=pl.CostEstimate(
            flops=4 * tiles * side**3, bytes_accessed=8 * tiles * side * side, transcendentals=0
        ),
        name="warp",
    )(tile_patch, weight, images, warp_rows, warp_cols)
    return out[0], out[1 : 1 + PARTS], out[1 + PARTS :]


def profile(position, centers):
    distance = position - centers
    return jnp.exp2(distance * distance * EXPONENT).astype(BF16)


def flux_kernel(lay, patch_ref, place_ref, warped, *refs):
    step = pl.program_id(0)
    sources, (flux, sums) = refs[: 2 * PAIR], refs[2 * PAIR :]

    @pl.when(step == 0)
    def _():
        sums[...] = jnp.zeros_like(sums)

    position = lax.broadcasted_iota(jnp.int32, (lay.side, lay.side), 0).astype(F32)
    for local in range(PAIR):
        tile = step * PAIR + local
        row_prof = profile(position, sources[local][0])
        col_prof = profile(position, sources[PAIR + local][0])
        by_column = jnp.dot(warped[local], col_prof, preferred_element_type=F32)
        value = jnp.sum(by_column * row_prof.astype(F32), axis=0, keepdims=True)
        flux[tile] = value
        spot = patch_ref[tile] * VIS_ROW + tile % VIS_ROW
        sums[pl.ds(spot, 1), :] += value


def forced_flux(lay, tile_patch, tile_place, warped, src_row, src_col):
    tiles, side = lay.tiles, lay.side
    sources = [
        pl.BlockSpec((1, 1, side), lambda step, patch, place, local=local: (place[step * PAIR + local], 0, 0))
        for local in range(PAIR)
    ]
    return pl.pallas_call(
        functools.partial(flux_kernel, lay),
        grid_spec=pltpu.PrefetchScalarGridSpec(
            num_scalar_prefetch=2,
            grid=(tiles // PAIR,),
            in_specs=[pl.BlockSpec((PAIR, side, side), lambda step, *_: (step, 0, 0))] + sources * 2,
            out_specs=[IN_VMEM, IN_VMEM],
        ),
        out_shape=[
            jax.ShapeDtypeStruct((tiles, 1, side), F32),
            jax.ShapeDtypeStruct((VIS_ROW * lay.patches, side), F32),
        ],
        compiler_params=pltpu.CompilerParams(vmem_limit_bytes=VMEM_LIMIT),
        cost_estimate=pl.CostEstimate(
            flops=2 * tiles * side**3, bytes_accessed=2 * tiles * side * side, transcendentals=2 * tiles * side * side
        ),
        name="forced_flux",
    )(tile_patch, tile_place, in_hbm(warped), *([src_row] * PAIR + [src_col] * PAIR))


def split(array):
    upper = array.astype(BF16)
    return upper, (array - upper.astype(F32)).astype(BF16)


def dot3(left, right, dims):
    product = functools.partial(lax.dot_general, dimension_numbers=dims, preferred_element_type=F32)
    return product(left[0], right[0]) + (product(left[0], right[1]) + product(left[1], right[0]))


def prepare_kernel(lay, src_row, src_col, match_rows, match_cols, rows_up, rows_low, row_flux, col_up, col_low, product_ref):
    side = lay.side
    product = functools.partial(lax.dot_general, dimension_numbers=TN, preferred_element_type=F32)
    position = lax.broadcasted_iota(jnp.int32, (side, side), 0).astype(F32)
    row_prof = profile(position, src_row[...].astype(F32))
    col_prof = profile(position, src_col[...].astype(F32))
    upper, lower = split(match_rows[...])
    rows_up[...], rows_low[...] = upper, lower
    row_flux[...] = product(upper, row_prof) + product(lower, row_prof)
    upper, lower = split(match_cols[...])
    product_ref[...] = (product(upper, col_prof) + product(lower, col_prof)).reshape(lay.visits, lay.width, side)
    col_up[...], col_low[...] = split(product_ref[lax.axis_index("visit")])


def prepare(lay, src_row, src_col, match_rows, match_cols):
    side = lay.side
    block = pltpu.HBM((lay.width, side), BF16)
    square = pltpu.HBM((side, side), BF16)
    return pl.pallas_call(
        functools.partial(prepare_kernel, lay),
        in_specs=[IN_VMEM] * 4,
        out_shape=[square, square, pltpu.HBM((side, side), F32), block, block],
        scratch_shapes=[pltpu.VMEM((lay.visits, lay.width, side), F32)],
        compiler_params=pltpu.CompilerParams(vmem_limit_bytes=VMEM_LIMIT),
        cost_estimate=pl.CostEstimate(
            flops=8 * side**3, bytes_accessed=20 * side * side, transcendentals=2 * side * side
        ),
        name="prepare",
    )(src_row, src_col, match_rows, match_cols)


def match_kernel(lay, extra, *refs):
    width, visits = lay.width, lay.visits
    pieces, refs = refs[: PARTS * lay.highs], refs[PARTS * lay.highs :]
    (rows_up, rows_low, row_flux, col_up, col_low, table), refs = refs[:6], refs[6:]
    messages, (spread, matched) = refs[:visits], refs[visits:]
    visit, patch = lax.axis_index("visit"), lax.axis_index("patch")
    stacked = jnp.concatenate(
        [
            sum(piece[...].astype(F32) for piece in pieces[part * lay.highs : (part + 1) * lay.highs])
            for part in range(PARTS)
        ],
        axis=0,
    )
    stacked = split(stacked)
    nn = (((1,), (0,)), ((), ()))
    result = dot3((rows_up[...], rows_low[...]), stacked, nn)
    matched[...] = result.reshape(visits, width, width)
    by_source = dot3(stacked, (col_up[...], col_low[...]), nn)
    flux = jnp.sum(by_source * row_flux[...], axis=0, keepdims=True)
    lane = lax.broadcasted_iota(jnp.int32, table.shape, 1)
    weight = jnp.sum(jnp.where(lane == patch * 8 + VIS_ROW, table[...], 0.0), keepdims=True)
    tail = jnp.concatenate(
        [flux[:, block * width : (block + 1) * width] for block in range(visits)]
        + [jnp.broadcast_to(weight, (extra - visits, width))],
        axis=0,
    )
    spread[...] = jnp.broadcast_to(tail[None], spread.shape)
    upper, lower = split(jnp.broadcast_to(weight, (8, width)))
    weight = jnp.concatenate([upper, lower], axis=0)
    for step, message in enumerate(messages):
        message[:width] = matched[visit ^ step].astype(BF16)
        message[width:] = weight


def match(lay, extra, pieces, prepared, table):
    side, width = lay.side, lay.width
    out = pl.pallas_call(
        functools.partial(match_kernel, lay, extra),
        in_specs=[IN_VMEM] * (len(pieces) + len(prepared) + 1),
        out_specs=[IN_VMEM] * (lay.visits + 1),
        out_shape=[pltpu.VMEM((width + 16, width), BF16)] * lay.visits
        + [jax.ShapeDtypeStruct((lay.visits * lay.patches, extra, width), F32)],
        scratch_shapes=[pltpu.VMEM((lay.visits, width, width), F32)],
        compiler_params=pltpu.CompilerParams(vmem_limit_bytes=VMEM_LIMIT),
        cost_estimate=pl.CostEstimate(
            flops=12 * width * side * side, bytes_accessed=10 * side * side, transcendentals=0
        ),
        name="match",
    )(*pieces, *prepared, table)
    return out[: lay.visits], out[lay.visits]


def coadd_kernel(lay, match_cols, *refs):
    parts, coadd = refs[:-1], refs[-1]
    width = lay.width
    visit = lax.axis_index("visit")
    blocks = []
    for block in range(lay.visits):
        value = parts[0][:width]
        for step in range(1, lay.visits):
            value = jnp.where((visit ^ step) == block, parts[step][:width], value)
        blocks.append(value)
    weight = 0.0
    for part in parts:
        halves = part[width:].astype(F32)
        weight = weight + (halves[0:1, 0:1] + halves[8:9, 0:1])
    blocks = jnp.concatenate(blocks, axis=1)
    product = functools.partial(lax.dot_general, dimension_numbers=NT, preferred_element_type=F32)
    upper, lower = split(match_cols[...])
    product = product(blocks, upper) + product(blocks, lower)
    coadd[...] = product / weight


def coadd_rows(lay, match_cols, parts):
    side, width = lay.side, lay.width
    return pl.pallas_call(
        functools.partial(coadd_kernel, lay),
        out_shape=jax.ShapeDtypeStruct((width, side), F32),
        compiler_params=pltpu.CompilerParams(vmem_limit_bytes=VMEM_LIMIT),
        cost_estimate=pl.CostEstimate(
            flops=12 * width * side * side, bytes_accessed=6 * side * side, transcendentals=0
        ),
        name="coadd_rows",
    )(match_cols, *parts)


def finish_kernel(lay, patch_ref, table, flux, sums, messages, zero, resid, lines):
    visits, patches = lay.visits, lay.patches
    for patch in range(patches):
        data = sum(messages[visit * patches + patch] for visit in range(visits))
        data = data / data[visits : visits + 1]
        lines[patch : patch + 1, :] = jnp.concatenate([data[block : block + 1] for block in range(visits)], axis=1)
    reference = lines[...]
    lane = lax.broadcasted_iota(jnp.int32, (patches, lay.side), 1) // 8
    row = lax.broadcasted_iota(jnp.int32, (patches, lay.side), 0)
    squares = jnp.sum(reference * reference, axis=1, keepdims=True)
    chosen = jnp.sum(jnp.where(lane == row, squares, 0.0), axis=0, keepdims=True) * table[...]
    products = 0.0
    denominators = 0.0
    for patch in range(patches):
        products = products + sums[patch] * reference[patch : patch + 1]
        denominators = denominators + chosen[:, patch * 8 : (patch + 1) * 8]
    columns = jnp.sum(products, axis=1, keepdims=True)
    place = lax.broadcasted_iota(jnp.int32, (1, VIS_ROW), 1)
    numerators = sum(jnp.where(place == visit, columns[visit : visit + 1], 0.0) for visit in range(VIS_ROW))
    scales = numerators / denominators[:, :VIS_ROW]
    zero[...] = scales
    for tile in range(lay.tiles):
        own = lines[pl.ds(patch_ref[tile], 1), :]
        visit = tile % VIS_ROW
        resid[tile : tile + 1, :] = flux[tile] - scales[:, visit : visit + 1] * own


def finish(lay, tile_patch, table, flux, sums, messages):
    return pl.pallas_call(
        functools.partial(finish_kernel, lay),
        in_specs=[pl.BlockSpec(memory_space=pltpu.SMEM)] + [IN_VMEM] * 4,
        out_specs=[IN_VMEM, IN_VMEM],
        out_shape=[
            jax.ShapeDtypeStruct((1, VIS_ROW), F32),
            jax.ShapeDtypeStruct((lay.tiles, lay.side), F32),
        ],
        scratch_shapes=[pltpu.VMEM((lay.patches, lay.side), F32)],
        compiler_params=pltpu.CompilerParams(vmem_limit_bytes=VMEM_LIMIT),
        name="finish",
    )(tile_patch, table, flux, sums, messages)


def spread_kernel(count, place_ref, kept, received, own, *sends):
    for step, out in enumerate((own, *sends)):
        spot = place_ref[0] ^ step
        out[...] = (kept[spot].astype(F32) + received[spot].astype(F32)).astype(out.dtype)


def spread(place, terms):
    kept, received = terms
    count, shape = kept.shape[0], kept.shape[1:]
    out = pl.pallas_call(
        functools.partial(spread_kernel, count),
        in_specs=[pl.BlockSpec(memory_space=pltpu.SMEM), IN_VMEM, IN_VMEM],
        out_specs=[IN_VMEM] * count,
        out_shape=[pltpu.VMEM(shape, BF16)] * count,
        compiler_params=pltpu.CompilerParams(vmem_limit_bytes=VMEM_LIMIT),
        name="spread",
    )(place.reshape(1).astype(jnp.int32), kept, received)
    return out[0], out[1:]


def fold_kernel(place_ref, kept, received, out):
    second = pl.program_id(0)
    value = kept[place_ref[0], second].astype(F32) + received[0, 0].astype(F32)
    out[second] = value.astype(BF16)


def fold(place, kept, received):
    shape = kept.shape[1:]
    return pl.pallas_call(
        fold_kernel,
        grid_spec=pltpu.PrefetchScalarGridSpec(
            num_scalar_prefetch=1,
            grid=(shape[0],),
            in_specs=[
                IN_VMEM,
                pl.BlockSpec((1, 1, *shape[1:]), lambda second, place: (place[0], second, 0, 0, 0)),
            ],
            out_specs=IN_VMEM,
        ),
        out_shape=pltpu.VMEM(shape, BF16),
        compiler_params=pltpu.CompilerParams(vmem_limit_bytes=VMEM_LIMIT),
        name="fold",
    )(place.reshape(1).astype(jnp.int32), kept, in_hbm(received))


def after(array, *others):
    return lax.optimization_barrier((array, *others))[0]


class Stream:
    def __init__(self, lay, send, keep):
        core, x, high, low = lay.place()
        self.own, self.received = keep, [lay.swap_core(send)]
        self.stages = [
            (jnp.where(core == 0, x, low), lay.swap_first),
            (jnp.where(core == 0, low, x), lay.swap_second),
            (high, lay.swap_high),
        ]

    def step(self, *before):
        place, swap = self.stages.pop(0)
        received = self.received[0]
        if len(self.received) > 1:
            received = sum(array.astype(F32) for array in self.received)
        received = after(received, *before)
        if len(self.stages) == 2:
            count = received.shape[0]
            self.sent = [fold(place ^ step, self.own, received) for step in range(1, count)]
            self.own = fold(place, self.own, after(received, *self.sent))
        else:
            self.own, self.sent = spread(place, (self.own, received))
        self.received = [swap(array, step) for step, array in enumerate(self.sent, 1)]

    def pieces(self):
        return [self.own] + self.received


def gather_double(lay, array):
    array = array[None]
    for size, swap in ((lay.group, lay.swap_low), (lay.highs, lay.swap_high)):
        step = 1
        while step < size:
            array = jnp.concatenate([array, swap(array, step)])
            step *= 2
    return array


def sum_steps(lay, array):
    steps = []
    for size, swap in ((lay.group, lay.swap_low), (lay.highs, lay.swap_high)):
        step = 1
        while step < size:
            array = array + swap(array, step)
            steps.append(array)
            step *= 2
    return steps


def shards(
    images, warp_rows, warp_cols, tile_weight, tile_patch, match_rows, match_cols, src_row, src_col
):
    lay = Layout(images.shape[0], images.shape[1])
    tiles, side, patches = lay.tiles, lay.side, lay.patches
    core, x, high, low = lay.place()
    weight = tile_weight.astype(F32)

    warped, sends, keeps = warp(lay, tile_patch, tile_weight, images, warp_rows, warp_cols)
    streams = [Stream(lay, send, keep) for send, keep in zip(sends, keeps)]
    prepared = prepare(lay, src_row, src_col, match_rows[0], match_cols[0])
    for stream in streams:
        stream.step(*prepared)

    named = (tile_patch[:, None] == jnp.arange(patches)[None, :]).astype(F32)
    counts = jnp.sum(named.reshape(tiles // VIS_ROW, VIS_ROW, patches), axis=0)
    table = jnp.concatenate([counts, jnp.sum(named * weight[:, None], axis=0, keepdims=True)])
    table = jnp.pad(table, ((0, 7 - VIS_ROW), (0, 0))).T.reshape(1, -1)
    table = jnp.pad(table, ((0, 0), (0, side - table.shape[1])))
    sources = jnp.concatenate([src_row.astype(F32), src_col.astype(F32), table])
    sources = after(sources, streams[-1].sent[-1])
    gathered = gather_double(lay, sources)
    all_rows, all_cols = gathered[:, 0:1, :], gathered[:, 1:2, :]
    table = jnp.sum(gathered[:, 2:3, :], axis=0)
    tile_place = ((tile_patch // lay.group) ^ high) * lay.group + ((tile_patch % lay.group) ^ low)

    for stream in streams:
        stream.step(gathered)
    tile_place = after(tile_place, streams[-1].own)
    flux, sums = forced_flux(lay, tile_patch, tile_place, warped, all_rows, all_cols)
    for stream in streams:
        stream.step(sums)
    sums = after(sums, streams[-1].own)
    steps = sum_steps(lay, sums)
    sums = steps[-1].reshape(patches, VIS_ROW, side)

    extra = -(-(lay.visits + 1) // 8) * 8
    pieces = [piece for stream in streams for piece in stream.pieces()]
    pieces[0] = after(pieces[0], steps[0])
    messages, fluxes = match(lay, extra, pieces, prepared, table)
    parts = [messages[0]] + [lay.swap_visit(messages[step], step) for step in range(1, lay.visits)]
    fluxes = after(fluxes, steps[1])
    fluxes = lax.all_to_all(fluxes, AXES, 0, 0, tiled=True)
    coadd = coadd_rows(lay, match_cols[0], parts)
    zero, resid = finish(lay, tile_patch, table, flux, sums, fluxes)
    return (coadd[None], zero.reshape(-1), resid)


def solution(mesh):
    in_specs = (
        P(AXES, None, None),
        P(AXES, None, None),
        P(AXES, None, None),
        P(AXES),
        P(AXES),
        P("patch", None, None),
        P("patch", None, None),
        P("patch", None),
        P("patch", None),
    )
    out_specs = (P("patch", "visit", None), P("visit"), P(AXES, None))
    return jax.shard_map(shards, mesh=mesh, in_specs=in_specs, out_specs=out_specs, check_vma=False)
```

time: 121 us -> 85.5 us (0.71)
  Pallas kernels: 42.3 us -> 28.6 us
  other arithmetic: 13.9 us -> 0.33 us
  matrix products: 3.7 us -> 0 us
  waiting for transfers between devices: 20.9 us -> 17.8 us
    pallas_call x4 -> x8, Pallas kernels: 31.9 us -> 21 us  [the longest x1 12 us: warp(): pl.pallas_call(functools.partial(warp_kernel, lay), in_specs=[pl.BlockSpe...]
    convert_element_type x8 -> x2, other arithmetic: 7.72 us -> 0.01 us  [shards(): sources = jnp.concatenate([src_row.astype(F32), src_col.astype(F32), table])]
    ppermute x27 -> x15, starting transfers between devices: 30.6 us -> 23.1 us  [permute(): return lax.ppermute(array, AXES, pairs)]
    all_to_all x0 -> x1, starting transfers between devices: none -> 7.14 us  [shards(): fluxes = lax.all_to_all(fluxes, AXES, 0, 0, tiled=True)]
    unnamed x24 -> x32, local copies, waits for them, and re-layouts: 1.61 us -> 6.95 us
    dot_general x4 -> x0, matrix products: 3.7 us -> none  [shards(): lax.dot_general(part[:width], lax.dynamic_index_in_dim(by_visit, visit ^...]
    add x5 -> x3, other arithmetic: 3.57 us -> 0.03 us  [sum_steps(): array = array + swap(array, step)]
    ppermute x27 -> x15, waiting for transfers between devices: 20.9 us -> 17.8 us  [permute(): return lax.ppermute(array, AXES, pairs)]
  transfers between devices with their start and end apart: 27 -> 16, of which waited for: 10 -> 9; matrix products, arithmetic and copies ran while one was open for 15% -> 1% of each run, Pallas kernels for 20% -> 13%
where the time goes in v2:
time: 85.5 us; the launch traced here: 85.1 us
  starting transfers between devices  30.3 us (35%)
  Pallas kernels  28.6 us (33%)
  waiting for transfers between devices  17.8 us (21%)
  local copies, waits for them, and re-layouts  7.21 us (8%)
    ppermute x15, starting transfers between devices, permute(): return lax.ppermute(array, AXES, pairs)  23.1 us
    ppermute x15, waiting for transfers between devices, permute(): return lax.ppermute(array, AXES, pairs)  17.8 us
    pallas_call x1, Pallas kernels, warp(): pl.pallas_call(functools.partial(warp_kernel, lay), in_specs=[pl.BlockSpe...  12 us
    all_to_all x1, starting transfers between devices, shards(): fluxes = lax.all_to_all(fluxes, AXES, 0, 0, tiled=True)  7.14 us
    unnamed x32, local copies, waits for them, and re-layouts  6.95 us
    pallas_call x1, Pallas kernels, forced_flux(): pl.pallas_call(functools.partial(flux_kernel, lay), grid_spec=pltpu.Prefe...  6.21 us
    pallas_call x2, Pallas kernels, fold(): pl.pallas_call(fold_kernel, grid_spec=pltpu.PrefetchScalarGridSpec(num_sc...  3.67 us
    pallas_call x1, Pallas kernels, prepare(): pl.pallas_call(functools.partial(prepare_kernel, lay), in_specs=[IN_VMEM]...  2.14 us
  transfers between devices with their start and end apart: 16, of which 9 were waited for; matrix products, arithmetic and copies ran while one was open for 1% of the time, Pallas kernels for 13%

profile of v2, /device:TPU:0, one launch (start us, length us, event | category | flops | bytes accessed | tf_op | source)
XLA Modules:
  0.0 85.1 jit_solution(13092352762811206505)
XLA Ops:
  1.3 2.2 %copy-done.9 = bf16[8,512,512]{2,1,0:T(8,128)(2,1)S(1)} copy-done((bf16[8,512,512]{2,1,0:T(8,128)(2,1)S(1)}, bf16[8,512,512]{2,1,0:T(8,128)(2,1)}, u32[]{:S(2)}) %copy-start.9) | copy-done | bytes 4194328
  3.5 2.2 %copy-done.10 = bf16[8,512,512]{2,1,0:T(8,128)(2,1)S(1)} copy-done((bf16[8,512,512]{2,1,0:T(8,128)(2,1)S(1)}, bf16[8,512,512]{2,1,0:T(8,128)(2,1)}, u32[]{:S(2)}) %copy-start.10) | copy-done | bytes 4194328
  6.3 12.0 %warp.1 = (bf16[8,512,512]{2,1,0:T(8,128)(2,1)}, bf16[2,2,4,512,128]{4,3,2,1,0:T(8,128)(2,1)}, bf16[2,2,4,512,128]{4,3,2,1,0:T(8,128)(2,1)S(1)}) custom-call(s32[8]{0:T(128)S(1)} %copy-done.5, bf16[8]{0:T(256)(128)(2,1)S(1)} %copy-done.14, bf16[8,512,512]{2,1,0:T(8,128)(2,1)S(1)} %copy-done.9, bf16[8,512,512]{2,1,0:T(8,128)(2,1)S(1)} %copy-done.10, ...), custom_call_target="tpu_custom_call" | custom-call | flops 4294967296 | bytes 16777216 | tf_op jit(solution)/shard_map/warp/pallas_call | solution.py:147
  18.8 1.2 %copy-done.12 = f32[1,512,512]{2,1,0:T(8,128)S(1)} copy-done((f32[1,512,512]{2,1,0:T(8,128)S(1)}, f32[1,512,512]{2,1,0:T(8,128)}, u32[]{:S(2)}) %copy-start.12) | copy-done | bytes 1048600
  20.1 2.1 %prepare.1 = (bf16[512,512]{1,0:T(8,128)(2,1)}, bf16[512,512]{1,0:T(8,128)(2,1)}, f32[512,512]{1,0:T(8,128)}, bf16[128,512]{1,0:T(8,128)(2,1)}, bf16[128,512]{1,0:T(8,128)(2,1)}) custom-call(s32[1,512]{1,0:T(1,128)S(1)} %copy-done.8, s32[1,512]{1,0:T(1,128)S(1)} %copy-done.7, f32[512,512]{1,0:T(8,128)S(1)} %bitcast.15, f32[512,512]{1,0:T(8,128)S(1)} %bitcast.16), custom_call_target="tpu_custom_call" | custom-call | flops 1073741824 | bytes 5242880 | tf_op jit(solution)/shard_map/prepare/pallas_call | solution.py:252
  22.2 0.7 collective-permute-done.received
  23.0 2.3 %fold.2 = bf16[2,4,512,128]{3,2,1,0:T(8,128)(2,1)} custom-call(s32[1]{0:T(128)} %bitcast.5.place_ref, bf16[2,2,4,512,128]{4,3,2,1,0:T(8,128)(2,1)S(1)} %get-tuple-element.35.kept, bf16[2,2,4,512,128]{4,3,2,1,0:T(8,128)(2,1)} %collective-permute-done.received), custom_call_target="tpu_custom_call" | custom-call | tf_op jit(solution)/shard_map/fold/pallas_call | solution.py:421
  25.3 2.9 %collective-permute-start.1 = (bf16[2,4,512,128]{3,2,1,0:T(8,128)(2,1)}, bf16[2,4,512,128]{3,2,1,0:T(8,128)(2,1)S(1)}, u32[]{:S(2)}, u32[]{:S(2)}) collective-permute-start(bf16[2,4,512,128]{3,2,1,0:T(8,128)(2,1)} %fold.2), channel_id=1, source_target_pairs={{0,16},{1,17},{2,18},{3,19},{4,20},{5,21},{6,22},{7,23},{8,9},{9,8... | collective-permute-start | bytes 3145736 | tf_op jit(solution)/shard_map/ppermute | solution.py:46
  28.6 1.6 %collective-permute-start.2 = (f32[1,3,512]{2,1,0:T(4,128)S(1)}, f32[1,3,512]{2,1,0:T(4,128)S(1)}, u32[]{:S(2)}, u32[]{:S(2)}) collective-permute-start(f32[1,3,512]{2,1,0:T(4,128)S(1)} %bitcast.18), channel_id=1, source_target_pairs={{0,1},{1,0},{2,3},{3,2},{4,5},{5,4},{6,7},{7,6},{8,9},{9,8},{10,11... | collective-permute-start | bytes 18440 | tf_op jit(solution)/shard_map/ppermute | solution.py:46
  30.2 2.3 %collective-permute-done.2 = f32[1,3,512]{2,1,0:T(4,128)S(1)} collective-permute-done((f32[1,3,512]{2,1,0:T(4,128)S(1)}, f32[1,3,512]{2,1,0:T(4,128)S(1)}, u32[]{:S(2)}, u32[]{:S(2)}) %collective-permute-start.2) | collective-permute-done | bytes 6176 | tf_op jit(solution)/shard_map/ppermute | solution.py:46
  32.5 1.6 %collective-permute-start.3 = (f32[2,3,512]{2,1,0:T(4,128)S(1)}, f32[2,3,512]{2,1,0:T(4,128)S(1)}, u32[]{:S(2)}, u32[]{:S(2)}) collective-permute-start(f32[2,3,512]{2,1,0:T(4,128)S(1)} %pad_maximum_fusion.2), channel_id=1, source_target_pairs={{0,2},{1,3},{2,0},{3,1},{4,6},{5,7},{6,4},{7,5},{8,10},{9,11},{10,... | collective-permute-start | bytes 36872 | tf_op jit(solution)/shard_map/ppermute | solution.py:46
  34.1 2.2 %collective-permute-done.3 = f32[2,3,512]{2,1,0:T(4,128)S(1)} collective-permute-done((f32[2,3,512]{2,1,0:T(4,128)S(1)}, f32[2,3,512]{2,1,0:T(4,128)S(1)}, u32[]{:S(2)}, u32[]{:S(2)}) %collective-permute-start.3) | collective-permute-done | bytes 12320 | tf_op jit(solution)/shard_map/ppermute | solution.py:46
  36.2 2.7 %collective-permute-start.4 = (f32[4,3,512]{2,1,0:T(4,128)S(1)}, f32[4,3,512]{2,1,0:T(4,128)S(1)}, u32[]{:S(2)}, u32[]{:S(2)}) collective-permute-start(f32[4,3,512]{2,1,0:T(4,128)S(1)} %pad_maximum_fusion.1), channel_id=1, source_target_pairs={{0,4},{1,5},{2,6},{3,7},{4,0},{5,1},{6,2},{7,3},{8,12},{9,13},{10,... | collective-permute-start | bytes 73736 | tf_op jit(solution)/shard_map/ppermute | solution.py:46
  38.9 1.3 %fold.3.kept = bf16[2,4,512,128]{3,2,1,0:T(8,128)(2,1)S(1)} custom-call(s32[1]{0:T(128)} %bitcast.3.place_ref, bf16[2,2,4,512,128]{4,3,2,1,0:T(8,128)(2,1)S(1)} %get-tuple-element.35.kept, bf16[2,2,4,512,128]{4,3,2,1,0:T(8,128)(2,1)} %collective-permute-done.received), custom_call_target="tpu_custom_call" | custom-call | tf_op jit(solution)/shard_map/fold/pallas_call | solution.py:421
  40.2 0.9 %collective-permute-done.4 = f32[4,3,512]{2,1,0:T(4,128)S(1)} collective-permute-done((f32[4,3,512]{2,1,0:T(4,128)S(1)}, f32[4,3,512]{2,1,0:T(4,128)S(1)}, u32[]{:S(2)}, u32[]{:S(2)}) %collective-permute-start.4) | collective-permute-done | bytes 24608 | tf_op jit(solution)/shard_map/ppermute | solution.py:46
  41.4 2.1 %collective-permute-start.5 = (bf16[4,512,128]{2,1,0:T(8,128)(2,1)S(1)}, bf16[4,512,128]{2,1,0:T(8,128)(2,1)S(1)}, u32[]{:S(2)}, u32[]{:S(2)}) collective-permute-start(bf16[4,512,128]{2,1,0:T(8,128)(2,1)S(1)} %get-tuple-element.47), channel_id=1, source_target_pairs={{0,1},{1,0},{2,3},{3,2},{4,5},{5,4},{6,7},{7,6},{8,24},{9,25},{10,... | collective-permute-start | bytes 1572872 | tf_op jit(solution)/shard_map/ppermute | solution.py:46
  43.6 6.2 %forced_flux.1 = (f32[8,1,512]{2,1,0:T(1,128)S(1)}, f32[32,512]{1,0:T(8,128)S(1)}) custom-call(s32[8]{0:T(128)S(1)} %copy-done.6, s32[8]{0:T(128)S(1)} %fusion.2.place_ref, bf16[8,512,512]{2,1,0:T(8,128)(2,1)} %get-tuple-element.49.warped, f32[8,1,512]{2,1,0:T(1,128)S(1)} %get-tuple-element.69.refs_0_.refs_1_, ...), custom_call_target="tpu_custom_call" | custom-call | flops 2147483648 | bytes 4194304 | tf_op jit(solution)/shard_map/forced_flux/pallas_call | solution.py:204
  49.9 0.8 collective-permute-done.5.received
  50.8 2.1 %collective-permute-start.6 = (f32[32,512]{1,0:T(8,128)S(1)}, f32[32,512]{1,0:T(8,128)S(1)}, u32[]{:S(2)}, u32[]{:S(2)}) collective-permute-start(f32[32,512]{1,0:T(8,128)S(1)} %get-tuple-element.53), channel_id=1, source_target_pairs={{0,1},{1,0},{2,3},{3,2},{4,5},{5,4},{6,7},{7,6},{8,9},{9,8},{10,11... | collective-permute-start | bytes 196616 | tf_op jit(solution)/shard_map/ppermute | solution.py:46
  52.9 1.6 %collective-permute-start.7 = (bf16[512,128]{1,0:T(8,128)(2,1)S(1)}, bf16[512,128]{1,0:T(8,128)(2,1)S(1)}, u32[]{:S(2)}, u32[]{:S(2)}) collective-permute-start(bf16[512,128]{1,0:T(8,128)(2,1)S(1)} %get-tuple-element.55), channel_id=1, source_target_pairs={{0,2},{1,3},{2,0},{3,1},{4,6},{5,7},{6,4},{7,5},{8,10},{9,11},{10,... | collective-permute-start | bytes 393224 | tf_op jit(solution)/shard_map/ppermute | solution.py:46
  54.5 2.6 %collective-permute-start.8 = (bf16[512,128]{1,0:T(8,128)(2,1)S(1)}, bf16[512,128]{1,0:T(8,128)(2,1)S(1)}, u32[]{:S(2)}, u32[]{:S(2)}) collective-permute-start(bf16[512,128]{1,0:T(8,128)(2,1)S(1)} %get-tuple-element.56), channel_id=1, source_target_pairs={{0,4},{1,5},{2,6},{3,7},{4,0},{5,1},{6,2},{7,3},{8,12},{9,13},{10,... | collective-permute-start | bytes 393224 | tf_op jit(solution)/shard_map/ppermute | solution.py:46
  57.3 0.7 collective-permute-start.13
  58.0 6.0 %collective-permute-done.13 = f32[32,512]{1,0:T(8,128)S(1)} collective-permute-done((f32[32,512]{1,0:T(8,128)S(1)}, f32[32,512]{1,0:T(8,128)S(1)}, u32[]{:S(2)}, u32[]{:S(2)}) %collective-permute-start.13) | collective-permute-done | bytes 65568 | tf_op jit(solution)/shard_map/ppermute | solution.py:46
  64.1 1.2 %collective-permute-done.9.refs_3_ = bf16[512,128]{1,0:T(8,128)(2,1)S(1)} collective-permute-done((bf16[512,128]{1,0:T(8,128)(2,1)S(1)}, bf16[512,128]{1,0:T(8,128)(2,1)S(1)}, u32[]{:S(2)}, u32[]{:S(2)}) %collective-permute-start.9) | collective-permute-done | bytes 131104 | tf_op jit(solution)/shard_map/ppermute | solution.py:46
  65.3 1.6 %match.1 = (bf16[144,128]{1,0:T(8,128)(2,1)S(1)}, bf16[144,128]{1,0:T(8,128)(2,1)S(1)}, bf16[144,128]{1,0:T(8,128)(2,1)S(1)}, bf16[144,128]{1,0:T(8,128)(2,1)S(1)}, f32[32,8,128]{2,1,0:T(8,128)}) custom-call(bf16[512,128]{1,0:T(8,128)(2,1)S(1)} %get-tuple-element.54.refs_0_, bf16[512,128]{1,0:T(8,128)(2,1)S(1)} %collective-permute-done.7.refs_1_, ...), custom_call_target="tpu_custom_call" | custom-call | flops 402653184 | bytes 2621440 | tf_op jit(solution)/shard_map/match/pallas_call | solution.py:301
  67.0 7.1 %all-to-all-start = ((f32[32,8,128]{2,1,0:T(8,128)}), f32[32,8,128]{2,1,0:T(8,128)S(1)}, u32[]{:S(2)}, u32[]{:S(2)}) async-start(f32[32,8,128]{2,1,0:T(8,128)} %get-tuple-element.64), calls=%async_computation | async-start | bytes 262144 | tf_op jit(solution)/shard_map/all_to_all | solution.py:533
  74.4 1.7 %collective-permute-start.11 = (bf16[144,128]{1,0:T(8,128)(2,1)S(1)}, bf16[144,128]{1,0:T(8,128)(2,1)S(1)}, u32[]{:S(2)}, u32[]{:S(2)}) collective-permute-start(bf16[144,128]{1,0:T(8,128)(2,1)S(1)} %get-tuple-element.60), channel_id=1, source_target_pairs={{0,16},{1,17},{2,18},{3,19},{4,20},{5,21},{6,22},{7,23},{8,24},{9,... | collective-permute-start | bytes 110600 | tf_op jit(solution)/shard_map/ppermute | solution.py:46
  76.1 2.6 %collective-permute-start.14 = (f32[32,512]{1,0:T(8,128)S(1)}, f32[32,512]{1,0:T(8,128)S(1)}, u32[]{:S(2)}, u32[]{:S(2)}) collective-permute-start(f32[32,512]{1,0:T(8,128)S(1)} %add.38), channel_id=1, source_target_pairs={{0,4},{1,5},{2,6},{3,7},{4,0},{5,1},{6,2},{7,3},{8,12},{9,13},{10,... | collective-permute-start | bytes 196616 | tf_op jit(solution)/shard_map/ppermute | solution.py:46
  78.7 1.0 %collective-permute-done.12.refs_3_ = bf16[144,128]{1,0:T(8,128)(2,1)S(1)} collective-permute-done((bf16[144,128]{1,0:T(8,128)(2,1)S(1)}, bf16[144,128]{1,0:T(8,128)(2,1)S(1)}, u32[]{:S(2)}, u32[]{:S(2)}) %collective-permute-start.12) | collective-permute-done | bytes 36896 | tf_op jit(solution)/shard_map/ppermute | solution.py:46
  79.8 1.2 %coadd_rows.1 = f32[128,512]{1,0:T(8,128)} custom-call(f32[512,512]{1,0:T(8,128)S(1)} %bitcast.17, bf16[144,128]{1,0:T(8,128)(2,1)S(1)} %get-tuple-element.58.refs_0_, bf16[144,128]{1,0:T(8,128)(2,1)S(1)} %collective-permute-done.10.refs_1_, bf16[144,128]{1,0:T(8,128)(2,1)S(1)} %collective-permute-done.11.refs_2_, ...), custom_call_target="tpu_custom_call" | custom-call | flops 402653184 | bytes 1572864 | tf_op jit(solution)/shard_map/coadd_rows/pallas_call | solution.py:340
  80.9 2.6 %collective-permute-done.14 = f32[32,512]{1,0:T(8,128)S(1)} collective-permute-done((f32[32,512]{1,0:T(8,128)S(1)}, f32[32,512]{1,0:T(8,128)S(1)}, u32[]{:S(2)}, u32[]{:S(2)}) %collective-permute-start.14) | collective-permute-done | bytes 65568 | tf_op jit(solution)/shard_map/ppermute | solution.py:46
  83.6 1.5 %finish.1 = (f32[1,4]{1,0:T(1,128)}, f32[8,512]{1,0:T(8,128)}) custom-call(s32[8]{0:T(128)S(1)} %copy-done.6, f32[1,512]{1,0:T(1,128)S(1)} %bitcast.14, f32[8,1,512]{2,1,0:T(1,128)S(1)} %get-tuple-element.62.flux, f32[8,4,512]{2,1,0:T(4,128)S(1)} %reshape.44.sums, f32[32,8,128]{2,1,0:T(8,128)S(1)} %all-to-all-done.messages), custom_call_target="tpu_custom_call" | custom-call | tf_op jit(solution)/shard_map/finish/pallas_call | solution.py:379
  (61 shorter events, 3.4 us)
Async XLA Ops:
  0.6 0.7 copy-start.5
  1.3 2.2 %copy-start.9 = (bf16[8,512,512]{2,1,0:T(8,128)(2,1)S(1)}, bf16[8,512,512]{2,1,0:T(8,128)(2,1)}, u32[]{:S(2)}) copy-start(bf16[8,512,512]{2,1,0:T(8,128)(2,1)} %images.1) | copy-start | bytes 12582916
  3.5 2.2 %copy-start.10 = (bf16[8,512,512]{2,1,0:T(8,128)(2,1)S(1)}, bf16[8,512,512]{2,1,0:T(8,128)(2,1)}, u32[]{:S(2)}) copy-start(bf16[8,512,512]{2,1,0:T(8,128)(2,1)} %rows.1) | copy-start | bytes 12582916
  5.7 0.7 copy-start.14
  6.3 12.5 %copy-start.7 = (s32[1,512]{1,0:T(1,128)S(1)}, s32[1,512]{1,0:T(1,128)}, u32[]{:S(2)}) copy-start(s32[1,512]{1,0:T(1,128)} %src_col.1) | copy-start | bytes 6148
  6.3 12.5 %copy-start.8 = (s32[1,512]{1,0:T(1,128)S(1)}, s32[1,512]{1,0:T(1,128)}, u32[]{:S(2)}) copy-start(s32[1,512]{1,0:T(1,128)} %src_row.1) | copy-start | bytes 6148
  6.3 12.5 %copy-start.11 = (f32[1,512,512]{2,1,0:T(8,128)S(1)}, f32[1,512,512]{2,1,0:T(8,128)}, u32[]{:S(2)}) copy-start(f32[1,512,512]{2,1,0:T(8,128)} %param.14) | copy-start | bytes 3145732
  18.3 4.6 %collective-permute-start = (bf16[2,2,4,512,128]{4,3,2,1,0:T(8,128)(2,1)}, bf16[2,2,4,512,128]{4,3,2,1,0:T(8,128)(2,1)}, u32[]{:S(2)}, u32[]{:S(2)}) collective-permute-start(bf16[2,2,4,512,128]{4,3,2,1,0:T(8,128)(2,1)} %get-tuple-element.36), channel_id=1, source_target_pairs={{0,8},{1,9},{2,10},{3,11},{4,12},{5,13},{6,14},{7,15},{8,0},{9,1},... | collective-permute-start | bytes 6291464 | tf_op jit(solution)/shard_map/ppermute | solution.py:46
  18.8 1.2 %copy-start.12 = (f32[1,512,512]{2,1,0:T(8,128)S(1)}, f32[1,512,512]{2,1,0:T(8,128)}, u32[]{:S(2)}) copy-start(f32[1,512,512]{2,1,0:T(8,128)} %param.15) | copy-start | bytes 3145732
  20.1 8.1 %copy-start.15 = (bf16[8]{0:T(256)(128)(2,1)S(1)}, bf16[8]{0:T(256)(128)(2,1)}, u32[]{:S(2)}) copy-start(bf16[8]{0:T(256)(128)(2,1)} %weight_ref.1) | copy-start | bytes 52
  20.1 8.1 %copy-start.6 = (s32[8]{0:T(128)S(1)}, s32[8]{0:T(128)}, u32[]{:S(2)}) copy-start(s32[8]{0:T(128)} %patch_ref.5) | copy-start | bytes 100
  25.3 15.8 %collective-permute-start.1 = (bf16[2,4,512,128]{3,2,1,0:T(8,128)(2,1)}, bf16[2,4,512,128]{3,2,1,0:T(8,128)(2,1)S(1)}, u32[]{:S(2)}, u32[]{:S(2)}) collective-permute-start(bf16[2,4,512,128]{3,2,1,0:T(8,128)(2,1)} %fold.2), channel_id=1, source_target_pairs={{0,16},{1,17},{2,18},{3,19},{4,20},{5,21},{6,22},{7,23},{8,9},{9,8... | collective-permute-start | bytes 3145736 | tf_op jit(solution)/shard_map/ppermute | solution.py:46
  28.6 3.9 %collective-permute-start.2 = (f32[1,3,512]{2,1,0:T(4,128)S(1)}, f32[1,3,512]{2,1,0:T(4,128)S(1)}, u32[]{:S(2)}, u32[]{:S(2)}) collective-permute-start(f32[1,3,512]{2,1,0:T(4,128)S(1)} %bitcast.18), channel_id=1, source_target_pairs={{0,1},{1,0},{2,3},{3,2},{4,5},{5,4},{6,7},{7,6},{8,9},{9,8},{10,11... | collective-permute-start | bytes 18440 | tf_op jit(solution)/shard_map/ppermute | solution.py:46
  32.5 3.7 %collective-permute-start.3 = (f32[2,3,512]{2,1,0:T(4,128)S(1)}, f32[2,3,512]{2,1,0:T(4,128)S(1)}, u32[]{:S(2)}, u32[]{:S(2)}) collective-permute-start(f32[2,3,512]{2,1,0:T(4,128)S(1)} %pad_maximum_fusion.2), channel_id=1, source_target_pairs={{0,2},{1,3},{2,0},{3,1},{4,6},{5,7},{6,4},{7,5},{8,10},{9,11},{10,... | collective-permute-start | bytes 36872 | tf_op jit(solution)/shard_map/ppermute | solution.py:46
  36.2 4.9 %collective-permute-start.4 = (f32[4,3,512]{2,1,0:T(4,128)S(1)}, f32[4,3,512]{2,1,0:T(4,128)S(1)}, u32[]{:S(2)}, u32[]{:S(2)}) collective-permute-start(f32[4,3,512]{2,1,0:T(4,128)S(1)} %pad_maximum_fusion.1), channel_id=1, source_target_pairs={{0,4},{1,5},{2,6},{3,7},{4,0},{5,1},{6,2},{7,3},{8,12},{9,13},{10,... | collective-permute-start | bytes 73736 | tf_op jit(solution)/shard_map/ppermute | solution.py:46
  41.4 9.3 %collective-permute-start.5 = (bf16[4,512,128]{2,1,0:T(8,128)(2,1)S(1)}, bf16[4,512,128]{2,1,0:T(8,128)(2,1)S(1)}, u32[]{:S(2)}, u32[]{:S(2)}) collective-permute-start(bf16[4,512,128]{2,1,0:T(8,128)(2,1)S(1)} %get-tuple-element.47), channel_id=1, source_target_pairs={{0,1},{1,0},{2,3},{3,2},{4,5},{5,4},{6,7},{7,6},{8,24},{9,25},{10,... | collective-permute-start | bytes 1572872 | tf_op jit(solution)/shard_map/ppermute | solution.py:46
  43.6 21.7 %copy-start = (f32[512,512]{1,0:T(8,128)S(1)}, f32[512,512]{1,0:T(8,128)}, u32[]{:S(2)}) copy-start(f32[512,512]{1,0:T(8,128)} %get-tuple-element.39.refs_6_) | copy-start | bytes 3145732
  43.6 21.7 %copy-start.1 = (bf16[512,512]{1,0:T(8,128)(2,1)S(1)}, bf16[512,512]{1,0:T(8,128)(2,1)}, u32[]{:S(2)}) copy-start(bf16[512,512]{1,0:T(8,128)(2,1)} %get-tuple-element.37.refs_4_) | copy-start | bytes 1572868
  43.6 21.7 %copy-start.2 = (bf16[512,512]{1,0:T(8,128)(2,1)S(1)}, bf16[512,512]{1,0:T(8,128)(2,1)}, u32[]{:S(2)}) copy-start(bf16[512,512]{1,0:T(8,128)(2,1)} %get-tuple-element.38.refs_5_) | copy-start | bytes 1572868
  43.6 21.7 %copy-start.3 = (bf16[128,512]{1,0:T(8,128)(2,1)S(1)}, bf16[128,512]{1,0:T(8,128)(2,1)}, u32[]{:S(2)}) copy-start(bf16[128,512]{1,0:T(8,128)(2,1)} %get-tuple-element.40.refs_7_) | copy-start | bytes 393220
  43.6 21.7 %copy-start.4 = (bf16[128,512]{1,0:T(8,128)(2,1)S(1)}, bf16[128,512]{1,0:T(8,128)(2,1)}, u32[]{:S(2)}) copy-start(bf16[128,512]{1,0:T(8,128)(2,1)} %get-tuple-element.41.refs_8_) | copy-start | bytes 393220
  49.8 29.9 %copy-start.13 = (f32[1,512,512]{2,1,0:T(8,128)S(1)}, f32[1,512,512]{2,1,0:T(8,128)}, u32[]{:S(2)}) copy-start(f32[1,512,512]{2,1,0:T(8,128)} %param.15) | copy-start | bytes 3145732
  50.8 6.5 %collective-permute-start.6 = (f32[32,512]{1,0:T(8,128)S(1)}, f32[32,512]{1,0:T(8,128)S(1)}, u32[]{:S(2)}, u32[]{:S(2)}) collective-permute-start(f32[32,512]{1,0:T(8,128)S(1)} %get-tuple-element.53), channel_id=1, source_target_pairs={{0,1},{1,0},{2,3},{3,2},{4,5},{5,4},{6,7},{7,6},{8,9},{9,8},{10,11... | collective-permute-start | bytes 196616 | tf_op jit(solution)/shard_map/ppermute | solution.py:46
  52.9 11.2 %collective-permute-start.7 = (bf16[512,128]{1,0:T(8,128)(2,1)S(1)}, bf16[512,128]{1,0:T(8,128)(2,1)S(1)}, u32[]{:S(2)}, u32[]{:S(2)}) collective-permute-start(bf16[512,128]{1,0:T(8,128)(2,1)S(1)} %get-tuple-element.55), channel_id=1, source_target_pairs={{0,2},{1,3},{2,0},{3,1},{4,6},{5,7},{6,4},{7,5},{8,10},{9,11},{10,... | collective-permute-start | bytes 393224 | tf_op jit(solution)/shard_map/ppermute | solution.py:46
  54.5 9.6 %collective-permute-start.8 = (bf16[512,128]{1,0:T(8,128)(2,1)S(1)}, bf16[512,128]{1,0:T(8,128)(2,1)S(1)}, u32[]{:S(2)}, u32[]{:S(2)}) collective-permute-start(bf16[512,128]{1,0:T(8,128)(2,1)S(1)} %get-tuple-element.56), channel_id=1, source_target_pairs={{0,4},{1,5},{2,6},{3,7},{4,0},{5,1},{6,2},{7,3},{8,12},{9,13},{10,... | collective-permute-start | bytes 393224 | tf_op jit(solution)/shard_map/ppermute | solution.py:46
  57.0 8.3 %collective-permute-start.9 = (bf16[512,128]{1,0:T(8,128)(2,1)S(1)}, bf16[512,128]{1,0:T(8,128)(2,1)S(1)}, u32[]{:S(2)}, u32[]{:S(2)}) collective-permute-start(bf16[512,128]{1,0:T(8,128)(2,1)S(1)} %get-tuple-element.57), channel_id=1, source_target_pairs={{0,6},{1,7},{2,4},{3,5},{4,2},{5,3},{6,0},{7,1},{8,14},{9,15},{10,... | collective-permute-start | bytes 393224 | tf_op jit(solution)/shard_map/ppermute | solution.py:46
  57.3 6.8 %collective-permute-start.13 = (f32[32,512]{1,0:T(8,128)S(1)}, f32[32,512]{1,0:T(8,128)S(1)}, u32[]{:S(2)}, u32[]{:S(2)}) collective-permute-start(f32[32,512]{1,0:T(8,128)S(1)} %add.37), channel_id=1, source_target_pairs={{0,2},{1,3},{2,0},{3,1},{4,6},{5,7},{6,4},{7,5},{8,10},{9,11},{10,... | collective-permute-start | bytes 196616 | tf_op jit(solution)/shard_map/ppermute | solution.py:46
  67.0 16.6 %all-to-all-start = ((f32[32,8,128]{2,1,0:T(8,128)}), f32[32,8,128]{2,1,0:T(8,128)S(1)}, u32[]{:S(2)}, u32[]{:S(2)}) async-start(f32[32,8,128]{2,1,0:T(8,128)} %get-tuple-element.64), calls=%async_computation | async-start | bytes 262144 | tf_op jit(solution)/shard_map/all_to_all | solution.py:533
  74.1 4.6 %collective-permute-start.10 = (bf16[144,128]{1,0:T(8,128)(2,1)S(1)}, bf16[144,128]{1,0:T(8,128)(2,1)S(1)}, u32[]{:S(2)}, u32[]{:S(2)}) collective-permute-start(bf16[144,128]{1,0:T(8,128)(2,1)S(1)} %get-tuple-element.59), channel_id=1, source_target_pairs={{0,8},{1,9},{2,10},{3,11},{4,12},{5,13},{6,14},{7,15},{8,0},{9,1},... | collective-permute-start | bytes 110600 | tf_op jit(solution)/shard_map/ppermute | solution.py:46
  74.4 4.3 %collective-permute-start.11 = (bf16[144,128]{1,0:T(8,128)(2,1)S(1)}, bf16[144,128]{1,0:T(8,128)(2,1)S(1)}, u32[]{:S(2)}, u32[]{:S(2)}) collective-permute-start(bf16[144,128]{1,0:T(8,128)(2,1)S(1)} %get-tuple-element.60), channel_id=1, source_target_pairs={{0,16},{1,17},{2,18},{3,19},{4,20},{5,21},{6,22},{7,23},{8,24},{9,... | collective-permute-start | bytes 110600 | tf_op jit(solution)/shard_map/ppermute | solution.py:46
  76.1 3.6 %collective-permute-start.12 = (bf16[144,128]{1,0:T(8,128)(2,1)S(1)}, bf16[144,128]{1,0:T(8,128)(2,1)S(1)}, u32[]{:S(2)}, u32[]{:S(2)}) collective-permute-start(bf16[144,128]{1,0:T(8,128)(2,1)S(1)} %get-tuple-element.61), channel_id=1, source_target_pairs={{0,24},{1,25},{2,26},{3,27},{4,28},{5,29},{6,30},{7,31},{8,16},{9,... | collective-permute-start | bytes 110600 | tf_op jit(solution)/shard_map/ppermute | solution.py:46
  76.1 7.4 %collective-permute-start.14 = (f32[32,512]{1,0:T(8,128)S(1)}, f32[32,512]{1,0:T(8,128)S(1)}, u32[]{:S(2)}, u32[]{:S(2)}) collective-permute-start(f32[32,512]{1,0:T(8,128)S(1)} %add.38), channel_id=1, source_target_pairs={{0,4},{1,5},{2,6},{3,7},{4,0},{5,1},{6,2},{7,3},{8,12},{9,13},{10,... | collective-permute-start | bytes 196616 | tf_op jit(solution)/shard_map/ppermute | solution.py:46

commit v3 on v2

--- a/solution.py
+++ b/solution.py
@@ -8,6 +8,7 @@
 from jax.sharding import PartitionSpec as P
 
 VIS_ROW = 4
+CAP = 2
 APERTURE = 2.5
 HIGHEST = lax.Precision.HIGHEST
 F32 = jnp.float32
@@ -74,11 +75,16 @@
         return self.permute(array, partner)
 
 
-def warp_kernel(lay, patch_ref, weight_ref, images, rows, cols, warped, *refs):
-    outs, (image, row, col, half, result, weights, total, arrive, leave, small) = refs[: 2 * PARTS], refs[2 * PARTS :]
+def warp_kernel(lay, patch_hbm, weight_hbm, images, rows, cols, warped, *refs):
+    outs, refs = refs[: 2 * PARTS], refs[2 * PARTS :]
+    image, row, col, half, result, weights, lines, stage, patches, named, chosen, arrive, leave, depart, small = refs
     sends, keeps = outs[:PARTS], outs[PARTS:]
-    fetch = pltpu.make_async_copy(weight_ref, weights, small)
-    fetch.start()
+    fetches = [
+        pltpu.make_async_copy(patch_hbm, patches, small.at[0]),
+        pltpu.make_async_copy(weight_hbm, weights, small.at[1]),
+    ]
+    for fetch in fetches:
+        fetch.start()
     loads = []
     for tile in range(lay.tiles):
         loads.append(
@@ -89,50 +95,77 @@
         )
         for load in loads[-1]:
             load.start()
-    total[...] = jnp.zeros_like(total)
-    fetch.wait()
-    lane = lax.broadcasted_iota(jnp.int32, (1, lay.tiles), 1)
     stores = []
     for tile in range(lay.tiles + 1):
         if tile < lay.tiles:
             loads[tile][0].wait()
             loads[tile][1].wait()
+        if tile:
+            loads[tile - 1][2].wait()
+        if tile == lay.tiles - 2:
+            for patch in range(lay.patches):
+                named[patch] = 0
+                for slot in range(CAP):
+                    chosen[patch, slot] = 0
+            for fetch in fetches:
+                fetch.wait()
+            for other in range(lay.tiles):
+                patch = patches[other]
+                chosen[patch, named[patch]] = other
+                named[patch] = named[patch] + 1
+            spread = weights[...].astype(F32).reshape(1, lay.tiles)
+            lane = lax.broadcasted_iota(jnp.int32, (1, lay.tiles), 1)
+            for patch in range(lay.patches):
+                for slot in range(CAP):
+                    picked = jnp.logical_and(lane == chosen[patch, slot], named[patch] > slot)
+                    weight = jnp.sum(jnp.where(picked, spread, 0.0), keepdims=True)
+                    spot = patch * CAP + slot
+                    lines[spot : spot + 1, :] = jnp.broadcast_to(weight, (1, lay.width))
+        if tile < lay.tiles:
             half[tile % 2] = lax.dot_general(image[tile], col[tile], NT, preferred_element_type=F32).astype(BF16)
         if tile:
             last = tile - 1
-            loads[last][2].wait()
-            value = jnp.dot(row[last], half[last % 2], preferred_element_type=F32).astype(BF16)
-            result[last] = value
+            result[last] = jnp.dot(row[last], half[last % 2], preferred_element_type=F32).astype(BF16)
             stores.append(pltpu.make_async_copy(result.at[last], warped.at[last], leave.at[last]))
             stores[-1].start()
-            spread = weights[...].astype(F32).reshape(1, lay.tiles)
-            weight = jnp.sum(jnp.where(lane == last, spread, 0.0), keepdims=True)
-            total[patch_ref[last]] += weight * value.astype(F32)
-
-    def write(outs, core):
-        for first in range(lay.group):
-            for second in range(lay.group):
-                x, low = (first, second) if core == 0 else (second, first)
-                start = (2 * x + core) * lay.width
-                for high in range(lay.highs):
-                    for part, out in enumerate(outs):
-                        block = total[
-                            high * lay.group + low,
-                            part * lay.part : (part + 1) * lay.part,
-                            start : start + lay.width,
-                        ]
-                        out[first, second, high] = block.astype(BF16)
+
+    def block(core, first, second, high):
+        x, low = (first, second) if core == 0 else (second, first)
+        start = (2 * x + core) * lay.width
+        patch = high * lay.group + low
+        value = 0.0
+        for slot in range(CAP):
+            tile = chosen[patch, slot]
+            weight = lines[patch * CAP + slot : patch * CAP + slot + 1, :]
+            value = value + weight * result[tile, :, start : start + lay.width].astype(F32)
+        return value.astype(BF16)
 
     core = lax.axis_index("visit") % 2
+    places = [(f, g, h) for f in range(lay.group) for g in range(lay.group) for h in range(lay.highs)]
+    departures = [
+        pltpu.make_async_copy(
+            stage.at[first, second, high, pl.ds(part * lay.part, lay.part)],
+            sends[part].at[first, second, high],
+            depart.at[part, spot],
+        )
+        for part in range(PARTS)
+        for spot, (first, second, high) in enumerate(places)
+    ]
     for own in range(2):
 
         @pl.when(core == own)
         def _():
-            write(sends, 1 - own)
-            write(keeps, own)
-
-    for store in stores:
-        store.wait()
+            for spot, (first, second, high) in enumerate(places):
+                stage[first, second, high] = block(1 - own, first, second, high)
+                for part in range(PARTS):
+                    departures[part * len(places) + spot].start()
+            for first, second, high in places:
+                value = block(own, first, second, high)
+                for part in range(PARTS):
+                    keeps[part][first, second, high] = value[part * lay.part : (part + 1) * lay.part]
+
+    for copy in stores + departures:
+        copy.wait()
 
 
 def in_hbm(array):
@@ -146,9 +179,11 @@
     stack = pltpu.VMEM((tiles, side, side), BF16)
     out = pl.pallas_call(
         functools.partial(warp_kernel, lay),
-        in_specs=[pl.BlockSpec(memory_space=pltpu.SMEM)] + [in_any] * 4,
-        out_specs=[in_any] + [IN_VMEM] * (2 * PARTS),
-        out_shape=[pltpu.HBM((tiles, side, side), BF16)] + [pltpu.VMEM(pieces, BF16)] * (2 * PARTS),
+        in_specs=[in_any] * 5,
+        out_specs=[in_any] * (1 + PARTS) + [IN_VMEM] * PARTS,
+        out_shape=[pltpu.HBM((tiles, side, side), BF16)]
+        + [pltpu.HBM(pieces, BF16)] * PARTS
+        + [pltpu.VMEM(pieces, BF16)] * PARTS,
         scratch_shapes=[
             stack,
             stack,
@@ -156,17 +191,22 @@
             pltpu.VMEM((2, side, side), BF16),
             stack,
             pltpu.VMEM((tiles,), BF16),
-            pltpu.VMEM((lay.patches, side, side), F32),
+            pltpu.VMEM((lay.patches * CAP, lay.width), F32),
+            pltpu.VMEM((lay.group, lay.group, lay.highs, side, lay.width), BF16),
+            pltpu.SMEM((tiles,), jnp.int32),
+            pltpu.SMEM((lay.patches,), jnp.int32),
+            pltpu.SMEM((lay.patches, CAP), jnp.int32),
             pltpu.SemaphoreType.DMA((3, tiles)),
             pltpu.SemaphoreType.DMA((tiles,)),
-            pltpu.SemaphoreType.DMA,
+            pltpu.SemaphoreType.DMA((PARTS, lay.group * lay.group * lay.highs)),
+            pltpu.SemaphoreType.DMA((2,)),
         ],
         compiler_params=pltpu.CompilerParams(vmem_limit_bytes=WARP_LIMIT),
         cost_estimate=pl.CostEstimate(
             flops=4 * tiles * side**3, bytes_accessed=8 * tiles * side * side, transcendentals=0
         ),
         name="warp",
-    )(tile_patch, weight, images, warp_rows, warp_cols)
+    )(in_hbm(tile_patch), in_hbm(weight), in_hbm(images), in_hbm(warp_rows), in_hbm(warp_cols))
     return out[0], out[1 : 1 + PARTS], out[1 + PARTS :]
 
 
@@ -247,12 +287,13 @@
 
 def prepare(lay, src_row, src_col, match_rows, match_cols):
     side = lay.side
-    block = pltpu.HBM((lay.width, side), BF16)
-    square = pltpu.HBM((side, side), BF16)
+    block = pltpu.VMEM((lay.width, side), BF16)
+    square = pltpu.VMEM((side, side), BF16)
     return pl.pallas_call(
         functools.partial(prepare_kernel, lay),
         in_specs=[IN_VMEM] * 4,
-        out_shape=[square, square, pltpu.HBM((side, side), F32), block, block],
+        out_specs=[IN_VMEM] * 5,
+        out_shape=[square, square, pltpu.VMEM((side, side), F32), block, block],
         scratch_shapes=[pltpu.VMEM((lay.visits, lay.width, side), F32)],
         compiler_params=pltpu.CompilerParams(vmem_limit_bytes=VMEM_LIMIT),
         cost_estimate=pl.CostEstimate(
@@ -467,14 +508,8 @@
         return [self.own] + self.received
 
 
-def gather_double(lay, array):
-    array = array[None]
-    for size, swap in ((lay.group, lay.swap_low), (lay.highs, lay.swap_high)):
-        step = 1
-        while step < size:
-            array = jnp.concatenate([array, swap(array, step)])
-            step *= 2
-    return array
+def gather_patch(lay, near):
+    return jnp.concatenate([near] + [lay.swap_high(near, step) for step in range(1, lay.highs)])
 
 
 def sum_steps(lay, array):
@@ -482,7 +517,7 @@
     for size, swap in ((lay.group, lay.swap_low), (lay.highs, lay.swap_high)):
         step = 1
         while step < size:
-            array = array + swap(array, step)
+            array = (array.astype(F32) + swap(array, step).astype(F32)).astype(array.dtype)
             steps.append(array)
             step *= 2
     return steps
@@ -497,41 +532,39 @@
     weight = tile_weight.astype(F32)
 
     warped, sends, keeps = warp(lay, tile_patch, tile_weight, images, warp_rows, warp_cols)
-    streams = [Stream(lay, send, keep) for send, keep in zip(sends, keeps)]
-    prepared = prepare(lay, src_row, src_col, match_rows[0], match_cols[0])
-    for stream in streams:
-        stream.step(*prepared)
-
     named = (tile_patch[:, None] == jnp.arange(patches)[None, :]).astype(F32)
     counts = jnp.sum(named.reshape(tiles // VIS_ROW, VIS_ROW, patches), axis=0)
     table = jnp.concatenate([counts, jnp.sum(named * weight[:, None], axis=0, keepdims=True)])
     table = jnp.pad(table, ((0, 7 - VIS_ROW), (0, 0))).T.reshape(1, -1)
     table = jnp.pad(table, ((0, 0), (0, side - table.shape[1])))
-    sources = jnp.concatenate([src_row.astype(F32), src_col.astype(F32), table])
-    sources = after(sources, streams[-1].sent[-1])
-    gathered = gather_double(lay, sources)
+    sources = jnp.concatenate([src_row.astype(F32), src_col.astype(F32), table])[None]
+    sources = after(sources, keeps[-1])
+    near = jnp.concatenate([sources] + [lay.swap_low(sources, step) for step in range(1, lay.group)])
+
+    streams = [Stream(lay, send, keep) for send, keep in zip(sends, keeps)]
+    for stream in streams:
+        stream.step(near)
+    gathered = gather_patch(lay, after(near, streams[-1].sent[-1]))
     all_rows, all_cols = gathered[:, 0:1, :], gathered[:, 1:2, :]
     table = jnp.sum(gathered[:, 2:3, :], axis=0)
     tile_place = ((tile_patch // lay.group) ^ high) * lay.group + ((tile_patch % lay.group) ^ low)
-
-    for stream in streams:
-        stream.step(gathered)
-    tile_place = after(tile_place, streams[-1].own)
     flux, sums = forced_flux(lay, tile_patch, tile_place, warped, all_rows, all_cols)
+
     for stream in streams:
         stream.step(sums)
-    sums = after(sums, streams[-1].own)
-    steps = sum_steps(lay, sums)
-    sums = steps[-1].reshape(patches, VIS_ROW, side)
+    steps = sum_steps(lay, after(sums.astype(BF16), streams[-1].own))
+    prepared = prepare(lay, after(src_row, steps[1]), src_col, match_rows[0], match_cols[0])
+    for stream in streams:
+        stream.step(steps[1])
 
     extra = -(-(lay.visits + 1) // 8) * 8
     pieces = [piece for stream in streams for piece in stream.pieces()]
-    pieces[0] = after(pieces[0], steps[0])
     messages, fluxes = match(lay, extra, pieces, prepared, table)
     parts = [messages[0]] + [lay.swap_visit(messages[step], step) for step in range(1, lay.visits)]
-    fluxes = after(fluxes, steps[1])
+    fluxes = after(fluxes, steps[-1])
     fluxes = lax.all_to_all(fluxes, AXES, 0, 0, tiled=True)
     coadd = coadd_rows(lay, match_cols[0], parts)
+    sums = steps[-1].astype(F32).reshape(patches, VIS_ROW, side)
     zero, resid = finish(lay, tile_patch, table, flux, sums, fluxes)
     return (coadd[None], zero.reshape(-1), resid)
 

time: 85.5 us -> 72.6 us (0.85)
  starting transfers between devices: 30.3 us -> 22.9 us
  local copies, waits for them, and re-layouts: 7.21 us -> 0.33 us
  waiting for transfers between devices: 17.8 us -> 23.4 us
  Pallas kernels: 28.6 us -> 24.5 us
    unnamed x32 -> x16, local copies, waits for them, and re-layouts: 6.95 us -> 0.05 us
    ppermute x15 -> x16, waiting for transfers between devices: 17.8 us -> 22.5 us  [permute(): return lax.ppermute(array, AXES, pairs)]
    ppermute x15 -> x16, starting transfers between devices: 23.1 us -> 18.6 us  [permute(): return lax.ppermute(array, AXES, pairs)]
    all_to_all x1, starting transfers between devices: 7.14 us -> 4.31 us  [shards(): fluxes = lax.all_to_all(fluxes, AXES, 0, 0, tiled=True)]
    pallas_call x1, Pallas kernels: 12 us -> 9.55 us  [warp(): pl.pallas_call(functools.partial(warp_kernel, lay), in_specs=[in_any] * 5...]
    pallas_call x2, Pallas kernels: 3.67 us -> 2.69 us  [fold(): pl.pallas_call(fold_kernel, grid_spec=pltpu.PrefetchScalarGridSpec(num_sc...]
    all_to_all x1, waiting for transfers between devices: 0.01 us -> 0.93 us  [shards(): fluxes = lax.all_to_all(fluxes, AXES, 0, 0, tiled=True)]
  transfers between devices with their start and end apart: 16 -> 17, of which waited for: 9 -> 12; matrix products, arithmetic and copies ran while one was open for 1% -> 1% of each run, Pallas kernels for 13% -> 14%
where the time goes in v3:
time: 72.6 us; the launch traced here: 72.3 us
  Pallas kernels  24.5 us (34%)
  waiting for transfers between devices  23.4 us (32%)
  starting transfers between devices  22.9 us (32%)
  between operations  0.87 us (1%)
    ppermute x16, waiting for transfers between devices, permute(): return lax.ppermute(array, AXES, pairs)  22.5 us
    ppermute x16, starting transfers between devices, permute(): return lax.ppermute(array, AXES, pairs)  18.6 us
    pallas_call x1, Pallas kernels, warp(): pl.pallas_call(functools.partial(warp_kernel, lay), in_specs=[in_any] * 5...  9.55 us
    pallas_call x1, Pallas kernels, forced_flux(): pl.pallas_call(functools.partial(flux_kernel, lay), grid_spec=pltpu.Prefe...  6.17 us
    all_to_all x1, starting transfers between devices, shards(): fluxes = lax.all_to_all(fluxes, AXES, 0, 0, tiled=True)  4.31 us
    pallas_call x2, Pallas kernels, fold(): pl.pallas_call(fold_kernel, grid_spec=pltpu.PrefetchScalarGridSpec(num_sc...  2.69 us
    pallas_call x1, Pallas kernels, match(): pl.pallas_call(functools.partial(match_kernel, lay, extra), in_specs=[IN_...  1.64 us
    pallas_call x1, Pallas kernels, prepare(): pl.pallas_call(functools.partial(prepare_kernel, lay), in_specs=[IN_VMEM]...  1.46 us
  transfers between devices with their start and end apart: 17, of which 12 were waited for; matrix products, arithmetic and copies ran while one was open for 1% of the time, Pallas kernels for 14%

profile of v3, /device:TPU:0, one launch (start us, length us, event | category | flops | bytes accessed | tf_op | source)
XLA Modules:
  0.0 72.3 jit_solution(2863212044291368026)
XLA Ops:
  0.7 9.5 %warp.1 = (bf16[8,512,512]{2,1,0:T(8,128)(2,1)}, bf16[2,2,4,512,128]{4,3,2,1,0:T(8,128)(2,1)}, bf16[2,2,4,512,128]{4,3,2,1,0:T(8,128)(2,1)S(1)}) custom-call(s32[8]{0:T(128)} %patch_ref.3, bf16[8]{0:T(256)(128)(2,1)} %weight_hbm.1, bf16[8,512,512]{2,1,0:T(8,128)(2,1)} %images.1, bf16[8,512,512]{2,1,0:T(8,128)(2,1)} %rows.1, bf16[8,512,512]{2,1,0:T(8,128)(2,1)} %cols.1), custom_call_target="tpu_custom_call" | custom-call | flops 4294967296 | bytes 16777216 | tf_op jit(solution)/shard_map/warp/pallas_call | solution.py:180
  10.2 0.5 collective-permute-start
  11.2 2.6 %collective-permute-start.1 = (f32[1,3,512]{2,1,0:T(4,128)S(1)}, f32[1,3,512]{2,1,0:T(4,128)S(1)}, u32[]{:S(2)}, u32[]{:S(2)}) collective-permute-start(f32[1,3,512]{2,1,0:T(4,128)S(1)} %fusion), channel_id=1, source_target_pairs={{0,1},{1,0},{2,3},{3,2},{4,5},{5,4},{6,7},{7,6},{8,9},{9,8},{10,11... | collective-permute-start | bytes 18440 | tf_op jit(solution)/shard_map/ppermute | solution.py:47
  13.8 1.6 %collective-permute-done.1 = f32[1,3,512]{2,1,0:T(4,128)S(1)} collective-permute-done((f32[1,3,512]{2,1,0:T(4,128)S(1)}, f32[1,3,512]{2,1,0:T(4,128)S(1)}, u32[]{:S(2)}, u32[]{:S(2)}) %collective-permute-start.1) | collective-permute-done | bytes 6176 | tf_op jit(solution)/shard_map/ppermute | solution.py:47
  15.5 1.3 %fold.2 = bf16[2,4,512,128]{3,2,1,0:T(8,128)(2,1)S(1)} custom-call(s32[1]{0:T(128)} %bitcast.7.place_ref, bf16[2,2,4,512,128]{4,3,2,1,0:T(8,128)(2,1)S(1)} %get-tuple-element.35.kept, bf16[2,2,4,512,128]{4,3,2,1,0:T(8,128)(2,1)} %collective-permute-done.received), custom_call_target="tpu_custom_call" | custom-call | tf_op jit(solution)/shard_map/fold/pallas_call | solution.py:462
  16.8 2.3 %collective-permute-start.2 = (bf16[2,4,512,128]{3,2,1,0:T(8,128)(2,1)S(1)}, bf16[2,4,512,128]{3,2,1,0:T(8,128)(2,1)S(1)}, u32[]{:S(2)}, u32[]{:S(2)}) collective-permute-start(bf16[2,4,512,128]{3,2,1,0:T(8,128)(2,1)S(1)} %fold.2), channel_id=1, source_target_pairs={{0,16},{1,17},{2,18},{3,19},{4,20},{5,21},{6,22},{7,23},{8,9},{9,8... | collective-permute-start | bytes 3145736 | tf_op jit(solution)/shard_map/ppermute | solution.py:47
  19.2 1.6 %collective-permute-start.3 = (f32[2,3,512]{2,1,0:T(4,128)S(1)}, f32[2,3,512]{2,1,0:T(4,128)S(1)}, u32[]{:S(2)}, u32[]{:S(2)}) collective-permute-start(f32[2,3,512]{2,1,0:T(4,128)S(1)} %constant_dynamic-update-slice_fusion), channel_id=1, source_target_pairs={{0,2},{1,3},{2,0},{3,1},{4,6},{5,7},{6,4},{7,5},{8,10},{9,11},{10,... | collective-permute-start | bytes 36872 | tf_op jit(solution)/shard_map/ppermute | solution.py:47
  20.8 2.6 %collective-permute-start.4 = (f32[2,3,512]{2,1,0:T(4,128)S(1)}, f32[2,3,512]{2,1,0:T(4,128)S(1)}, u32[]{:S(2)}, u32[]{:S(2)}) collective-permute-start(f32[2,3,512]{2,1,0:T(4,128)S(1)} %constant_dynamic-update-slice_fusion), channel_id=1, source_target_pairs={{0,4},{1,5},{2,6},{3,7},{4,0},{5,1},{6,2},{7,3},{8,12},{9,13},{10,... | collective-permute-start | bytes 36872 | tf_op jit(solution)/shard_map/ppermute | solution.py:47
  23.6 1.3 %fold.3.kept = bf16[2,4,512,128]{3,2,1,0:T(8,128)(2,1)S(1)} custom-call(s32[1]{0:T(128)} %bitcast.3.place_ref, bf16[2,2,4,512,128]{4,3,2,1,0:T(8,128)(2,1)S(1)} %get-tuple-element.35.kept, bf16[2,2,4,512,128]{4,3,2,1,0:T(8,128)(2,1)} %collective-permute-done.received), custom_call_target="tpu_custom_call" | custom-call | tf_op jit(solution)/shard_map/fold/pallas_call | solution.py:462
  25.0 0.7 collective-permute-done.4
  25.7 3.2 %collective-permute-done.5 = f32[2,3,512]{2,1,0:T(4,128)S(1)} collective-permute-done((f32[2,3,512]{2,1,0:T(4,128)S(1)}, f32[2,3,512]{2,1,0:T(4,128)S(1)}, u32[]{:S(2)}, u32[]{:S(2)}) %collective-permute-start.5) | collective-permute-done | bytes 12320 | tf_op jit(solution)/shard_map/ppermute | solution.py:47
  29.0 6.2 %forced_flux.1 = (f32[8,1,512]{2,1,0:T(1,128)S(1)}, f32[32,512]{1,0:T(8,128)S(1)}) custom-call(s32[8]{0:T(128)S(1)} %copy-done, s32[8]{0:T(128)S(1)} %fusion.3.place_ref, bf16[8,512,512]{2,1,0:T(8,128)(2,1)} %get-tuple-element.40.warped, f32[8,1,512]{2,1,0:T(1,128)S(1)} %get-tuple-element.69.refs_0_.refs_1_, ...), custom_call_target="tpu_custom_call" | custom-call | flops 2147483648 | bytes 4194304 | tf_op jit(solution)/shard_map/forced_flux/pallas_call | solution.py:244
  35.5 1.6 %collective-permute-start.7 = (bf16[32,512]{1,0:T(8,128)(2,1)S(1)}, bf16[32,512]{1,0:T(8,128)(2,1)S(1)}, u32[]{:S(2)}, u32[]{:S(2)}) collective-permute-start(bf16[32,512]{1,0:T(8,128)(2,1)S(1)} %convert_element_type.52), channel_id=1, source_target_pairs={{0,1},{1,0},{2,3},{3,2},{4,5},{5,4},{6,7},{7,6},{8,9},{9,8},{10,11... | collective-permute-start | bytes 98312 | tf_op jit(solution)/shard_map/ppermute | solution.py:47
  37.1 0.5 collective-permute-start.6
  37.6 1.9 %collective-permute-done.7 = bf16[32,512]{1,0:T(8,128)(2,1)S(1)} collective-permute-done((bf16[32,512]{1,0:T(8,128)(2,1)S(1)}, bf16[32,512]{1,0:T(8,128)(2,1)S(1)}, u32[]{:S(2)}, u32[]{:S(2)}) %collective-permute-start.7) | collective-permute-done | bytes 32800 | tf_op jit(solution)/shard_map/ppermute | solution.py:47
  39.6 4.3 %collective-permute-done.8 = bf16[32,512]{1,0:T(8,128)(2,1)S(1)} collective-permute-done((bf16[32,512]{1,0:T(8,128)(2,1)S(1)}, bf16[32,512]{1,0:T(8,128)(2,1)S(1)}, u32[]{:S(2)}, u32[]{:S(2)}) %collective-permute-start.8) | collective-permute-done | bytes 32800 | tf_op jit(solution)/shard_map/ppermute | solution.py:47
  43.9 1.5 %prepare.1 = (bf16[512,512]{1,0:T(8,128)(2,1)S(1)}, bf16[512,512]{1,0:T(8,128)(2,1)S(1)}, f32[512,512]{1,0:T(8,128)S(1)}, bf16[128,512]{1,0:T(8,128)(2,1)S(1)}, bf16[128,512]{1,0:T(8,128)(2,1)S(1)}) custom-call(s32[1,512]{1,0:T(1,128)S(1)} %copy-done.1, s32[1,512]{1,0:T(1,128)S(1)} %copy-done.2, f32[512,512]{1,0:T(8,128)S(1)} %bitcast.16, ...), custom_call_target="tpu_custom_call" | custom-call | flops 1073741824 | bytes 5242880 | tf_op jit(solution)/shard_map/prepare/pallas_call | solution.py:292
  45.4 0.9 %collective-permute-done.6.received = bf16[4,512,128]{2,1,0:T(8,128)(2,1)S(1)} collective-permute-done((bf16[4,512,128]{2,1,0:T(8,128)(2,1)S(1)}, bf16[4,512,128]{2,1,0:T(8,128)(2,1)S(1)}, u32[]{:S(2)}, u32[]{:S(2)}) %collective-permute-start.6) | collective-permute-done | bytes 524320 | tf_op jit(solution)/shard_map/ppermute | solution.py:47
  46.6 2.0 %collective-permute-start.10 = (bf16[512,128]{1,0:T(8,128)(2,1)S(1)}, bf16[512,128]{1,0:T(8,128)(2,1)S(1)}, u32[]{:S(2)}, u32[]{:S(2)}) collective-permute-start(bf16[512,128]{1,0:T(8,128)(2,1)S(1)} %get-tuple-element.50), channel_id=1, source_target_pairs={{0,4},{1,5},{2,6},{3,7},{4,0},{5,1},{6,2},{7,3},{8,12},{9,13},{10,... | collective-permute-start | bytes 393224 | tf_op jit(solution)/shard_map/ppermute | solution.py:47
  48.6 2.3 %collective-permute-start.11 = (bf16[512,128]{1,0:T(8,128)(2,1)S(1)}, bf16[512,128]{1,0:T(8,128)(2,1)S(1)}, u32[]{:S(2)}, u32[]{:S(2)}) collective-permute-start(bf16[512,128]{1,0:T(8,128)(2,1)S(1)} %get-tuple-element.51), channel_id=1, source_target_pairs={{0,6},{1,7},{2,4},{3,5},{4,2},{5,3},{6,0},{7,1},{8,14},{9,15},{10,... | collective-permute-start | bytes 393224 | tf_op jit(solution)/shard_map/ppermute | solution.py:47
  50.8 1.0 %collective-permute-done.15 = bf16[32,512]{1,0:T(8,128)(2,1)S(1)} collective-permute-done((bf16[32,512]{1,0:T(8,128)(2,1)S(1)}, bf16[32,512]{1,0:T(8,128)(2,1)S(1)}, u32[]{:S(2)}, u32[]{:S(2)}) %collective-permute-start.15) | collective-permute-done | bytes 32800 | tf_op jit(solution)/shard_map/ppermute | solution.py:47
  51.9 1.6 %collective-permute-done.9.refs_1_ = bf16[512,128]{1,0:T(8,128)(2,1)S(1)} collective-permute-done((bf16[512,128]{1,0:T(8,128)(2,1)S(1)}, bf16[512,128]{1,0:T(8,128)(2,1)S(1)}, u32[]{:S(2)}, u32[]{:S(2)}) %collective-permute-start.9) | collective-permute-done | bytes 131104 | tf_op jit(solution)/shard_map/ppermute | solution.py:47
  53.5 3.6 %collective-permute-done.10.refs_2_ = bf16[512,128]{1,0:T(8,128)(2,1)S(1)} collective-permute-done((bf16[512,128]{1,0:T(8,128)(2,1)S(1)}, bf16[512,128]{1,0:T(8,128)(2,1)S(1)}, u32[]{:S(2)}, u32[]{:S(2)}) %collective-permute-start.10) | collective-permute-done | bytes 131104 | tf_op jit(solution)/shard_map/ppermute | solution.py:47
  57.1 1.6 %match.1 = (bf16[144,128]{1,0:T(8,128)(2,1)S(1)}, bf16[144,128]{1,0:T(8,128)(2,1)S(1)}, bf16[144,128]{1,0:T(8,128)(2,1)S(1)}, bf16[144,128]{1,0:T(8,128)(2,1)S(1)}, f32[32,8,128]{2,1,0:T(8,128)}) custom-call(bf16[512,128]{1,0:T(8,128)(2,1)S(1)} %get-tuple-element.48.refs_0_, bf16[512,128]{1,0:T(8,128)(2,1)S(1)} %collective-permute-done.9.refs_1_, ...), custom_call_target="tpu_custom_call" | custom-call | flops 402653184 | bytes 2621440 | tf_op jit(solution)/shard_map/match/pallas_call | solution.py:342
  58.8 4.3 %all-to-all-start = ((f32[32,8,128]{2,1,0:T(8,128)}), f32[32,8,128]{2,1,0:T(8,128)S(1)}, u32[]{:S(2)}, u32[]{:S(2)}) async-start(f32[32,8,128]{2,1,0:T(8,128)} %get-tuple-element.64), calls=%async_computation | async-start | bytes 262144 | tf_op jit(solution)/shard_map/all_to_all | solution.py:565
  63.1 0.3 collective-permute-start.12
  63.4 1.7 %collective-permute-start.13 = (bf16[144,128]{1,0:T(8,128)(2,1)S(1)}, bf16[144,128]{1,0:T(8,128)(2,1)S(1)}, u32[]{:S(2)}, u32[]{:S(2)}) collective-permute-start(bf16[144,128]{1,0:T(8,128)(2,1)S(1)} %get-tuple-element.60), channel_id=1, source_target_pairs={{0,16},{1,17},{2,18},{3,19},{4,20},{5,21},{6,22},{7,23},{8,24},{9,... | collective-permute-start | bytes 110600 | tf_op jit(solution)/shard_map/ppermute | solution.py:47
  65.1 2.4 %collective-permute-done.13.refs_2_ = bf16[144,128]{1,0:T(8,128)(2,1)S(1)} collective-permute-done((bf16[144,128]{1,0:T(8,128)(2,1)S(1)}, bf16[144,128]{1,0:T(8,128)(2,1)S(1)}, u32[]{:S(2)}, u32[]{:S(2)}) %collective-permute-start.13) | collective-permute-done | bytes 36896 | tf_op jit(solution)/shard_map/ppermute | solution.py:47
  67.5 1.2 %collective-permute-done.14.refs_3_ = bf16[144,128]{1,0:T(8,128)(2,1)S(1)} collective-permute-done((bf16[144,128]{1,0:T(8,128)(2,1)S(1)}, bf16[144,128]{1,0:T(8,128)(2,1)S(1)}, u32[]{:S(2)}, u32[]{:S(2)}) %collective-permute-start.14) | collective-permute-done | bytes 36896 | tf_op jit(solution)/shard_map/ppermute | solution.py:47
  68.7 1.2 %coadd_rows.1 = f32[128,512]{1,0:T(8,128)} custom-call(f32[512,512]{1,0:T(8,128)S(1)} %bitcast.18, bf16[144,128]{1,0:T(8,128)(2,1)S(1)} %get-tuple-element.58.refs_0_, bf16[144,128]{1,0:T(8,128)(2,1)S(1)} %collective-permute-done.12.refs_1_, bf16[144,128]{1,0:T(8,128)(2,1)S(1)} %collective-permute-done.13.refs_2_, ...), custom_call_target="tpu_custom_call" | custom-call | flops 402653184 | bytes 1572864 | tf_op jit(solution)/shard_map/coadd_rows/pallas_call | solution.py:381
  69.9 0.9 %all-to-all-done.messages = f32[32,8,128]{2,1,0:T(8,128)S(1)} async-done(((f32[32,8,128]{2,1,0:T(8,128)}), f32[32,8,128]{2,1,0:T(8,128)S(1)}, u32[]{:S(2)}, u32[]{:S(2)}) %all-to-all-start) | async-done | bytes 131104 | tf_op jit(solution)/shard_map/all_to_all | solution.py:565
  70.8 1.5 %finish.1 = (f32[1,4]{1,0:T(1,128)}, f32[8,512]{1,0:T(8,128)}) custom-call(s32[8]{0:T(128)S(1)} %copy-done, f32[1,512]{1,0:T(1,128)S(1)} %bitcast.15, f32[8,1,512]{2,1,0:T(1,128)S(1)} %get-tuple-element.62.flux, f32[8,4,512]{2,1,0:T(4,128)S(1)} %reshape.50.sums, f32[32,8,128]{2,1,0:T(8,128)S(1)} %all-to-all-done.messages), custom_call_target="tpu_custom_call" | custom-call | tf_op jit(solution)/shard_map/finish/pallas_call | solution.py:420
  (47 shorter events, 1.6 us)
Async XLA Ops:
  0.6 10.1 %copy-start = (s32[8]{0:T(128)S(1)}, s32[8]{0:T(128)}, u32[]{:S(2)}) copy-start(s32[8]{0:T(128)} %patch_ref.3) | copy-start | bytes 100
  0.6 10.1 %copy-start.5 = (bf16[8]{0:T(256)(128)(2,1)S(1)}, bf16[8]{0:T(256)(128)(2,1)}, u32[]{:S(2)}) copy-start(bf16[8]{0:T(256)(128)(2,1)} %weight_hbm.1) | copy-start | bytes 52
  0.7 10.5 %copy-start.2 = (s32[1,512]{1,0:T(1,128)S(1)}, s32[1,512]{1,0:T(1,128)}, u32[]{:S(2)}) copy-start(s32[1,512]{1,0:T(1,128)} %src_col.1) | copy-start | bytes 6148
  0.7 10.5 %copy-start.1 = (s32[1,512]{1,0:T(1,128)S(1)}, s32[1,512]{1,0:T(1,128)}, u32[]{:S(2)}) copy-start(s32[1,512]{1,0:T(1,128)} %src_row) | copy-start | bytes 6148
  10.2 5.3 %collective-permute-start = (bf16[2,2,4,512,128]{4,3,2,1,0:T(8,128)(2,1)}, bf16[2,2,4,512,128]{4,3,2,1,0:T(8,128)(2,1)}, u32[]{:S(2)}, u32[]{:S(2)}) collective-permute-start(bf16[2,2,4,512,128]{4,3,2,1,0:T(8,128)(2,1)} %get-tuple-element.36), channel_id=1, source_target_pairs={{0,8},{1,9},{2,10},{3,11},{4,12},{5,13},{6,14},{7,15},{8,0},{9,1},... | collective-permute-start | bytes 6291464 | tf_op jit(solution)/shard_map/ppermute | solution.py:47
  11.2 4.2 %collective-permute-start.1 = (f32[1,3,512]{2,1,0:T(4,128)S(1)}, f32[1,3,512]{2,1,0:T(4,128)S(1)}, u32[]{:S(2)}, u32[]{:S(2)}) collective-permute-start(f32[1,3,512]{2,1,0:T(4,128)S(1)} %fusion), channel_id=1, source_target_pairs={{0,1},{1,0},{2,3},{3,2},{4,5},{5,4},{6,7},{7,6},{8,9},{9,8},{10,11... | collective-permute-start | bytes 18440 | tf_op jit(solution)/shard_map/ppermute | solution.py:47
  16.8 18.4 %collective-permute-start.2 = (bf16[2,4,512,128]{3,2,1,0:T(8,128)(2,1)S(1)}, bf16[2,4,512,128]{3,2,1,0:T(8,128)(2,1)S(1)}, u32[]{:S(2)}, u32[]{:S(2)}) collective-permute-start(bf16[2,4,512,128]{3,2,1,0:T(8,128)(2,1)S(1)} %fold.2), channel_id=1, source_target_pairs={{0,16},{1,17},{2,18},{3,19},{4,20},{5,21},{6,22},{7,23},{8,9},{9,8... | collective-permute-start | bytes 3145736 | tf_op jit(solution)/shard_map/ppermute | solution.py:47
  19.2 5.8 %collective-permute-start.3 = (f32[2,3,512]{2,1,0:T(4,128)S(1)}, f32[2,3,512]{2,1,0:T(4,128)S(1)}, u32[]{:S(2)}, u32[]{:S(2)}) collective-permute-start(f32[2,3,512]{2,1,0:T(4,128)S(1)} %constant_dynamic-update-slice_fusion), channel_id=1, source_target_pairs={{0,2},{1,3},{2,0},{3,1},{4,6},{5,7},{6,4},{7,5},{8,10},{9,11},{10,... | collective-permute-start | bytes 36872 | tf_op jit(solution)/shard_map/ppermute | solution.py:47
  20.8 4.9 %collective-permute-start.4 = (f32[2,3,512]{2,1,0:T(4,128)S(1)}, f32[2,3,512]{2,1,0:T(4,128)S(1)}, u32[]{:S(2)}, u32[]{:S(2)}) collective-permute-start(f32[2,3,512]{2,1,0:T(4,128)S(1)} %constant_dynamic-update-slice_fusion), channel_id=1, source_target_pairs={{0,4},{1,5},{2,6},{3,7},{4,0},{5,1},{6,2},{7,3},{8,12},{9,13},{10,... | collective-permute-start | bytes 36872 | tf_op jit(solution)/shard_map/ppermute | solution.py:47
  23.4 5.5 %collective-permute-start.5 = (f32[2,3,512]{2,1,0:T(4,128)S(1)}, f32[2,3,512]{2,1,0:T(4,128)S(1)}, u32[]{:S(2)}, u32[]{:S(2)}) collective-permute-start(f32[2,3,512]{2,1,0:T(4,128)S(1)} %constant_dynamic-update-slice_fusion), channel_id=1, source_target_pairs={{0,6},{1,7},{2,4},{3,5},{4,2},{5,3},{6,0},{7,1},{8,14},{9,15},{10,... | collective-permute-start | bytes 36872 | tf_op jit(solution)/shard_map/ppermute | solution.py:47
  29.0 14.9 %copy-start.3 = (f32[1,512,512]{2,1,0:T(8,128)S(1)}, f32[1,512,512]{2,1,0:T(8,128)}, u32[]{:S(2)}) copy-start(f32[1,512,512]{2,1,0:T(8,128)} %param.14) | copy-start | bytes 3145732
  29.0 14.9 %copy-start.4 = (f32[1,512,512]{2,1,0:T(8,128)S(1)}, f32[1,512,512]{2,1,0:T(8,128)}, u32[]{:S(2)}) copy-start(f32[1,512,512]{2,1,0:T(8,128)} %param.15) | copy-start | bytes 3145732
  35.5 4.0 %collective-permute-start.7 = (bf16[32,512]{1,0:T(8,128)(2,1)S(1)}, bf16[32,512]{1,0:T(8,128)(2,1)S(1)}, u32[]{:S(2)}, u32[]{:S(2)}) collective-permute-start(bf16[32,512]{1,0:T(8,128)(2,1)S(1)} %convert_element_type.52), channel_id=1, source_target_pairs={{0,1},{1,0},{2,3},{3,2},{4,5},{5,4},{6,7},{7,6},{8,9},{9,8},{10,11... | collective-permute-start | bytes 98312 | tf_op jit(solution)/shard_map/ppermute | solution.py:47
  37.1 9.2 %collective-permute-start.6 = (bf16[4,512,128]{2,1,0:T(8,128)(2,1)S(1)}, bf16[4,512,128]{2,1,0:T(8,128)(2,1)S(1)}, u32[]{:S(2)}, u32[]{:S(2)}) collective-permute-start(bf16[4,512,128]{2,1,0:T(8,128)(2,1)S(1)} %get-tuple-element.45), channel_id=1, source_target_pairs={{0,1},{1,0},{2,3},{3,2},{4,5},{5,4},{6,7},{7,6},{8,24},{9,25},{10,... | collective-permute-start | bytes 1572872 | tf_op jit(solution)/shard_map/ppermute | solution.py:47
  39.5 4.3 %collective-permute-start.8 = (bf16[32,512]{1,0:T(8,128)(2,1)S(1)}, bf16[32,512]{1,0:T(8,128)(2,1)S(1)}, u32[]{:S(2)}, u32[]{:S(2)}) collective-permute-start(bf16[32,512]{1,0:T(8,128)(2,1)S(1)} %add_convert_fusion.2), channel_id=1, source_target_pairs={{0,2},{1,3},{2,0},{3,1},{4,6},{5,7},{6,4},{7,5},{8,10},{9,11},{10,... | collective-permute-start | bytes 98312 | tf_op jit(solution)/shard_map/ppermute | solution.py:47
  43.8 8.0 %collective-permute-start.15 = (bf16[32,512]{1,0:T(8,128)(2,1)S(1)}, bf16[32,512]{1,0:T(8,128)(2,1)S(1)}, u32[]{:S(2)}, u32[]{:S(2)}) collective-permute-start(bf16[32,512]{1,0:T(8,128)(2,1)S(1)} %add_convert_fusion.1), channel_id=1, source_target_pairs={{0,4},{1,5},{2,6},{3,7},{4,0},{5,1},{6,2},{7,3},{8,12},{9,13},{10,... | collective-permute-start | bytes 98312 | tf_op jit(solution)/shard_map/ppermute | solution.py:47
  46.4 7.1 %collective-permute-start.9 = (bf16[512,128]{1,0:T(8,128)(2,1)S(1)}, bf16[512,128]{1,0:T(8,128)(2,1)S(1)}, u32[]{:S(2)}, u32[]{:S(2)}) collective-permute-start(bf16[512,128]{1,0:T(8,128)(2,1)S(1)} %get-tuple-element.49), channel_id=1, source_target_pairs={{0,2},{1,3},{2,0},{3,1},{4,6},{5,7},{6,4},{7,5},{8,10},{9,11},{10,... | collective-permute-start | bytes 393224 | tf_op jit(solution)/shard_map/ppermute | solution.py:47
  46.6 10.5 %collective-permute-start.10 = (bf16[512,128]{1,0:T(8,128)(2,1)S(1)}, bf16[512,128]{1,0:T(8,128)(2,1)S(1)}, u32[]{:S(2)}, u32[]{:S(2)}) collective-permute-start(bf16[512,128]{1,0:T(8,128)(2,1)S(1)} %get-tuple-element.50), channel_id=1, source_target_pairs={{0,4},{1,5},{2,6},{3,7},{4,0},{5,1},{6,2},{7,3},{8,12},{9,13},{10,... | collective-permute-start | bytes 393224 | tf_op jit(solution)/shard_map/ppermute | solution.py:47
  48.6 8.6 %collective-permute-start.11 = (bf16[512,128]{1,0:T(8,128)(2,1)S(1)}, bf16[512,128]{1,0:T(8,128)(2,1)S(1)}, u32[]{:S(2)}, u32[]{:S(2)}) collective-permute-start(bf16[512,128]{1,0:T(8,128)(2,1)S(1)} %get-tuple-element.51), channel_id=1, source_target_pairs={{0,6},{1,7},{2,4},{3,5},{4,2},{5,3},{6,0},{7,1},{8,14},{9,15},{10,... | collective-permute-start | bytes 393224 | tf_op jit(solution)/shard_map/ppermute | solution.py:47
  58.8 12.1 %all-to-all-start = ((f32[32,8,128]{2,1,0:T(8,128)}), f32[32,8,128]{2,1,0:T(8,128)S(1)}, u32[]{:S(2)}, u32[]{:S(2)}) async-start(f32[32,8,128]{2,1,0:T(8,128)} %get-tuple-element.64), calls=%async_computation | async-start | bytes 262144 | tf_op jit(solution)/shard_map/all_to_all | solution.py:565
  63.1 2.0 %collective-permute-start.12 = (bf16[144,128]{1,0:T(8,128)(2,1)S(1)}, bf16[144,128]{1,0:T(8,128)(2,1)S(1)}, u32[]{:S(2)}, u32[]{:S(2)}) collective-permute-start(bf16[144,128]{1,0:T(8,128)(2,1)S(1)} %get-tuple-element.59), channel_id=1, source_target_pairs={{0,8},{1,9},{2,10},{3,11},{4,12},{5,13},{6,14},{7,15},{8,0},{9,1},... | collective-permute-start | bytes 110600 | tf_op jit(solution)/shard_map/ppermute | solution.py:47
  63.4 4.1 %collective-permute-start.13 = (bf16[144,128]{1,0:T(8,128)(2,1)S(1)}, bf16[144,128]{1,0:T(8,128)(2,1)S(1)}, u32[]{:S(2)}, u32[]{:S(2)}) collective-permute-start(bf16[144,128]{1,0:T(8,128)(2,1)S(1)} %get-tuple-element.60), channel_id=1, source_target_pairs={{0,16},{1,17},{2,18},{3,19},{4,20},{5,21},{6,22},{7,23},{8,24},{9,... | collective-permute-start | bytes 110600 | tf_op jit(solution)/shard_map/ppermute | solution.py:47
  65.1 3.6 %collective-permute-start.14 = (bf16[144,128]{1,0:T(8,128)(2,1)S(1)}, bf16[144,128]{1,0:T(8,128)(2,1)S(1)}, u32[]{:S(2)}, u32[]{:S(2)}) collective-permute-start(bf16[144,128]{1,0:T(8,128)(2,1)S(1)} %get-tuple-element.61), channel_id=1, source_target_pairs={{0,24},{1,25},{2,26},{3,27},{4,28},{5,29},{6,30},{7,31},{8,16},{9,... | collective-permute-start | bytes 110600 | tf_op jit(solution)/shard_map/ppermute | solution.py:47

commit v4 on v3

--- a/solution.py
+++ b/solution.py
@@ -21,6 +21,7 @@
 PAIR = 2
 IN_VMEM = pl.BlockSpec(memory_space=pltpu.VMEM)
 NT = (((1,), (1,)), ((), ()))
+NN = (((1,), (0,)), ((), ()))
 TN = (((0,), (0,)), ((), ()))
 
 
@@ -215,50 +216,52 @@
     return jnp.exp2(distance * distance * EXPONENT).astype(BF16)
 
 
-def flux_kernel(lay, patch_ref, place_ref, warped, *refs):
+def flux_kernel(lay, begin, patch_ref, place_ref, warped, *refs):
     step = pl.program_id(0)
-    sources, (flux, sums) = refs[: 2 * PAIR], refs[2 * PAIR :]
+    sources, (earlier, flux, sums) = refs[: 2 * PAIR], refs[2 * PAIR :]
 
     @pl.when(step == 0)
     def _():
-        sums[...] = jnp.zeros_like(sums)
+        sums[...] = earlier[...]
 
     position = lax.broadcasted_iota(jnp.int32, (lay.side, lay.side), 0).astype(F32)
     for local in range(PAIR):
-        tile = step * PAIR + local
+        tile = begin + step * PAIR + local
         row_prof = profile(position, sources[local][0])
         col_prof = profile(position, sources[PAIR + local][0])
         by_column = jnp.dot(warped[local], col_prof, preferred_element_type=F32)
         value = jnp.sum(by_column * row_prof.astype(F32), axis=0, keepdims=True)
-        flux[tile] = value
+        flux[step * PAIR + local] = value
         spot = patch_ref[tile] * VIS_ROW + tile % VIS_ROW
         sums[pl.ds(spot, 1), :] += value
 
 
-def forced_flux(lay, tile_patch, tile_place, warped, src_row, src_col):
-    tiles, side = lay.tiles, lay.side
+def forced_flux(lay, begin, end, tile_patch, tile_place, warped, src_row, src_col, earlier):
+    count, side = end - begin, lay.side
     sources = [
-        pl.BlockSpec((1, 1, side), lambda step, patch, place, local=local: (place[step * PAIR + local], 0, 0))
+        pl.BlockSpec((1, 1, side), lambda step, patch, place, at=begin + local: (place[step * PAIR + at], 0, 0))
         for local in range(PAIR)
     ]
     return pl.pallas_call(
-        functools.partial(flux_kernel, lay),
+        functools.partial(flux_kernel, lay, begin),
         grid_spec=pltpu.PrefetchScalarGridSpec(
             num_scalar_prefetch=2,
-            grid=(tiles // PAIR,),
-            in_specs=[pl.BlockSpec((PAIR, side, side), lambda step, *_: (step, 0, 0))] + sources * 2,
+            grid=(count // PAIR,),
+            in_specs=[pl.BlockSpec((PAIR, side, side), lambda step, *_: (step + begin // PAIR, 0, 0))]
+            + sources * 2
+            + [IN_VMEM],
             out_specs=[IN_VMEM, IN_VMEM],
         ),
         out_shape=[
-            jax.ShapeDtypeStruct((tiles, 1, side), F32),
+            jax.ShapeDtypeStruct((count, 1, side), F32),
             jax.ShapeDtypeStruct((VIS_ROW * lay.patches, side), F32),
         ],
         compiler_params=pltpu.CompilerParams(vmem_limit_bytes=VMEM_LIMIT),
         cost_estimate=pl.CostEstimate(
-            flops=2 * tiles * side**3, bytes_accessed=2 * tiles * side * side, transcendentals=2 * tiles * side * side
+            flops=2 * count * side**3, bytes_accessed=2 * count * side * side, transcendentals=2 * count * side * side
         ),
         name="forced_flux",
-    )(tile_patch, tile_place, in_hbm(warped), *([src_row] * PAIR + [src_col] * PAIR))
+    )(tile_patch, tile_place, in_hbm(warped), *([src_row] * PAIR + [src_col] * PAIR), earlier)
 
 
 def split(array):
@@ -303,34 +306,41 @@
     )(src_row, src_col, match_rows, match_cols)
 
 
-def match_kernel(lay, extra, *refs):
+def own_weight(lay, table):
+    lane = lax.broadcasted_iota(jnp.int32, table.shape, 1)
+    return jnp.sum(jnp.where(lane == lax.axis_index("patch") * 8 + VIS_ROW, table[...], 0.0), keepdims=True)
+
+
+def stacked_columns(lay, pieces):
+    parts = [
+        sum(piece[...].astype(F32) for piece in pieces[part * lay.highs : (part + 1) * lay.highs])
+        for part in range(PARTS)
+    ]
+    return split(jnp.concatenate(parts, axis=0))
+
+
+def share_kernel(lay, extra, *refs):
+    pieces, (row_flux, col_up, col_low, table, shares) = refs[:-5], refs[-5:]
     width, visits = lay.width, lay.visits
-    pieces, refs = refs[: PARTS * lay.highs], refs[PARTS * lay.highs :]
-    (rows_up, rows_low, row_flux, col_up, col_low, table), refs = refs[:6], refs[6:]
-    messages, (spread, matched) = refs[:visits], refs[visits:]
-    visit, patch = lax.axis_index("visit"), lax.axis_index("patch")
-    stacked = jnp.concatenate(
-        [
-            sum(piece[...].astype(F32) for piece in pieces[part * lay.highs : (part + 1) * lay.highs])
-            for part in range(PARTS)
-        ],
+    stacked = stacked_columns(lay, pieces)
+    by_source = dot3(stacked, (col_up[...], col_low[...]), NN)
+    flux = jnp.sum(by_source * row_flux[...], axis=0, keepdims=True)
+    tail = jnp.concatenate(
+        [flux[:, block * width : (block + 1) * width] for block in range(visits)]
+        + [jnp.broadcast_to(own_weight(lay, table), (extra - visits, width))],
         axis=0,
     )
-    stacked = split(stacked)
-    nn = (((1,), (0,)), ((), ()))
-    result = dot3((rows_up[...], rows_low[...]), stacked, nn)
+    shares[...] = jnp.broadcast_to(tail[None], shares.shape)
+
+
+def match_kernel(lay, *refs):
+    width, visits = lay.width, lay.visits
+    pieces, (rows_up, rows_low, table), refs = refs[: PARTS * lay.highs], refs[-visits - 4 : -visits - 1], refs[-visits - 1 :]
+    messages, matched = refs[:-1], refs[-1]
+    visit = lax.axis_index("visit")
+    result = dot3((rows_up[...], rows_low[...]), stacked_columns(lay, pieces), NN)
     matched[...] = result.reshape(visits, width, width)
-    by_source = dot3(stacked, (col_up[...], col_low[...]), nn)
-    flux = jnp.sum(by_source * row_flux[...], axis=0, keepdims=True)
-    lane = lax.broadcasted_iota(jnp.int32, table.shape, 1)
-    weight = jnp.sum(jnp.where(lane == patch * 8 + VIS_ROW, table[...], 0.0), keepdims=True)
-    tail = jnp.concatenate(
-        [flux[:, block * width : (block + 1) * width] for block in range(visits)]
-        + [jnp.broadcast_to(weight, (extra - visits, width))],
-        axis=0,
-    )
-    spread[...] = jnp.broadcast_to(tail[None], spread.shape)
-    upper, lower = split(jnp.broadcast_to(weight, (8, width)))
+    upper, lower = split(jnp.broadcast_to(own_weight(lay, table), (8, width)))
     weight = jnp.concatenate([upper, lower], axis=0)
     for step, message in enumerate(messages):
         message[:width] = matched[visit ^ step].astype(BF16)
@@ -339,20 +349,29 @@
 
 def match(lay, extra, pieces, prepared, table):
     side, width = lay.side, lay.width
-    out = pl.pallas_call(
-        functools.partial(match_kernel, lay, extra),
-        in_specs=[IN_VMEM] * (len(pieces) + len(prepared) + 1),
-        out_specs=[IN_VMEM] * (lay.visits + 1),
-        out_shape=[pltpu.VMEM((width + 16, width), BF16)] * lay.visits
-        + [jax.ShapeDtypeStruct((lay.visits * lay.patches, extra, width), F32)],
+    rows_up, rows_low, row_flux, col_up, col_low = prepared
+    params = pltpu.CompilerParams(vmem_limit_bytes=VMEM_LIMIT)
+    cost = pl.CostEstimate(flops=6 * width * side * side, bytes_accessed=5 * side * side, transcendentals=0)
+    shares = pl.pallas_call(
+        functools.partial(share_kernel, lay, extra),
+        in_specs=[IN_VMEM] * (len(pieces) + 4),
+        out_specs=IN_VMEM,
+        out_shape=jax.ShapeDtypeStruct((lay.visits * lay.patches, extra, width), F32),
+        compiler_params=params,
+        cost_estimate=cost,
+        name="share",
+    )(*pieces, row_flux, col_up, col_low, table)
+    messages = pl.pallas_call(
+        functools.partial(match_kernel, lay),
+        in_specs=[IN_VMEM] * (len(pieces) + 3),
+        out_specs=[IN_VMEM] * lay.visits,
+        out_shape=[pltpu.VMEM((width + 16, width), BF16)] * lay.visits,
         scratch_shapes=[pltpu.VMEM((lay.visits, width, width), F32)],
-        compiler_params=pltpu.CompilerParams(vmem_limit_bytes=VMEM_LIMIT),
-        cost_estimate=pl.CostEstimate(
-            flops=12 * width * side * side, bytes_accessed=10 * side * side, transcendentals=0
-        ),
+        compiler_params=params,
+        cost_estimate=cost,
         name="match",
-    )(*pieces, *prepared, table)
-    return out[: lay.visits], out[lay.visits]
+    )(*pieces, rows_up, rows_low, after(table, shares))
+    return messages, shares
 
 
 def coadd_kernel(lay, match_cols, *refs):
@@ -389,7 +408,7 @@
     )(match_cols, *parts)
 
 
-def finish_kernel(lay, patch_ref, table, flux, sums, messages, zero, resid, lines):
+def finish_kernel(lay, patch_ref, table, flux_a, flux_b, sums, messages, zero, resid, lines):
     visits, patches = lay.visits, lay.patches
     for patch in range(patches):
         data = sum(messages[visit * patches + patch] for visit in range(visits))
@@ -413,13 +432,14 @@
     for tile in range(lay.tiles):
         own = lines[pl.ds(patch_ref[tile], 1), :]
         visit = tile % VIS_ROW
-        resid[tile : tile + 1, :] = flux[tile] - scales[:, visit : visit + 1] * own
-
-
-def finish(lay, tile_patch, table, flux, sums, messages):
+        flux = flux_a[tile] if tile < flux_a.shape[0] else flux_b[tile - flux_a.shape[0]]
+        resid[tile : tile + 1, :] = flux - scales[:, visit : visit + 1] * own
+
+
+def finish(lay, tile_patch, table, flux_a, flux_b, sums, messages):
     return pl.pallas_call(
         functools.partial(finish_kernel, lay),
-        in_specs=[pl.BlockSpec(memory_space=pltpu.SMEM)] + [IN_VMEM] * 4,
+        in_specs=[pl.BlockSpec(memory_space=pltpu.SMEM)] + [IN_VMEM] * 5,
         out_specs=[IN_VMEM, IN_VMEM],
         out_shape=[
             jax.ShapeDtypeStruct((1, VIS_ROW), F32),
@@ -428,7 +448,7 @@
         scratch_shapes=[pltpu.VMEM((lay.patches, lay.side), F32)],
         compiler_params=pltpu.CompilerParams(vmem_limit_bytes=VMEM_LIMIT),
         name="finish",
-    )(tile_patch, table, flux, sums, messages)
+    )(tile_patch, table, flux_a, flux_b, sums, messages)
 
 
 def spread_kernel(count, place_ref, kept, received, own, *sends):
@@ -512,15 +532,12 @@
     return jnp.concatenate([near] + [lay.swap_high(near, step) for step in range(1, lay.highs)])
 
 
-def sum_steps(lay, array):
-    steps = []
-    for size, swap in ((lay.group, lay.swap_low), (lay.highs, lay.swap_high)):
-        step = 1
-        while step < size:
-            array = (array.astype(F32) + swap(array, step).astype(F32)).astype(array.dtype)
-            steps.append(array)
-            step *= 2
-    return steps
+def add_wide(left, right):
+    return (left.astype(F32) + right.astype(F32)).astype(left.dtype)
+
+
+def swaps_of(swap, size):
+    return [functools.partial(swap, step=1 << bit) for bit in range(size.bit_length() - 1)]
 
 
 def shards(
@@ -548,24 +565,35 @@
     all_rows, all_cols = gathered[:, 0:1, :], gathered[:, 1:2, :]
     table = jnp.sum(gathered[:, 2:3, :], axis=0)
     tile_place = ((tile_patch // lay.group) ^ high) * lay.group + ((tile_patch % lay.group) ^ low)
-    flux, sums = forced_flux(lay, tile_patch, tile_place, warped, all_rows, all_cols)
+    middle = tiles * 6 // 8 // PAIR * PAIR
+    targets = (tile_patch, tile_place, warped, all_rows, all_cols)
+    sums = jnp.zeros((VIS_ROW * patches, side), F32)
+    flux_a, sums = forced_flux(lay, 0, middle, *targets, sums)
 
     for stream in streams:
         stream.step(sums)
-    steps = sum_steps(lay, after(sums.astype(BF16), streams[-1].own))
-    prepared = prepare(lay, after(src_row, steps[1]), src_col, match_rows[0], match_cols[0])
+    sums = after(sums, streams[-1].own)
+    flux_b, sums = forced_flux(lay, middle, tiles, *targets, sums)
+    sums = sums.astype(BF16)
+    swaps = swaps_of(lay.swap_high, lay.highs) + swaps_of(lay.swap_low, lay.group)
+    sums = add_wide(sums, swaps[0](sums))
+    received = swaps[1](sums)
     for stream in streams:
-        stream.step(steps[1])
+        stream.step(sums)
+    sums = add_wide(sums, after(received, streams[-1].own))
+    for swap in swaps[2:]:
+        sums = add_wide(sums, swap(sums))
+    prepared = prepare(lay, after(src_row, streams[-1].own), src_col, match_rows[0], match_cols[0])
 
     extra = -(-(lay.visits + 1) // 8) * 8
     pieces = [piece for stream in streams for piece in stream.pieces()]
     messages, fluxes = match(lay, extra, pieces, prepared, table)
     parts = [messages[0]] + [lay.swap_visit(messages[step], step) for step in range(1, lay.visits)]
-    fluxes = after(fluxes, steps[-1])
+    fluxes = after(fluxes, sums)
     fluxes = lax.all_to_all(fluxes, AXES, 0, 0, tiled=True)
     coadd = coadd_rows(lay, match_cols[0], parts)
-    sums = steps[-1].astype(F32).reshape(patches, VIS_ROW, side)
-    zero, resid = finish(lay, tile_patch, table, flux, sums, fluxes)
+    sums = sums.astype(F32).reshape(patches, VIS_ROW, side)
+    zero, resid = finish(lay, tile_patch, table, flux_a, flux_b, sums, fluxes)
     return (coadd[None], zero.reshape(-1), resid)
 
 

time: 72.6 us -> 72 us (level)
  waiting for transfers between devices: 23.4 us -> 19.7 us
  Pallas kernels: 24.5 us -> 26.4 us
  starting transfers between devices: 22.9 us -> 24 us
    ppermute x16, waiting for transfers between devices: 22.5 us -> 19.7 us  [permute(): return lax.ppermute(array, AXES, pairs)]
    pallas_call x2 -> x4, Pallas kernels: 7.81 us -> 9.69 us  [the longest x2 7.82 us: forced_flux(): pl.pallas_call(functools.partial(flux_kernel, lay, begin), grid_spec=pltp...]
    all_to_all x1, waiting for transfers between devices: 0.93 us -> 0.01 us  [shards(): fluxes = lax.all_to_all(fluxes, AXES, 0, 0, tiled=True)]
  transfers between devices with their start and end apart: 17 -> 17, of which waited for: 12 -> 9; matrix products, arithmetic and copies ran while one was open for 1% -> 1% of each run, Pallas kernels for 14% -> 18%
where the time goes in v4:
time: 72 us; the launch traced here: 71.7 us
  Pallas kernels  26.4 us (37%)
  starting transfers between devices  24 us (33%)
  waiting for transfers between devices  19.7 us (27%)
  between operations  0.89 us (1%)
    ppermute x16, waiting for transfers between devices, permute(): return lax.ppermute(array, AXES, pairs)  19.7 us
    ppermute x16, starting transfers between devices, permute(): return lax.ppermute(array, AXES, pairs)  19.1 us
    pallas_call x1, Pallas kernels, warp(): pl.pallas_call(functools.partial(warp_kernel, lay), in_specs=[in_any] * 5...  9.55 us
    pallas_call x2, Pallas kernels, forced_flux(): pl.pallas_call(functools.partial(flux_kernel, lay, begin), grid_spec=pltp...  7.82 us
    all_to_all x1, starting transfers between devices, shards(): fluxes = lax.all_to_all(fluxes, AXES, 0, 0, tiled=True)  4.93 us
    pallas_call x2, Pallas kernels, fold(): pl.pallas_call(fold_kernel, grid_spec=pltpu.PrefetchScalarGridSpec(num_sc...  2.69 us
    pallas_call x1, Pallas kernels, prepare(): pl.pallas_call(functools.partial(prepare_kernel, lay), in_specs=[IN_VMEM]...  1.46 us
    pallas_call x1, Pallas kernels, finish(): pl.pallas_call(functools.partial(finish_kernel, lay), in_specs=[pl.BlockS...  1.45 us
  transfers between devices with their start and end apart: 17, of which 9 were waited for; matrix products, arithmetic and copies ran while one was open for 1% of the time, Pallas kernels for 18%

profile of v4, /device:TPU:0, one launch (start us, length us, event | category | flops | bytes accessed | tf_op | source)
XLA Modules:
  0.0 71.7 jit_solution(5287327240090096858)
XLA Ops:
  0.7 9.5 %warp.1 = (bf16[8,512,512]{2,1,0:T(8,128)(2,1)}, bf16[2,2,4,512,128]{4,3,2,1,0:T(8,128)(2,1)}, bf16[2,2,4,512,128]{4,3,2,1,0:T(8,128)(2,1)S(1)}) custom-call(s32[8]{0:T(128)} %patch_ref.5, bf16[8]{0:T(256)(128)(2,1)} %weight_hbm.1, bf16[8,512,512]{2,1,0:T(8,128)(2,1)} %images.1, bf16[8,512,512]{2,1,0:T(8,128)(2,1)} %rows.1, bf16[8,512,512]{2,1,0:T(8,128)(2,1)} %cols.1), custom_call_target="tpu_custom_call" | custom-call | flops 4294967296 | bytes 16777216 | tf_op jit(solution)/shard_map/warp/pallas_call | solution.py:181
  10.2 0.5 collective-permute-start
  11.2 2.6 %collective-permute-start.1 = (f32[1,3,512]{2,1,0:T(4,128)S(1)}, f32[1,3,512]{2,1,0:T(4,128)S(1)}, u32[]{:S(2)}, u32[]{:S(2)}) collective-permute-start(f32[1,3,512]{2,1,0:T(4,128)S(1)} %fusion), channel_id=1, source_target_pairs={{0,1},{1,0},{2,3},{3,2},{4,5},{5,4},{6,7},{7,6},{8,9},{9,8},{10,11... | collective-permute-start | bytes 18440 | tf_op jit(solution)/shard_map/ppermute | solution.py:48
  13.8 1.6 %collective-permute-done.1 = f32[1,3,512]{2,1,0:T(4,128)S(1)} collective-permute-done((f32[1,3,512]{2,1,0:T(4,128)S(1)}, f32[1,3,512]{2,1,0:T(4,128)S(1)}, u32[]{:S(2)}, u32[]{:S(2)}) %collective-permute-start.1) | collective-permute-done | bytes 6176 | tf_op jit(solution)/shard_map/ppermute | solution.py:48
  15.5 1.3 %fold.2 = bf16[2,4,512,128]{3,2,1,0:T(8,128)(2,1)S(1)} custom-call(s32[1]{0:T(128)} %bitcast.7.place_ref, bf16[2,2,4,512,128]{4,3,2,1,0:T(8,128)(2,1)S(1)} %get-tuple-element.38.kept, bf16[2,2,4,512,128]{4,3,2,1,0:T(8,128)(2,1)} %collective-permute-done.received), custom_call_target="tpu_custom_call" | custom-call | tf_op jit(solution)/shard_map/fold/pallas_call | solution.py:482
  16.8 2.3 %collective-permute-start.2 = (bf16[2,4,512,128]{3,2,1,0:T(8,128)(2,1)S(1)}, bf16[2,4,512,128]{3,2,1,0:T(8,128)(2,1)S(1)}, u32[]{:S(2)}, u32[]{:S(2)}) collective-permute-start(bf16[2,4,512,128]{3,2,1,0:T(8,128)(2,1)S(1)} %fold.2), channel_id=1, source_target_pairs={{0,16},{1,17},{2,18},{3,19},{4,20},{5,21},{6,22},{7,23},{8,9},{9,8... | collective-permute-start | bytes 3145736 | tf_op jit(solution)/shard_map/ppermute | solution.py:48
  19.2 1.6 %collective-permute-start.3 = (f32[2,3,512]{2,1,0:T(4,128)S(1)}, f32[2,3,512]{2,1,0:T(4,128)S(1)}, u32[]{:S(2)}, u32[]{:S(2)}) collective-permute-start(f32[2,3,512]{2,1,0:T(4,128)S(1)} %constant_dynamic-update-slice_fusion), channel_id=1, source_target_pairs={{0,2},{1,3},{2,0},{3,1},{4,6},{5,7},{6,4},{7,5},{8,10},{9,11},{10,... | collective-permute-start | bytes 36872 | tf_op jit(solution)/shard_map/ppermute | solution.py:48
  20.8 2.6 %collective-permute-start.4 = (f32[2,3,512]{2,1,0:T(4,128)S(1)}, f32[2,3,512]{2,1,0:T(4,128)S(1)}, u32[]{:S(2)}, u32[]{:S(2)}) collective-permute-start(f32[2,3,512]{2,1,0:T(4,128)S(1)} %constant_dynamic-update-slice_fusion), channel_id=1, source_target_pairs={{0,4},{1,5},{2,6},{3,7},{4,0},{5,1},{6,2},{7,3},{8,12},{9,13},{10,... | collective-permute-start | bytes 36872 | tf_op jit(solution)/shard_map/ppermute | solution.py:48
  23.6 1.3 %fold.3.kept = bf16[2,4,512,128]{3,2,1,0:T(8,128)(2,1)S(1)} custom-call(s32[1]{0:T(128)} %bitcast.3.place_ref, bf16[2,2,4,512,128]{4,3,2,1,0:T(8,128)(2,1)S(1)} %get-tuple-element.38.kept, bf16[2,2,4,512,128]{4,3,2,1,0:T(8,128)(2,1)} %collective-permute-done.received), custom_call_target="tpu_custom_call" | custom-call | tf_op jit(solution)/shard_map/fold/pallas_call | solution.py:482
  25.0 0.7 collective-permute-done.4
  25.7 3.2 %collective-permute-done.5 = f32[2,3,512]{2,1,0:T(4,128)S(1)} collective-permute-done((f32[2,3,512]{2,1,0:T(4,128)S(1)}, f32[2,3,512]{2,1,0:T(4,128)S(1)}, u32[]{:S(2)}, u32[]{:S(2)}) %collective-permute-start.5) | collective-permute-done | bytes 12320 | tf_op jit(solution)/shard_map/ppermute | solution.py:48
  29.0 5.0 %forced_flux.2 = (f32[6,1,512]{2,1,0:T(1,128)S(1)}, f32[32,512]{1,0:T(8,128)S(1)}) custom-call(s32[8]{0:T(128)S(1)} %copy-done, s32[8]{0:T(128)S(1)} %fusion.3.place_ref, bf16[8,512,512]{2,1,0:T(8,128)(2,1)} %get-tuple-element.43.warped, f32[8,1,512]{2,1,0:T(1,128)S(1)} %get-tuple-element.75.refs_0_.refs_1_, ...), custom_call_target="tpu_custom_call" | custom-call | flops 1610612736 | bytes 3145728 | tf_op jit(solution)/shard_map/forced_flux/pallas_call | solution.py:245
  34.3 1.6 %collective-permute-start.6 = (bf16[4,512,128]{2,1,0:T(8,128)(2,1)S(1)}, bf16[4,512,128]{2,1,0:T(8,128)(2,1)S(1)}, u32[]{:S(2)}, u32[]{:S(2)}) collective-permute-start(bf16[4,512,128]{2,1,0:T(8,128)(2,1)S(1)} %get-tuple-element.48), channel_id=1, source_target_pairs={{0,1},{1,0},{2,3},{3,2},{4,5},{5,4},{6,7},{7,6},{8,24},{9,25},{10,... | collective-permute-start | bytes 1572872 | tf_op jit(solution)/shard_map/ppermute | solution.py:48
  35.9 2.8 %forced_flux.3 = (f32[2,1,512]{2,1,0:T(1,128)S(1)}, f32[32,512]{1,0:T(8,128)S(1)}) custom-call(s32[8]{0:T(128)S(1)} %copy-done, s32[8]{0:T(128)S(1)} %fusion.3.place_ref, bf16[8,512,512]{2,1,0:T(8,128)(2,1)} %get-tuple-element.43.warped, f32[8,1,512]{2,1,0:T(1,128)S(1)} %get-tuple-element.75.refs_0_.refs_1_, ...), custom_call_target="tpu_custom_call" | custom-call | flops 536870912 | bytes 1048576 | tf_op jit(solution)/shard_map/forced_flux/pallas_call | solution.py:245
  38.8 3.9 %collective-permute-done.7 = bf16[32,512]{1,0:T(8,128)(2,1)S(1)} collective-permute-done((bf16[32,512]{1,0:T(8,128)(2,1)S(1)}, bf16[32,512]{1,0:T(8,128)(2,1)S(1)}, u32[]{:S(2)}, u32[]{:S(2)}) %collective-permute-start.7) | collective-permute-done | bytes 32800 | tf_op jit(solution)/shard_map/ppermute | solution.py:48
  42.7 1.0 %collective-permute-start.14 = (bf16[32,512]{1,0:T(8,128)(2,1)S(1)}, bf16[32,512]{1,0:T(8,128)(2,1)S(1)}, u32[]{:S(2)}, u32[]{:S(2)}) collective-permute-start(bf16[32,512]{1,0:T(8,128)(2,1)S(1)} %add_convert_fusion.2), channel_id=1, source_target_pairs={{0,4},{1,5},{2,6},{3,7},{4,0},{5,1},{6,2},{7,3},{8,12},{9,13},{10,... | collective-permute-start | bytes 98312 | tf_op jit(solution)/shard_map/ppermute | solution.py:48
  43.9 1.6 %collective-permute-start.8 = (bf16[512,128]{1,0:T(8,128)(2,1)S(1)}, bf16[512,128]{1,0:T(8,128)(2,1)S(1)}, u32[]{:S(2)}, u32[]{:S(2)}) collective-permute-start(bf16[512,128]{1,0:T(8,128)(2,1)S(1)} %get-tuple-element.53), channel_id=1, source_target_pairs={{0,2},{1,3},{2,0},{3,1},{4,6},{5,7},{6,4},{7,5},{8,10},{9,11},{10,... | collective-permute-start | bytes 393224 | tf_op jit(solution)/shard_map/ppermute | solution.py:48
  45.5 0.8 %collective-permute-start.9 = (bf16[512,128]{1,0:T(8,128)(2,1)S(1)}, bf16[512,128]{1,0:T(8,128)(2,1)S(1)}, u32[]{:S(2)}, u32[]{:S(2)}) collective-permute-start(bf16[512,128]{1,0:T(8,128)(2,1)S(1)} %get-tuple-element.54), channel_id=1, source_target_pairs={{0,4},{1,5},{2,6},{3,7},{4,0},{5,1},{6,2},{7,3},{8,12},{9,13},{10,... | collective-permute-start | bytes 393224 | tf_op jit(solution)/shard_map/ppermute | solution.py:48
  46.3 2.0 %collective-permute-start.10 = (bf16[512,128]{1,0:T(8,128)(2,1)S(1)}, bf16[512,128]{1,0:T(8,128)(2,1)S(1)}, u32[]{:S(2)}, u32[]{:S(2)}) collective-permute-start(bf16[512,128]{1,0:T(8,128)(2,1)S(1)} %get-tuple-element.55), channel_id=1, source_target_pairs={{0,6},{1,7},{2,4},{3,5},{4,2},{5,3},{6,0},{7,1},{8,14},{9,15},{10,... | collective-permute-start | bytes 393224 | tf_op jit(solution)/shard_map/ppermute | solution.py:48
  48.3 1.8 %collective-permute-done.14 = bf16[32,512]{1,0:T(8,128)(2,1)S(1)} collective-permute-done((bf16[32,512]{1,0:T(8,128)(2,1)S(1)}, bf16[32,512]{1,0:T(8,128)(2,1)S(1)}, u32[]{:S(2)}, u32[]{:S(2)}) %collective-permute-start.14) | collective-permute-done | bytes 32800 | tf_op jit(solution)/shard_map/ppermute | solution.py:48
  50.2 1.5 %prepare.1 = (bf16[512,512]{1,0:T(8,128)(2,1)S(1)}, bf16[512,512]{1,0:T(8,128)(2,1)S(1)}, f32[512,512]{1,0:T(8,128)S(1)}, bf16[128,512]{1,0:T(8,128)(2,1)S(1)}, bf16[128,512]{1,0:T(8,128)(2,1)S(1)}) custom-call(s32[1,512]{1,0:T(1,128)S(1)} %copy-done.1, s32[1,512]{1,0:T(1,128)S(1)} %copy-done.2, f32[512,512]{1,0:T(8,128)S(1)} %bitcast.17, ...), custom_call_target="tpu_custom_call" | custom-call | flops 1073741824 | bytes 5242880 | tf_op jit(solution)/shard_map/prepare/pallas_call | solution.py:295
  51.7 2.4 %collective-permute-done.15 = bf16[32,512]{1,0:T(8,128)(2,1)S(1)} collective-permute-done((bf16[32,512]{1,0:T(8,128)(2,1)S(1)}, bf16[32,512]{1,0:T(8,128)(2,1)S(1)}, u32[]{:S(2)}, u32[]{:S(2)}) %collective-permute-start.15) | collective-permute-done | bytes 32800 | tf_op jit(solution)/shard_map/ppermute | solution.py:48
  54.1 2.1 %collective-permute-done.9.refs_2_ = bf16[512,128]{1,0:T(8,128)(2,1)S(1)} collective-permute-done((bf16[512,128]{1,0:T(8,128)(2,1)S(1)}, bf16[512,128]{1,0:T(8,128)(2,1)S(1)}, u32[]{:S(2)}, u32[]{:S(2)}) %collective-permute-start.9) | collective-permute-done | bytes 131104 | tf_op jit(solution)/shard_map/ppermute | solution.py:48
  56.2 1.2 %share.1 = f32[32,8,128]{2,1,0:T(8,128)} custom-call(bf16[512,128]{1,0:T(8,128)(2,1)S(1)} %get-tuple-element.52.refs_0_, bf16[512,128]{1,0:T(8,128)(2,1)S(1)} %collective-permute-done.8.refs_1_, bf16[512,128]{1,0:T(8,128)(2,1)S(1)} %collective-permute-done.9.refs_2_, bf16[512,128]{1,0:T(8,128)(2,1)S(1)} %collective-permute-done.10.refs_3_, ...), custom_call_target="tpu_custom_call" | custom-call | flops 201326592 | bytes 1310720 | tf_op jit(solution)/shard_map/share/pallas_call | solution.py:355
  57.5 4.9 %all-to-all-start = ((f32[32,8,128]{2,1,0:T(8,128)}), f32[32,8,128]{2,1,0:T(8,128)S(1)}, u32[]{:S(2)}, u32[]{:S(2)}) async-start(f32[32,8,128]{2,1,0:T(8,128)} %share.1), calls=%async_computation | async-start | bytes 262144 | tf_op jit(solution)/shard_map/all_to_all | solution.py:593
  62.4 0.6 match.1
  63.0 0.3 collective-permute-start.11
  63.4 1.7 %collective-permute-start.12 = (bf16[144,128]{1,0:T(8,128)(2,1)S(1)}, bf16[144,128]{1,0:T(8,128)(2,1)S(1)}, u32[]{:S(2)}, u32[]{:S(2)}) collective-permute-start(bf16[144,128]{1,0:T(8,128)(2,1)S(1)} %get-tuple-element.65), channel_id=1, source_target_pairs={{0,16},{1,17},{2,18},{3,19},{4,20},{5,21},{6,22},{7,23},{8,24},{9,... | collective-permute-start | bytes 110600 | tf_op jit(solution)/shard_map/ppermute | solution.py:48
  65.1 2.4 %collective-permute-done.12.refs_2_ = bf16[144,128]{1,0:T(8,128)(2,1)S(1)} collective-permute-done((bf16[144,128]{1,0:T(8,128)(2,1)S(1)}, bf16[144,128]{1,0:T(8,128)(2,1)S(1)}, u32[]{:S(2)}, u32[]{:S(2)}) %collective-permute-start.12) | collective-permute-done | bytes 36896 | tf_op jit(solution)/shard_map/ppermute | solution.py:48
  67.5 1.5 %collective-permute-done.13.refs_3_ = bf16[144,128]{1,0:T(8,128)(2,1)S(1)} collective-permute-done((bf16[144,128]{1,0:T(8,128)(2,1)S(1)}, bf16[144,128]{1,0:T(8,128)(2,1)S(1)}, u32[]{:S(2)}, u32[]{:S(2)}) %collective-permute-start.13) | collective-permute-done | bytes 36896 | tf_op jit(solution)/shard_map/ppermute | solution.py:48
  69.0 1.2 %coadd_rows.1 = f32[128,512]{1,0:T(8,128)} custom-call(f32[512,512]{1,0:T(8,128)S(1)} %bitcast.19, bf16[144,128]{1,0:T(8,128)(2,1)S(1)} %get-tuple-element.63.refs_0_, bf16[144,128]{1,0:T(8,128)(2,1)S(1)} %collective-permute-done.11.refs_1_, bf16[144,128]{1,0:T(8,128)(2,1)S(1)} %collective-permute-done.12.refs_2_, ...), custom_call_target="tpu_custom_call" | custom-call | flops 402653184 | bytes 1572864 | tf_op jit(solution)/shard_map/coadd_rows/pallas_call | solution.py:400
  70.2 1.5 %finish.1 = (f32[1,4]{1,0:T(1,128)}, f32[8,512]{1,0:T(8,128)}) custom-call(s32[8]{0:T(128)S(1)} %copy-done, f32[1,512]{1,0:T(1,128)S(1)} %bitcast.16, f32[6,1,512]{2,1,0:T(1,128)S(1)} %get-tuple-element.67.flux_a, f32[2,1,512]{2,1,0:T(1,128)S(1)} %get-tuple-element.68.flux_b, f32[8,4,512]{2,1,0:T(4,128)S(1)} %reshape.50.sums, ...), custom_call_target="tpu_custom_call" | custom-call | tf_op jit(solution)/shard_map/finish/pallas_call | solution.py:440
  (50 shorter events, 1.4 us)
Async XLA Ops:
  0.6 10.1 %copy-start = (s32[8]{0:T(128)S(1)}, s32[8]{0:T(128)}, u32[]{:S(2)}) copy-start(s32[8]{0:T(128)} %patch_ref.5) | copy-start | bytes 100
  0.6 10.1 %copy-start.5 = (bf16[8]{0:T(256)(128)(2,1)S(1)}, bf16[8]{0:T(256)(128)(2,1)}, u32[]{:S(2)}) copy-start(bf16[8]{0:T(256)(128)(2,1)} %weight_hbm.1) | copy-start | bytes 52
  0.7 10.5 %copy-start.2 = (s32[1,512]{1,0:T(1,128)S(1)}, s32[1,512]{1,0:T(1,128)}, u32[]{:S(2)}) copy-start(s32[1,512]{1,0:T(1,128)} %src_col.1) | copy-start | bytes 6148
  0.7 10.5 %copy-start.1 = (s32[1,512]{1,0:T(1,128)S(1)}, s32[1,512]{1,0:T(1,128)}, u32[]{:S(2)}) copy-start(s32[1,512]{1,0:T(1,128)} %src_row) | copy-start | bytes 6148
  10.2 5.3 %collective-permute-start = (bf16[2,2,4,512,128]{4,3,2,1,0:T(8,128)(2,1)}, bf16[2,2,4,512,128]{4,3,2,1,0:T(8,128)(2,1)}, u32[]{:S(2)}, u32[]{:S(2)}) collective-permute-start(bf16[2,2,4,512,128]{4,3,2,1,0:T(8,128)(2,1)} %get-tuple-element.39), channel_id=1, source_target_pairs={{0,8},{1,9},{2,10},{3,11},{4,12},{5,13},{6,14},{7,15},{8,0},{9,1},... | collective-permute-start | bytes 6291464 | tf_op jit(solution)/shard_map/ppermute | solution.py:48
  11.2 4.2 %collective-permute-start.1 = (f32[1,3,512]{2,1,0:T(4,128)S(1)}, f32[1,3,512]{2,1,0:T(4,128)S(1)}, u32[]{:S(2)}, u32[]{:S(2)}) collective-permute-start(f32[1,3,512]{2,1,0:T(4,128)S(1)} %fusion), channel_id=1, source_target_pairs={{0,1},{1,0},{2,3},{3,2},{4,5},{5,4},{6,7},{7,6},{8,9},{9,8},{10,11... | collective-permute-start | bytes 18440 | tf_op jit(solution)/shard_map/ppermute | solution.py:48
  16.8 17.2 %collective-permute-start.2 = (bf16[2,4,512,128]{3,2,1,0:T(8,128)(2,1)S(1)}, bf16[2,4,512,128]{3,2,1,0:T(8,128)(2,1)S(1)}, u32[]{:S(2)}, u32[]{:S(2)}) collective-permute-start(bf16[2,4,512,128]{3,2,1,0:T(8,128)(2,1)S(1)} %fold.2), channel_id=1, source_target_pairs={{0,16},{1,17},{2,18},{3,19},{4,20},{5,21},{6,22},{7,23},{8,9},{9,8... | collective-permute-start | bytes 3145736 | tf_op jit(solution)/shard_map/ppermute | solution.py:48
  19.2 5.8 %collective-permute-start.3 = (f32[2,3,512]{2,1,0:T(4,128)S(1)}, f32[2,3,512]{2,1,0:T(4,128)S(1)}, u32[]{:S(2)}, u32[]{:S(2)}) collective-permute-start(f32[2,3,512]{2,1,0:T(4,128)S(1)} %constant_dynamic-update-slice_fusion), channel_id=1, source_target_pairs={{0,2},{1,3},{2,0},{3,1},{4,6},{5,7},{6,4},{7,5},{8,10},{9,11},{10,... | collective-permute-start | bytes 36872 | tf_op jit(solution)/shard_map/ppermute | solution.py:48
  20.8 4.9 %collective-permute-start.4 = (f32[2,3,512]{2,1,0:T(4,128)S(1)}, f32[2,3,512]{2,1,0:T(4,128)S(1)}, u32[]{:S(2)}, u32[]{:S(2)}) collective-permute-start(f32[2,3,512]{2,1,0:T(4,128)S(1)} %constant_dynamic-update-slice_fusion), channel_id=1, source_target_pairs={{0,4},{1,5},{2,6},{3,7},{4,0},{5,1},{6,2},{7,3},{8,12},{9,13},{10,... | collective-permute-start | bytes 36872 | tf_op jit(solution)/shard_map/ppermute | solution.py:48
  23.4 5.5 %collective-permute-start.5 = (f32[2,3,512]{2,1,0:T(4,128)S(1)}, f32[2,3,512]{2,1,0:T(4,128)S(1)}, u32[]{:S(2)}, u32[]{:S(2)}) collective-permute-start(f32[2,3,512]{2,1,0:T(4,128)S(1)} %constant_dynamic-update-slice_fusion), channel_id=1, source_target_pairs={{0,6},{1,7},{2,4},{3,5},{4,2},{5,3},{6,0},{7,1},{8,14},{9,15},{10,... | collective-permute-start | bytes 36872 | tf_op jit(solution)/shard_map/ppermute | solution.py:48
  34.1 16.2 %copy-start.3 = (f32[1,512,512]{2,1,0:T(8,128)S(1)}, f32[1,512,512]{2,1,0:T(8,128)}, u32[]{:S(2)}) copy-start(f32[1,512,512]{2,1,0:T(8,128)} %param.14) | copy-start | bytes 3145732
  34.1 16.2 %copy-start.4 = (f32[1,512,512]{2,1,0:T(8,128)S(1)}, f32[1,512,512]{2,1,0:T(8,128)}, u32[]{:S(2)}) copy-start(f32[1,512,512]{2,1,0:T(8,128)} %param.15) | copy-start | bytes 3145732
  34.3 9.4 %collective-permute-start.6 = (bf16[4,512,128]{2,1,0:T(8,128)(2,1)S(1)}, bf16[4,512,128]{2,1,0:T(8,128)(2,1)S(1)}, u32[]{:S(2)}, u32[]{:S(2)}) collective-permute-start(bf16[4,512,128]{2,1,0:T(8,128)(2,1)S(1)} %get-tuple-element.48), channel_id=1, source_target_pairs={{0,1},{1,0},{2,3},{3,2},{4,5},{5,4},{6,7},{7,6},{8,24},{9,25},{10,... | collective-permute-start | bytes 1572872 | tf_op jit(solution)/shard_map/ppermute | solution.py:48
  38.7 4.0 %collective-permute-start.7 = (bf16[32,512]{1,0:T(8,128)(2,1)S(1)}, bf16[32,512]{1,0:T(8,128)(2,1)S(1)}, u32[]{:S(2)}, u32[]{:S(2)}) collective-permute-start(bf16[32,512]{1,0:T(8,128)(2,1)S(1)} %convert_element_type.52), channel_id=1, source_target_pairs={{0,2},{1,3},{2,0},{3,1},{4,6},{5,7},{6,4},{7,5},{8,10},{9,11},{10,... | collective-permute-start | bytes 98312 | tf_op jit(solution)/shard_map/ppermute | solution.py:48
  42.7 7.4 %collective-permute-start.14 = (bf16[32,512]{1,0:T(8,128)(2,1)S(1)}, bf16[32,512]{1,0:T(8,128)(2,1)S(1)}, u32[]{:S(2)}, u32[]{:S(2)}) collective-permute-start(bf16[32,512]{1,0:T(8,128)(2,1)S(1)} %add_convert_fusion.2), channel_id=1, source_target_pairs={{0,4},{1,5},{2,6},{3,7},{4,0},{5,1},{6,2},{7,3},{8,12},{9,13},{10,... | collective-permute-start | bytes 98312 | tf_op jit(solution)/shard_map/ppermute | solution.py:48
  43.9 10.3 %collective-permute-start.8 = (bf16[512,128]{1,0:T(8,128)(2,1)S(1)}, bf16[512,128]{1,0:T(8,128)(2,1)S(1)}, u32[]{:S(2)}, u32[]{:S(2)}) collective-permute-start(bf16[512,128]{1,0:T(8,128)(2,1)S(1)} %get-tuple-element.53), channel_id=1, source_target_pairs={{0,2},{1,3},{2,0},{3,1},{4,6},{5,7},{6,4},{7,5},{8,10},{9,11},{10,... | collective-permute-start | bytes 393224 | tf_op jit(solution)/shard_map/ppermute | solution.py:48
  45.5 10.7 %collective-permute-start.9 = (bf16[512,128]{1,0:T(8,128)(2,1)S(1)}, bf16[512,128]{1,0:T(8,128)(2,1)S(1)}, u32[]{:S(2)}, u32[]{:S(2)}) collective-permute-start(bf16[512,128]{1,0:T(8,128)(2,1)S(1)} %get-tuple-element.54), channel_id=1, source_target_pairs={{0,4},{1,5},{2,6},{3,7},{4,0},{5,1},{6,2},{7,3},{8,12},{9,13},{10,... | collective-permute-start | bytes 393224 | tf_op jit(solution)/shard_map/ppermute | solution.py:48
  46.3 9.9 %collective-permute-start.10 = (bf16[512,128]{1,0:T(8,128)(2,1)S(1)}, bf16[512,128]{1,0:T(8,128)(2,1)S(1)}, u32[]{:S(2)}, u32[]{:S(2)}) collective-permute-start(bf16[512,128]{1,0:T(8,128)(2,1)S(1)} %get-tuple-element.55), channel_id=1, source_target_pairs={{0,6},{1,7},{2,4},{3,5},{4,2},{5,3},{6,0},{7,1},{8,14},{9,15},{10,... | collective-permute-start | bytes 393224 | tf_op jit(solution)/shard_map/ppermute | solution.py:48
  50.1 4.0 %collective-permute-start.15 = (bf16[32,512]{1,0:T(8,128)(2,1)S(1)}, bf16[32,512]{1,0:T(8,128)(2,1)S(1)}, u32[]{:S(2)}, u32[]{:S(2)}) collective-permute-start(bf16[32,512]{1,0:T(8,128)(2,1)S(1)} %add_convert_fusion.1), channel_id=1, source_target_pairs={{0,1},{1,0},{2,3},{3,2},{4,5},{5,4},{6,7},{7,6},{8,9},{9,8},{10,11... | collective-permute-start | bytes 98312 | tf_op jit(solution)/shard_map/ppermute | solution.py:48
  57.5 12.8 %all-to-all-start = ((f32[32,8,128]{2,1,0:T(8,128)}), f32[32,8,128]{2,1,0:T(8,128)S(1)}, u32[]{:S(2)}, u32[]{:S(2)}) async-start(f32[32,8,128]{2,1,0:T(8,128)} %share.1), calls=%async_computation | async-start | bytes 262144 | tf_op jit(solution)/shard_map/all_to_all | solution.py:593
  63.0 2.0 %collective-permute-start.11 = (bf16[144,128]{1,0:T(8,128)(2,1)S(1)}, bf16[144,128]{1,0:T(8,128)(2,1)S(1)}, u32[]{:S(2)}, u32[]{:S(2)}) collective-permute-start(bf16[144,128]{1,0:T(8,128)(2,1)S(1)} %get-tuple-element.64), channel_id=1, source_target_pairs={{0,8},{1,9},{2,10},{3,11},{4,12},{5,13},{6,14},{7,15},{8,0},{9,1},... | collective-permute-start | bytes 110600 | tf_op jit(solution)/shard_map/ppermute | solution.py:48
  63.4 4.1 %collective-permute-start.12 = (bf16[144,128]{1,0:T(8,128)(2,1)S(1)}, bf16[144,128]{1,0:T(8,128)(2,1)S(1)}, u32[]{:S(2)}, u32[]{:S(2)}) collective-permute-start(bf16[144,128]{1,0:T(8,128)(2,1)S(1)} %get-tuple-element.65), channel_id=1, source_target_pairs={{0,16},{1,17},{2,18},{3,19},{4,20},{5,21},{6,22},{7,23},{8,24},{9,... | collective-permute-start | bytes 110600 | tf_op jit(solution)/shard_map/ppermute | solution.py:48
  65.0 4.0 %collective-permute-start.13 = (bf16[144,128]{1,0:T(8,128)(2,1)S(1)}, bf16[144,128]{1,0:T(8,128)(2,1)S(1)}, u32[]{:S(2)}, u32[]{:S(2)}) collective-permute-start(bf16[144,128]{1,0:T(8,128)(2,1)S(1)} %get-tuple-element.66), channel_id=1, source_target_pairs={{0,24},{1,25},{2,26},{3,27},{4,28},{5,29},{6,30},{7,31},{8,16},{9,... | collective-permute-start | bytes 110600 | tf_op jit(solution)/shard_map/ppermute | solution.py:48

commit v5 on v4

--- a/solution.py
+++ b/solution.py
@@ -522,14 +522,17 @@
             self.own = fold(place, self.own, after(received, *self.sent))
         else:
             self.own, self.sent = spread(place, (self.own, received))
-        self.received = [swap(array, step) for step, array in enumerate(self.sent, 1)]
+        order = sorted(range(1, len(self.sent) + 1), reverse=True)
+        made = {step: swap(self.sent[step - 1], step) for step in order}
+        self.received = [made[step] for step in sorted(made)]
 
     def pieces(self):
         return [self.own] + self.received
 
 
 def gather_patch(lay, near):
-    return jnp.concatenate([near] + [lay.swap_high(near, step) for step in range(1, lay.highs)])
+    far = [lay.swap_high(near, step) for step in reversed(range(1, lay.highs))]
+    return jnp.concatenate([near] + far[::-1])
 
 
 def add_wide(left, right):

time: 72 us -> 72 us (level)
  no operation moved by 1% of the time
where the time goes in v5:
time: 72 us; the launch traced here: 71.7 us
  Pallas kernels  26.4 us (37%)
  starting transfers between devices  24 us (33%)
  waiting for transfers between devices  19.7 us (27%)
  between operations  0.89 us (1%)
    ppermute x16, waiting for transfers between devices, permute(): return lax.ppermute(array, AXES, pairs)  19.7 us
    ppermute x16, starting transfers between devices, permute(): return lax.ppermute(array, AXES, pairs)  19.1 us
    pallas_call x1, Pallas kernels, warp(): pl.pallas_call(functools.partial(warp_kernel, lay), in_specs=[in_any] * 5...  9.55 us
    pallas_call x2, Pallas kernels, forced_flux(): pl.pallas_call(functools.partial(flux_kernel, lay, begin), grid_spec=pltp...  7.82 us
    all_to_all x1, starting transfers between devices, shards(): fluxes = lax.all_to_all(fluxes, AXES, 0, 0, tiled=True)  4.93 us
    pallas_call x2, Pallas kernels, fold(): pl.pallas_call(fold_kernel, grid_spec=pltpu.PrefetchScalarGridSpec(num_sc...  2.69 us
    pallas_call x1, Pallas kernels, prepare(): pl.pallas_call(functools.partial(prepare_kernel, lay), in_specs=[IN_VMEM]...  1.46 us
    pallas_call x1, Pallas kernels, finish(): pl.pallas_call(functools.partial(finish_kernel, lay), in_specs=[pl.BlockS...  1.45 us
  transfers between devices with their start and end apart: 17, of which 9 were waited for; matrix products, arithmetic and copies ran while one was open for 1% of the time, Pallas kernels for 18%

profile of v5, /device:TPU:0, one launch (start us, length us, event | category | flops | bytes accessed | tf_op | source)
XLA Modules:
  0.0 71.7 jit_solution(5287327240090096858)
XLA Ops:
  0.7 9.5 %warp.1 = (bf16[8,512,512]{2,1,0:T(8,128)(2,1)}, bf16[2,2,4,512,128]{4,3,2,1,0:T(8,128)(2,1)}, bf16[2,2,4,512,128]{4,3,2,1,0:T(8,128)(2,1)S(1)}) custom-call(s32[8]{0:T(128)} %patch_ref.5, bf16[8]{0:T(256)(128)(2,1)} %weight_hbm.1, bf16[8,512,512]{2,1,0:T(8,128)(2,1)} %images.1, bf16[8,512,512]{2,1,0:T(8,128)(2,1)} %rows.1, bf16[8,512,512]{2,1,0:T(8,128)(2,1)} %cols.1), custom_call_target="tpu_custom_call" | custom-call | flops 4294967296 | bytes 16777216 | tf_op jit(solution)/shard_map/warp/pallas_call | solution.py:181
  10.2 0.5 collective-permute-start
  11.2 2.6 %collective-permute-start.1 = (f32[1,3,512]{2,1,0:T(4,128)S(1)}, f32[1,3,512]{2,1,0:T(4,128)S(1)}, u32[]{:S(2)}, u32[]{:S(2)}) collective-permute-start(f32[1,3,512]{2,1,0:T(4,128)S(1)} %fusion), channel_id=1, source_target_pairs={{0,1},{1,0},{2,3},{3,2},{4,5},{5,4},{6,7},{7,6},{8,9},{9,8},{10,11... | collective-permute-start | bytes 18440 | tf_op jit(solution)/shard_map/ppermute | solution.py:48
  13.8 1.6 %collective-permute-done.1 = f32[1,3,512]{2,1,0:T(4,128)S(1)} collective-permute-done((f32[1,3,512]{2,1,0:T(4,128)S(1)}, f32[1,3,512]{2,1,0:T(4,128)S(1)}, u32[]{:S(2)}, u32[]{:S(2)}) %collective-permute-start.1) | collective-permute-done | bytes 6176 | tf_op jit(solution)/shard_map/ppermute | solution.py:48
  15.5 1.3 %fold.2 = bf16[2,4,512,128]{3,2,1,0:T(8,128)(2,1)S(1)} custom-call(s32[1]{0:T(128)} %bitcast.7.place_ref, bf16[2,2,4,512,128]{4,3,2,1,0:T(8,128)(2,1)S(1)} %get-tuple-element.38.kept, bf16[2,2,4,512,128]{4,3,2,1,0:T(8,128)(2,1)} %collective-permute-done.received), custom_call_target="tpu_custom_call" | custom-call | tf_op jit(solution)/shard_map/fold/pallas_call | solution.py:482
  16.8 2.3 %collective-permute-start.2 = (bf16[2,4,512,128]{3,2,1,0:T(8,128)(2,1)S(1)}, bf16[2,4,512,128]{3,2,1,0:T(8,128)(2,1)S(1)}, u32[]{:S(2)}, u32[]{:S(2)}) collective-permute-start(bf16[2,4,512,128]{3,2,1,0:T(8,128)(2,1)S(1)} %fold.2), channel_id=1, source_target_pairs={{0,16},{1,17},{2,18},{3,19},{4,20},{5,21},{6,22},{7,23},{8,9},{9,8... | collective-permute-start | bytes 3145736 | tf_op jit(solution)/shard_map/ppermute | solution.py:48
  19.2 1.6 %collective-permute-start.3 = (f32[2,3,512]{2,1,0:T(4,128)S(1)}, f32[2,3,512]{2,1,0:T(4,128)S(1)}, u32[]{:S(2)}, u32[]{:S(2)}) collective-permute-start(f32[2,3,512]{2,1,0:T(4,128)S(1)} %constant_dynamic-update-slice_fusion), channel_id=1, source_target_pairs={{0,2},{1,3},{2,0},{3,1},{4,6},{5,7},{6,4},{7,5},{8,10},{9,11},{10,... | collective-permute-start | bytes 36872 | tf_op jit(solution)/shard_map/ppermute | solution.py:48
  20.8 2.6 %collective-permute-start.4 = (f32[2,3,512]{2,1,0:T(4,128)S(1)}, f32[2,3,512]{2,1,0:T(4,128)S(1)}, u32[]{:S(2)}, u32[]{:S(2)}) collective-permute-start(f32[2,3,512]{2,1,0:T(4,128)S(1)} %constant_dynamic-update-slice_fusion), channel_id=1, source_target_pairs={{0,4},{1,5},{2,6},{3,7},{4,0},{5,1},{6,2},{7,3},{8,12},{9,13},{10,... | collective-permute-start | bytes 36872 | tf_op jit(solution)/shard_map/ppermute | solution.py:48
  23.6 1.3 %fold.3.kept = bf16[2,4,512,128]{3,2,1,0:T(8,128)(2,1)S(1)} custom-call(s32[1]{0:T(128)} %bitcast.3.place_ref, bf16[2,2,4,512,128]{4,3,2,1,0:T(8,128)(2,1)S(1)} %get-tuple-element.38.kept, bf16[2,2,4,512,128]{4,3,2,1,0:T(8,128)(2,1)} %collective-permute-done.received), custom_call_target="tpu_custom_call" | custom-call | tf_op jit(solution)/shard_map/fold/pallas_call | solution.py:482
  25.0 0.7 collective-permute-done.4
  25.7 3.2 %collective-permute-done.5 = f32[2,3,512]{2,1,0:T(4,128)S(1)} collective-permute-done((f32[2,3,512]{2,1,0:T(4,128)S(1)}, f32[2,3,512]{2,1,0:T(4,128)S(1)}, u32[]{:S(2)}, u32[]{:S(2)}) %collective-permute-start.5) | collective-permute-done | bytes 12320 | tf_op jit(solution)/shard_map/ppermute | solution.py:48
  29.0 5.0 %forced_flux.2 = (f32[6,1,512]{2,1,0:T(1,128)S(1)}, f32[32,512]{1,0:T(8,128)S(1)}) custom-call(s32[8]{0:T(128)S(1)} %copy-done, s32[8]{0:T(128)S(1)} %fusion.3.place_ref, bf16[8,512,512]{2,1,0:T(8,128)(2,1)} %get-tuple-element.43.warped, f32[8,1,512]{2,1,0:T(1,128)S(1)} %get-tuple-element.75.refs_0_.refs_1_, ...), custom_call_target="tpu_custom_call" | custom-call | flops 1610612736 | bytes 3145728 | tf_op jit(solution)/shard_map/forced_flux/pallas_call | solution.py:245
  34.3 1.6 %collective-permute-start.6 = (bf16[4,512,128]{2,1,0:T(8,128)(2,1)S(1)}, bf16[4,512,128]{2,1,0:T(8,128)(2,1)S(1)}, u32[]{:S(2)}, u32[]{:S(2)}) collective-permute-start(bf16[4,512,128]{2,1,0:T(8,128)(2,1)S(1)} %get-tuple-element.48), channel_id=1, source_target_pairs={{0,1},{1,0},{2,3},{3,2},{4,5},{5,4},{6,7},{7,6},{8,24},{9,25},{10,... | collective-permute-start | bytes 1572872 | tf_op jit(solution)/shard_map/ppermute | solution.py:48
  35.9 2.8 %forced_flux.3 = (f32[2,1,512]{2,1,0:T(1,128)S(1)}, f32[32,512]{1,0:T(8,128)S(1)}) custom-call(s32[8]{0:T(128)S(1)} %copy-done, s32[8]{0:T(128)S(1)} %fusion.3.place_ref, bf16[8,512,512]{2,1,0:T(8,128)(2,1)} %get-tuple-element.43.warped, f32[8,1,512]{2,1,0:T(1,128)S(1)} %get-tuple-element.75.refs_0_.refs_1_, ...), custom_call_target="tpu_custom_call" | custom-call | flops 536870912 | bytes 1048576 | tf_op jit(solution)/shard_map/forced_flux/pallas_call | solution.py:245
  38.8 3.9 %collective-permute-done.7 = bf16[32,512]{1,0:T(8,128)(2,1)S(1)} collective-permute-done((bf16[32,512]{1,0:T(8,128)(2,1)S(1)}, bf16[32,512]{1,0:T(8,128)(2,1)S(1)}, u32[]{:S(2)}, u32[]{:S(2)}) %collective-permute-start.7) | collective-permute-done | bytes 32800 | tf_op jit(solution)/shard_map/ppermute | solution.py:48
  42.7 1.0 %collective-permute-start.14 = (bf16[32,512]{1,0:T(8,128)(2,1)S(1)}, bf16[32,512]{1,0:T(8,128)(2,1)S(1)}, u32[]{:S(2)}, u32[]{:S(2)}) collective-permute-start(bf16[32,512]{1,0:T(8,128)(2,1)S(1)} %add_convert_fusion.2), channel_id=1, source_target_pairs={{0,4},{1,5},{2,6},{3,7},{4,0},{5,1},{6,2},{7,3},{8,12},{9,13},{10,... | collective-permute-start | bytes 98312 | tf_op jit(solution)/shard_map/ppermute | solution.py:48
  43.9 1.6 %collective-permute-start.8 = (bf16[512,128]{1,0:T(8,128)(2,1)S(1)}, bf16[512,128]{1,0:T(8,128)(2,1)S(1)}, u32[]{:S(2)}, u32[]{:S(2)}) collective-permute-start(bf16[512,128]{1,0:T(8,128)(2,1)S(1)} %get-tuple-element.53), channel_id=1, source_target_pairs={{0,2},{1,3},{2,0},{3,1},{4,6},{5,7},{6,4},{7,5},{8,10},{9,11},{10,... | collective-permute-start | bytes 393224 | tf_op jit(solution)/shard_map/ppermute | solution.py:48
  45.5 0.8 %collective-permute-start.9 = (bf16[512,128]{1,0:T(8,128)(2,1)S(1)}, bf16[512,128]{1,0:T(8,128)(2,1)S(1)}, u32[]{:S(2)}, u32[]{:S(2)}) collective-permute-start(bf16[512,128]{1,0:T(8,128)(2,1)S(1)} %get-tuple-element.54), channel_id=1, source_target_pairs={{0,4},{1,5},{2,6},{3,7},{4,0},{5,1},{6,2},{7,3},{8,12},{9,13},{10,... | collective-permute-start | bytes 393224 | tf_op jit(solution)/shard_map/ppermute | solution.py:48
  46.3 2.0 %collective-permute-start.10 = (bf16[512,128]{1,0:T(8,128)(2,1)S(1)}, bf16[512,128]{1,0:T(8,128)(2,1)S(1)}, u32[]{:S(2)}, u32[]{:S(2)}) collective-permute-start(bf16[512,128]{1,0:T(8,128)(2,1)S(1)} %get-tuple-element.55), channel_id=1, source_target_pairs={{0,6},{1,7},{2,4},{3,5},{4,2},{5,3},{6,0},{7,1},{8,14},{9,15},{10,... | collective-permute-start | bytes 393224 | tf_op jit(solution)/shard_map/ppermute | solution.py:48
  48.3 1.9 %collective-permute-done.14 = bf16[32,512]{1,0:T(8,128)(2,1)S(1)} collective-permute-done((bf16[32,512]{1,0:T(8,128)(2,1)S(1)}, bf16[32,512]{1,0:T(8,128)(2,1)S(1)}, u32[]{:S(2)}, u32[]{:S(2)}) %collective-permute-start.14) | collective-permute-done | bytes 32800 | tf_op jit(solution)/shard_map/ppermute | solution.py:48
  50.3 1.5 %prepare.1 = (bf16[512,512]{1,0:T(8,128)(2,1)S(1)}, bf16[512,512]{1,0:T(8,128)(2,1)S(1)}, f32[512,512]{1,0:T(8,128)S(1)}, bf16[128,512]{1,0:T(8,128)(2,1)S(1)}, bf16[128,512]{1,0:T(8,128)(2,1)S(1)}) custom-call(s32[1,512]{1,0:T(1,128)S(1)} %copy-done.1, s32[1,512]{1,0:T(1,128)S(1)} %copy-done.2, f32[512,512]{1,0:T(8,128)S(1)} %bitcast.17, ...), custom_call_target="tpu_custom_call" | custom-call | flops 1073741824 | bytes 5242880 | tf_op jit(solution)/shard_map/prepare/pallas_call | solution.py:295
  51.8 2.4 %collective-permute-done.15 = bf16[32,512]{1,0:T(8,128)(2,1)S(1)} collective-permute-done((bf16[32,512]{1,0:T(8,128)(2,1)S(1)}, bf16[32,512]{1,0:T(8,128)(2,1)S(1)}, u32[]{:S(2)}, u32[]{:S(2)}) %collective-permute-start.15) | collective-permute-done | bytes 32800 | tf_op jit(solution)/shard_map/ppermute | solution.py:48
  54.2 2.0 %collective-permute-done.9.refs_2_ = bf16[512,128]{1,0:T(8,128)(2,1)S(1)} collective-permute-done((bf16[512,128]{1,0:T(8,128)(2,1)S(1)}, bf16[512,128]{1,0:T(8,128)(2,1)S(1)}, u32[]{:S(2)}, u32[]{:S(2)}) %collective-permute-start.9) | collective-permute-done | bytes 131104 | tf_op jit(solution)/shard_map/ppermute | solution.py:48
  56.2 1.2 %share.1 = f32[32,8,128]{2,1,0:T(8,128)} custom-call(bf16[512,128]{1,0:T(8,128)(2,1)S(1)} %get-tuple-element.52.refs_0_, bf16[512,128]{1,0:T(8,128)(2,1)S(1)} %collective-permute-done.8.refs_1_, bf16[512,128]{1,0:T(8,128)(2,1)S(1)} %collective-permute-done.9.refs_2_, bf16[512,128]{1,0:T(8,128)(2,1)S(1)} %collective-permute-done.10.refs_3_, ...), custom_call_target="tpu_custom_call" | custom-call | flops 201326592 | bytes 1310720 | tf_op jit(solution)/shard_map/share/pallas_call | solution.py:355
  57.5 4.9 %all-to-all-start = ((f32[32,8,128]{2,1,0:T(8,128)}), f32[32,8,128]{2,1,0:T(8,128)S(1)}, u32[]{:S(2)}, u32[]{:S(2)}) async-start(f32[32,8,128]{2,1,0:T(8,128)} %share.1), calls=%async_computation | async-start | bytes 262144 | tf_op jit(solution)/shard_map/all_to_all | solution.py:596
  62.4 0.6 match.1
  63.0 0.3 collective-permute-start.11
  63.4 1.7 %collective-permute-start.12 = (bf16[144,128]{1,0:T(8,128)(2,1)S(1)}, bf16[144,128]{1,0:T(8,128)(2,1)S(1)}, u32[]{:S(2)}, u32[]{:S(2)}) collective-permute-start(bf16[144,128]{1,0:T(8,128)(2,1)S(1)} %get-tuple-element.65), channel_id=1, source_target_pairs={{0,16},{1,17},{2,18},{3,19},{4,20},{5,21},{6,22},{7,23},{8,24},{9,... | collective-permute-start | bytes 110600 | tf_op jit(solution)/shard_map/ppermute | solution.py:48
  65.1 2.4 %collective-permute-done.12.refs_2_ = bf16[144,128]{1,0:T(8,128)(2,1)S(1)} collective-permute-done((bf16[144,128]{1,0:T(8,128)(2,1)S(1)}, bf16[144,128]{1,0:T(8,128)(2,1)S(1)}, u32[]{:S(2)}, u32[]{:S(2)}) %collective-permute-start.12) | collective-permute-done | bytes 36896 | tf_op jit(solution)/shard_map/ppermute | solution.py:48
  67.5 1.5 %collective-permute-done.13.refs_3_ = bf16[144,128]{1,0:T(8,128)(2,1)S(1)} collective-permute-done((bf16[144,128]{1,0:T(8,128)(2,1)S(1)}, bf16[144,128]{1,0:T(8,128)(2,1)S(1)}, u32[]{:S(2)}, u32[]{:S(2)}) %collective-permute-start.13) | collective-permute-done | bytes 36896 | tf_op jit(solution)/shard_map/ppermute | solution.py:48
  69.0 1.2 %coadd_rows.1 = f32[128,512]{1,0:T(8,128)} custom-call(f32[512,512]{1,0:T(8,128)S(1)} %bitcast.19, bf16[144,128]{1,0:T(8,128)(2,1)S(1)} %get-tuple-element.63.refs_0_, bf16[144,128]{1,0:T(8,128)(2,1)S(1)} %collective-permute-done.11.refs_1_, bf16[144,128]{1,0:T(8,128)(2,1)S(1)} %collective-permute-done.12.refs_2_, ...), custom_call_target="tpu_custom_call" | custom-call | flops 402653184 | bytes 1572864 | tf_op jit(solution)/shard_map/coadd_rows/pallas_call | solution.py:400
  70.2 1.5 %finish.1 = (f32[1,4]{1,0:T(1,128)}, f32[8,512]{1,0:T(8,128)}) custom-call(s32[8]{0:T(128)S(1)} %copy-done, f32[1,512]{1,0:T(1,128)S(1)} %bitcast.16, f32[6,1,512]{2,1,0:T(1,128)S(1)} %get-tuple-element.67.flux_a, f32[2,1,512]{2,1,0:T(1,128)S(1)} %get-tuple-element.68.flux_b, f32[8,4,512]{2,1,0:T(4,128)S(1)} %reshape.50.sums, ...), custom_call_target="tpu_custom_call" | custom-call | tf_op jit(solution)/shard_map/finish/pallas_call | solution.py:440
  (50 shorter events, 1.4 us)
Async XLA Ops:
  0.6 10.1 %copy-start = (s32[8]{0:T(128)S(1)}, s32[8]{0:T(128)}, u32[]{:S(2)}) copy-start(s32[8]{0:T(128)} %patch_ref.5) | copy-start | bytes 100
  0.6 10.1 %copy-start.5 = (bf16[8]{0:T(256)(128)(2,1)S(1)}, bf16[8]{0:T(256)(128)(2,1)}, u32[]{:S(2)}) copy-start(bf16[8]{0:T(256)(128)(2,1)} %weight_hbm.1) | copy-start | bytes 52
  0.7 10.5 %copy-start.2 = (s32[1,512]{1,0:T(1,128)S(1)}, s32[1,512]{1,0:T(1,128)}, u32[]{:S(2)}) copy-start(s32[1,512]{1,0:T(1,128)} %src_col.1) | copy-start | bytes 6148
  0.7 10.5 %copy-start.1 = (s32[1,512]{1,0:T(1,128)S(1)}, s32[1,512]{1,0:T(1,128)}, u32[]{:S(2)}) copy-start(s32[1,512]{1,0:T(1,128)} %src_row) | copy-start | bytes 6148
  10.2 5.3 %collective-permute-start = (bf16[2,2,4,512,128]{4,3,2,1,0:T(8,128)(2,1)}, bf16[2,2,4,512,128]{4,3,2,1,0:T(8,128)(2,1)}, u32[]{:S(2)}, u32[]{:S(2)}) collective-permute-start(bf16[2,2,4,512,128]{4,3,2,1,0:T(8,128)(2,1)} %get-tuple-element.39), channel_id=1, source_target_pairs={{0,8},{1,9},{2,10},{3,11},{4,12},{5,13},{6,14},{7,15},{8,0},{9,1},... | collective-permute-start | bytes 6291464 | tf_op jit(solution)/shard_map/ppermute | solution.py:48
  11.2 4.2 %collective-permute-start.1 = (f32[1,3,512]{2,1,0:T(4,128)S(1)}, f32[1,3,512]{2,1,0:T(4,128)S(1)}, u32[]{:S(2)}, u32[]{:S(2)}) collective-permute-start(f32[1,3,512]{2,1,0:T(4,128)S(1)} %fusion), channel_id=1, source_target_pairs={{0,1},{1,0},{2,3},{3,2},{4,5},{5,4},{6,7},{7,6},{8,9},{9,8},{10,11... | collective-permute-start | bytes 18440 | tf_op jit(solution)/shard_map/ppermute | solution.py:48
  16.8 17.2 %collective-permute-start.2 = (bf16[2,4,512,128]{3,2,1,0:T(8,128)(2,1)S(1)}, bf16[2,4,512,128]{3,2,1,0:T(8,128)(2,1)S(1)}, u32[]{:S(2)}, u32[]{:S(2)}) collective-permute-start(bf16[2,4,512,128]{3,2,1,0:T(8,128)(2,1)S(1)} %fold.2), channel_id=1, source_target_pairs={{0,16},{1,17},{2,18},{3,19},{4,20},{5,21},{6,22},{7,23},{8,9},{9,8... | collective-permute-start | bytes 3145736 | tf_op jit(solution)/shard_map/ppermute | solution.py:48
  19.2 5.8 %collective-permute-start.3 = (f32[2,3,512]{2,1,0:T(4,128)S(1)}, f32[2,3,512]{2,1,0:T(4,128)S(1)}, u32[]{:S(2)}, u32[]{:S(2)}) collective-permute-start(f32[2,3,512]{2,1,0:T(4,128)S(1)} %constant_dynamic-update-slice_fusion), channel_id=1, source_target_pairs={{0,2},{1,3},{2,0},{3,1},{4,6},{5,7},{6,4},{7,5},{8,10},{9,11},{10,... | collective-permute-start | bytes 36872 | tf_op jit(solution)/shard_map/ppermute | solution.py:48
  20.8 4.9 %collective-permute-start.4 = (f32[2,3,512]{2,1,0:T(4,128)S(1)}, f32[2,3,512]{2,1,0:T(4,128)S(1)}, u32[]{:S(2)}, u32[]{:S(2)}) collective-permute-start(f32[2,3,512]{2,1,0:T(4,128)S(1)} %constant_dynamic-update-slice_fusion), channel_id=1, source_target_pairs={{0,4},{1,5},{2,6},{3,7},{4,0},{5,1},{6,2},{7,3},{8,12},{9,13},{10,... | collective-permute-start | bytes 36872 | tf_op jit(solution)/shard_map/ppermute | solution.py:48
  23.4 5.5 %collective-permute-start.5 = (f32[2,3,512]{2,1,0:T(4,128)S(1)}, f32[2,3,512]{2,1,0:T(4,128)S(1)}, u32[]{:S(2)}, u32[]{:S(2)}) collective-permute-start(f32[2,3,512]{2,1,0:T(4,128)S(1)} %constant_dynamic-update-slice_fusion), channel_id=1, source_target_pairs={{0,6},{1,7},{2,4},{3,5},{4,2},{5,3},{6,0},{7,1},{8,14},{9,15},{10,... | collective-permute-start | bytes 36872 | tf_op jit(solution)/shard_map/ppermute | solution.py:48
  34.1 16.2 %copy-start.3 = (f32[1,512,512]{2,1,0:T(8,128)S(1)}, f32[1,512,512]{2,1,0:T(8,128)}, u32[]{:S(2)}) copy-start(f32[1,512,512]{2,1,0:T(8,128)} %param.14) | copy-start | bytes 3145732
  34.1 16.2 %copy-start.4 = (f32[1,512,512]{2,1,0:T(8,128)S(1)}, f32[1,512,512]{2,1,0:T(8,128)}, u32[]{:S(2)}) copy-start(f32[1,512,512]{2,1,0:T(8,128)} %param.15) | copy-start | bytes 3145732
  34.3 9.4 %collective-permute-start.6 = (bf16[4,512,128]{2,1,0:T(8,128)(2,1)S(1)}, bf16[4,512,128]{2,1,0:T(8,128)(2,1)S(1)}, u32[]{:S(2)}, u32[]{:S(2)}) collective-permute-start(bf16[4,512,128]{2,1,0:T(8,128)(2,1)S(1)} %get-tuple-element.48), channel_id=1, source_target_pairs={{0,1},{1,0},{2,3},{3,2},{4,5},{5,4},{6,7},{7,6},{8,24},{9,25},{10,... | collective-permute-start | bytes 1572872 | tf_op jit(solution)/shard_map/ppermute | solution.py:48
  38.7 4.0 %collective-permute-start.7 = (bf16[32,512]{1,0:T(8,128)(2,1)S(1)}, bf16[32,512]{1,0:T(8,128)(2,1)S(1)}, u32[]{:S(2)}, u32[]{:S(2)}) collective-permute-start(bf16[32,512]{1,0:T(8,128)(2,1)S(1)} %convert_element_type.52), channel_id=1, source_target_pairs={{0,2},{1,3},{2,0},{3,1},{4,6},{5,7},{6,4},{7,5},{8,10},{9,11},{10,... | collective-permute-start | bytes 98312 | tf_op jit(solution)/shard_map/ppermute | solution.py:48
  42.7 7.5 %collective-permute-start.14 = (bf16[32,512]{1,0:T(8,128)(2,1)S(1)}, bf16[32,512]{1,0:T(8,128)(2,1)S(1)}, u32[]{:S(2)}, u32[]{:S(2)}) collective-permute-start(bf16[32,512]{1,0:T(8,128)(2,1)S(1)} %add_convert_fusion.2), channel_id=1, source_target_pairs={{0,4},{1,5},{2,6},{3,7},{4,0},{5,1},{6,2},{7,3},{8,12},{9,13},{10,... | collective-permute-start | bytes 98312 | tf_op jit(solution)/shard_map/ppermute | solution.py:48
  43.9 10.4 %collective-permute-start.8 = (bf16[512,128]{1,0:T(8,128)(2,1)S(1)}, bf16[512,128]{1,0:T(8,128)(2,1)S(1)}, u32[]{:S(2)}, u32[]{:S(2)}) collective-permute-start(bf16[512,128]{1,0:T(8,128)(2,1)S(1)} %get-tuple-element.53), channel_id=1, source_target_pairs={{0,2},{1,3},{2,0},{3,1},{4,6},{5,7},{6,4},{7,5},{8,10},{9,11},{10,... | collective-permute-start | bytes 393224 | tf_op jit(solution)/shard_map/ppermute | solution.py:48
  45.5 10.7 %collective-permute-start.9 = (bf16[512,128]{1,0:T(8,128)(2,1)S(1)}, bf16[512,128]{1,0:T(8,128)(2,1)S(1)}, u32[]{:S(2)}, u32[]{:S(2)}) collective-permute-start(bf16[512,128]{1,0:T(8,128)(2,1)S(1)} %get-tuple-element.54), channel_id=1, source_target_pairs={{0,4},{1,5},{2,6},{3,7},{4,0},{5,1},{6,2},{7,3},{8,12},{9,13},{10,... | collective-permute-start | bytes 393224 | tf_op jit(solution)/shard_map/ppermute | solution.py:48
  46.3 9.9 %collective-permute-start.10 = (bf16[512,128]{1,0:T(8,128)(2,1)S(1)}, bf16[512,128]{1,0:T(8,128)(2,1)S(1)}, u32[]{:S(2)}, u32[]{:S(2)}) collective-permute-start(bf16[512,128]{1,0:T(8,128)(2,1)S(1)} %get-tuple-element.55), channel_id=1, source_target_pairs={{0,6},{1,7},{2,4},{3,5},{4,2},{5,3},{6,0},{7,1},{8,14},{9,15},{10,... | collective-permute-start | bytes 393224 | tf_op jit(solution)/shard_map/ppermute | solution.py:48
  50.2 4.0 %collective-permute-start.15 = (bf16[32,512]{1,0:T(8,128)(2,1)S(1)}, bf16[32,512]{1,0:T(8,128)(2,1)S(1)}, u32[]{:S(2)}, u32[]{:S(2)}) collective-permute-start(bf16[32,512]{1,0:T(8,128)(2,1)S(1)} %add_convert_fusion.1), channel_id=1, source_target_pairs={{0,1},{1,0},{2,3},{3,2},{4,5},{5,4},{6,7},{7,6},{8,9},{9,8},{10,11... | collective-permute-start | bytes 98312 | tf_op jit(solution)/shard_map/ppermute | solution.py:48
  57.5 12.8 %all-to-all-start = ((f32[32,8,128]{2,1,0:T(8,128)}), f32[32,8,128]{2,1,0:T(8,128)S(1)}, u32[]{:S(2)}, u32[]{:S(2)}) async-start(f32[32,8,128]{2,1,0:T(8,128)} %share.1), calls=%async_computation | async-start | bytes 262144 | tf_op jit(solution)/shard_map/all_to_all | solution.py:596
  63.0 2.0 %collective-permute-start.11 = (bf16[144,128]{1,0:T(8,128)(2,1)S(1)}, bf16[144,128]{1,0:T(8,128)(2,1)S(1)}, u32[]{:S(2)}, u32[]{:S(2)}) collective-permute-start(bf16[144,128]{1,0:T(8,128)(2,1)S(1)} %get-tuple-element.64), channel_id=1, source_target_pairs={{0,8},{1,9},{2,10},{3,11},{4,12},{5,13},{6,14},{7,15},{8,0},{9,1},... | collective-permute-start | bytes 110600 | tf_op jit(solution)/shard_map/ppermute | solution.py:48
  63.4 4.1 %collective-permute-start.12 = (bf16[144,128]{1,0:T(8,128)(2,1)S(1)}, bf16[144,128]{1,0:T(8,128)(2,1)S(1)}, u32[]{:S(2)}, u32[]{:S(2)}) collective-permute-start(bf16[144,128]{1,0:T(8,128)(2,1)S(1)} %get-tuple-element.65), channel_id=1, source_target_pairs={{0,16},{1,17},{2,18},{3,19},{4,20},{5,21},{6,22},{7,23},{8,24},{9,... | collective-permute-start | bytes 110600 | tf_op jit(solution)/shard_map/ppermute | solution.py:48
  65.0 4.0 %collective-permute-start.13 = (bf16[144,128]{1,0:T(8,128)(2,1)S(1)}, bf16[144,128]{1,0:T(8,128)(2,1)S(1)}, u32[]{:S(2)}, u32[]{:S(2)}) collective-permute-start(bf16[144,128]{1,0:T(8,128)(2,1)S(1)} %get-tuple-element.66), channel_id=1, source_target_pairs={{0,24},{1,25},{2,26},{3,27},{4,28},{5,29},{6,30},{7,31},{8,16},{9,... | collective-permute-start | bytes 110600 | tf_op jit(solution)/shard_map/ppermute | solution.py:48
